TPU v7x, 256 devices: a whole 4x4x8 slice. The times are simulated.
256 devices in a mesh: emit: 16 (over x, y_hi, core), recv: 16 (over z, y_lo).
Axes of the slice: x: 4, y: 4 (y_hi: 2, y_lo: 2; y = y_hi * 2 + y_lo), z: 8, core: 2. Of those that a mesh axis runs over, the one named last changes fastest.
Arguments:
- features: bfloat16 [16, 2048, 256], P('emit', 'recv'), may hold values from -6 to 6
- cotangent: bfloat16 [16, 2048, 256], P('recv', 'emit'), may hold values from -6 to 6
- w_msg: bfloat16 [256, 256], replicated, may hold values from -0.375 to 0.375
- w_out: bfloat16 [256, 256], replicated, may hold values from -0.375 to 0.375
- tile_vals: bfloat16 [16, 16, 64, 256, 256], P('emit', 'recv'), may hold values from -0.1875 to 0.1875
- tile_emit: int32 [16, 16, 64], P('emit', 'recv'), may hold values from 0 to 7
- tile_recv: int32 [16, 16, 64], P('emit', 'recv'), may hold values from 0 to 7
- tile_count: int32 [16, 16], P('emit', 'recv'), may hold values from 1 to 64, as said below
Outputs:
- grad_features: bfloat16 [16, 2048, 256], P('emit', 'recv')
- grad_w_msg: float32 [256, 256], replicated
- grad_w_out: float32 [256, 256], replicated
Inputs may be any that keep to these rules, and one draw needn't show every extreme that they name: Slots at or beyond a pair's tile_count are unused; some pair holds exactly 64 live slots.
All inputs are finite; a program needn't handle non-finite values.
Results may differ from a plain program's by a relative error of at most 0.034.
Values may be sent and summed in bfloat16 or wider, within the bound.
No kernel may reach another device: no remote copies, remote signals or barrier semaphores. Data moves between devices by JAX's collectives and lax.ppermute only.
A program may use at most 64 MiB of HBM per device.

v0:
```python
import jax
import jax.numpy as jnp
from jax import lax
from jax.sharding import PartitionSpec as P

tiles_per_step = 8


def silu_slope(preact):
    sigmoid_pre = jax.nn.sigmoid(preact)
    return sigmoid_pre * (1.0 + preact * (1.0 - sigmoid_pre))


def tile_sweep(
    values, source_blocks, source_index, target_index, live_count, target_blocks, transposed
):
    tile_dim = values.shape[-1]
    feature_width = source_blocks.shape[-1]
    steps_needed = (live_count + tiles_per_step - 1) // tiles_per_step

    def advance(step_index, running):
        first_tile = step_index * tiles_per_step
        value_block = lax.dynamic_slice_in_dim(values, first_tile, tiles_per_step, 0)
        sources = jnp.take(
            source_blocks,
            lax.dynamic_slice_in_dim(source_index, first_tile, tiles_per_step, 0),
            axis=0,
        )
        targets = lax.dynamic_slice_in_dim(target_index, first_tile, tiles_per_step, 0)
        if transposed:
            product = jnp.einsum(
                "tab,tah->tbh", value_block, sources, preferred_element_type=jnp.float32
            )
        else:
            product = jnp.einsum(
                "tba,tah->tbh", value_block, sources, preferred_element_type=jnp.float32
            )
        live_mask = first_tile + jnp.arange(tiles_per_step, dtype=jnp.int32) < live_count
        product = product * live_mask.astype(jnp.float32)[:, None, None]
        return running.at[targets].add(product)

    return lax.fori_loop(
        0, steps_needed, advance, jnp.zeros((target_blocks, tile_dim, feature_width), jnp.float32)
    )


def per_device(features, cotangent, w_msg, w_out, tile_vals, tile_emit, tile_recv, tile_count):
    own_rows = features[0]
    facet_rows, feature_width = own_rows.shape
    tile_dim = tile_vals.shape[-1]
    emit_size = lax.axis_size("emit")
    recv_size = lax.axis_size("recv")
    recv_blocks = facet_rows * emit_size // tile_dim
    emit_blocks = facet_rows * recv_size // tile_dim
    values = tile_vals[0, 0]
    emit_slots = tile_emit[0, 0]
    recv_slots = tile_recv[0, 0]
    live_count = tile_count[0, 0]
    emitted = jnp.dot(own_rows, w_msg, preferred_element_type=jnp.float32).astype(jnp.bfloat16)
    emitter_group = lax.all_gather(emitted, "recv", axis=0, tiled=True)
    message_terms = tile_sweep(
        values,
        emitter_group.reshape(emit_blocks, tile_dim, feature_width),
        emit_slots,
        recv_slots,
        live_count,
        recv_blocks,
        False,
    )
    message_terms = message_terms.reshape(recv_blocks * tile_dim, feature_width)
    cotangent_rows = cotangent[0]
    message_share = lax.psum_scatter(
        message_terms.astype(jnp.bfloat16), "emit", scatter_dimension=0, tiled=True
    )
    preact = jnp.dot(message_share, w_out, preferred_element_type=jnp.float32)
    grad_preact = (cotangent_rows.astype(jnp.float32) * silu_slope(preact)).astype(jnp.bfloat16)
    out_partial = jnp.dot(message_share.T, grad_preact, preferred_element_type=jnp.float32)
    grad_share = jnp.dot(grad_preact, w_out.T, preferred_element_type=jnp.float32).astype(
        jnp.bfloat16
    )
    grad_message = lax.all_gather(grad_share, "emit", axis=0, tiled=True)
    grad_w_out = lax.psum(out_partial, ("emit", "recv"))
    emitter_terms = tile_sweep(
        values,
        grad_message.reshape(recv_blocks, tile_dim, feature_width),
        recv_slots,
        emit_slots,
        live_count,
        emit_blocks,
        True,
    )
    emitter_terms = emitter_terms.reshape(emit_blocks * tile_dim, feature_width)
    grad_emitted = lax.psum_scatter(
        emitter_terms.astype(jnp.bfloat16), "recv", scatter_dimension=0, tiled=True
    )
    emit_partial = jnp.dot(own_rows.T, grad_emitted, preferred_element_type=jnp.float32)
    grad_features = jnp.dot(grad_emitted, w_msg.T, preferred_element_type=jnp.float32).astype(
        jnp.bfloat16
    )[None]
    grad_w_msg = lax.psum(emit_partial, ("emit", "recv"))
    return (grad_features, grad_w_msg, grad_w_out)


def solution(mesh):
    in_specs = (
        P("emit", "recv", None),
        P("recv", "emit", None),
        P(),
        P(),
        P("emit", "recv", None, None, None),
        P("emit", "recv", None),
        P("emit", "recv", None),
        P("emit", "recv"),
    )
    out_specs = (P("emit", "recv", None), P(), P())
    return jax.shard_map(
        per_device, mesh=mesh, in_specs=in_specs, out_specs=out_specs, check_vma=False
    )
```

profile of v0, /device:TPU:1, one launch (start us, length us, event | category | flops | bytes accessed | tf_op | source)
XLA Modules:
  0.0 674.9 jit_solution(16774905923686926868)
XLA Ops:
  7.2 0.0 copy-start
  7.2 0.0 copy-start.5
  7.2 0.0 copy-start.4
  7.2 0.0 all-gather.3.cloned.1.call-start
  7.2 1.7 convolution_convert_fusion.2
  9.0 0.0 all-gather.3.cloned.1.call-update
  9.0 0.0 reduce-scatter.3.cloned.1.call-start
  9.7 63.0 %all-gather.3.cloned.1.call-done = bf16[2048,256]{1,0:T(8,128)(2,1)} async-done(((bf16[128,256]{1,0:T(8,128)(2,1)}), bf16[2048,256]{1,0:T(8,128)(2,1)}) %all-gather.3.cloned.1.call-update) | async-done | bytes 1048592 | tf_op jit(solution)/shard_map/all_gather | solution.py:60
  72.8 1.5 broadcast.48.clone
  74.3 25.7 %while.20 = (s32[]{:T(128)}, f32[8,256,256]{2,1,0:T(8,128)}, s32[]{:T(128)}, s32[64]{0:T(128)S(1)}, bf16[64,256,256]{2,1,0:T(8,128)(2,1)}, /*index=5*/s32[64]{0:...) while((s32[]{:T(128)}, f32[8,256,256]{2,1,0:T(8,128)}, ...), condition=%wide.region_2.4_spmd, body=%wide.region_0.3_spmd.sunk | while | flops 270009440 | bytes 12587495 | solution.py:42
  74.3 0.7 compare_and_fusion.4
  75.0 1.8 gather_fusion
  76.9 1.7 convolution_multiply_fusion.4
  78.6 0.1 compare_select_fusion.8
  78.7 4.2 scatter_fusion
  82.9 0.7 compare_and_fusion.4
  83.6 1.8 gather_fusion
  85.4 1.7 convolution_multiply_fusion.4
  87.2 0.1 compare_select_fusion.8
  87.3 4.2 scatter_fusion
  91.4 0.7 compare_and_fusion.4
  92.1 1.8 gather_fusion
  94.0 1.7 convolution_multiply_fusion.4
  95.7 0.1 compare_select_fusion.8
  95.8 4.2 scatter_fusion
  100.0 2.7 convert_element_type.47
  102.8 0.0 reduce-scatter.3.cloned.1.call-update
  102.8 0.0 all-gather.5.cloned.1.call-start
  102.8 113.5 %reduce-scatter.3.cloned.1.call-done = bf16[128,256]{1,0:T(8,128)(2,1)} async-done(((bf16[2048,256]{1,0:T(8,128)(2,1)}), bf16[128,256]{1,0:T(8,128)(2,1)}) %reduce-scatter.3.cloned.1.call-update) | async-done | bytes 65552 | tf_op jit(solution)/shard_map/reduce_scatter | solution.py:72
  216.3 0.0 copy-done
  216.3 1.1 fusion.13
  217.4 0.8 convolution_convert_fusion.1
  218.2 0.0 all-gather.5.cloned.1.call-update
  218.3 0.0 reduce-scatter.5.cloned.1.call-start
  218.3 12.0 %copy.11 = bf16[1,1,64,256,256]{3,4,2,1,0:T(8,128)(2,1)} copy(bf16[1,1,64,256,256]{4,3,2,1,0:T(8,128)(2,1)} %bitcast.33) | data formatting | bytes 16777216 | tf_op args[4]
  230.3 41.3 %all-gather.5.cloned.1.call-done = bf16[2048,256]{1,0:T(8,128)(2,1)} async-done(((bf16[128,256]{1,0:T(8,128)(2,1)}), bf16[2048,256]{1,0:T(8,128)(2,1)}) %all-gather.5.cloned.1.call-update) | async-done | bytes 1048592 | tf_op jit(solution)/shard_map/all_gather | solution.py:81
  271.6 1.5 broadcast.48
  273.1 25.9 %while.21 = (s32[]{:T(128)}, f32[8,256,256]{2,1,0:T(8,128)}, s32[]{:T(128)}, s32[64]{0:T(128)S(1)}, bf16[64,256,256]{1,2,0:T(8,128)(2,1)}, /*index=5*/s32[64]{0:...) while((s32[]{:T(128)}, f32[8,256,256]{2,1,0:T(8,128)}, ...), condition=%wide.region_6.8_spmd, body=%wide.region_4.7_spmd.sunk | while | flops 270009440 | bytes 12587495 | solution.py:42
  273.1 0.7 compare_and_fusion.5
  273.8 1.8 gather_fusion.1
  275.7 1.7 convolution_multiply_fusion.5
  277.4 0.1 compare_select_fusion.9
  277.5 4.3 scatter_fusion.1
  281.9 0.7 compare_and_fusion.5
  282.6 1.8 gather_fusion.1
  284.4 1.7 convolution_multiply_fusion.5
  286.2 0.1 compare_select_fusion.9
  286.3 4.3 scatter_fusion.1
  290.5 0.7 compare_and_fusion.5
  291.3 1.8 gather_fusion.1
  293.1 1.7 convolution_multiply_fusion.5
  294.9 0.1 compare_select_fusion.9
  294.9 4.1 scatter_fusion.1
  299.0 2.7 convert_element_type.51
  301.8 0.0 reduce-scatter.5.cloned.1.call-update
  301.8 0.0 all-reduce.3.cloned.1.call-start
  301.8 0.9 fusion.16
  302.8 95.7 %reduce-scatter.5.cloned.1.call-done = bf16[128,256]{1,0:T(8,128)(2,1)} async-done(((bf16[2048,256]{1,0:T(8,128)(2,1)}), bf16[128,256]{1,0:T(8,128)(2,1)}) %reduce-scatter.5.cloned.1.call-update) | async-done | bytes 65552 | tf_op jit(solution)/shard_map/reduce_scatter | solution.py:93
  398.5 1.8 convolution_bitcast_fusion
  400.2 0.0 all-reduce.3.cloned.1.call-update
  400.3 1.7 fusion.12
  401.9 263.0 %all-reduce.3.cloned.1.call-done = (f32[256,256]{0,1:T(8,128)}, f32[256,256]{1,0:T(8,128)}) async-done(((f32[256,256]{0,1:T(8,128)}, f32[256,256]{1,0:T(8,128)}), (f32[256,256]{0,1:T(8,128)}, f32[256,256]{1,0:T(8,128)})) %all-reduce.3.cloned.1.call-update) | async-done | bytes 524304 | tf_op jit(solution)/shard_map/psum | solution.py:100
  664.9 1.8 copy.13
  666.7 1.7 copy.32
  (16 shorter events, 0.1 us)
Async XLA Ops:
  7.2 209.2 %copy-start = (bf16[256,256]{1,0:T(8,128)(2,1)S(1)}, bf16[256,256]{1,0:T(8,128)(2,1)}, u32[]{:S(2)}) copy-start(bf16[256,256]{1,0:T(8,128)(2,1)} %param.17) | copy-start | bytes 393220
  7.2 67.1 %copy-start.5 = (s32[1,1,64]{2,1,0:T(1,128)S(1)}, s32[1,1,64]{2,1,0:T(1,128)}, u32[]{:S(2)}) copy-start(s32[1,1,64]{2,1,0:T(1,128)} %param.19) | copy-start | bytes 772
  7.2 67.1 %copy-start.4 = (s32[1,1,64]{2,1,0:T(1,128)S(1)}, s32[1,1,64]{2,1,0:T(1,128)}, u32[]{:S(2)}) copy-start(s32[1,1,64]{2,1,0:T(1,128)} %param.20) | copy-start | bytes 772
  7.2 65.6 %all-gather.3.cloned.1.call-start = ((), (), s32[]{:S(2)}) async-start(), calls=%async_computation.2 | async-start | bytes 1114112 | tf_op jit(solution)/shard_map/all_gather | solution.py:60
  9.0 207.3 %reduce-scatter.3.cloned.1.call-start = ((), (), s32[]{:S(2)}) async-start(), calls=%async_computation.3 | async-start | bytes 1114112 | tf_op jit(solution)/shard_map/reduce_scatter | solution.py:72
  100.0 116.3 %copy-start.6 = (bf16[1,128,256]{2,1,0:T(8,128)(2,1)S(1)}, bf16[1,128,256]{2,1,0:T(8,128)(2,1)}, u32[]{:S(2)}) copy-start(bf16[1,128,256]{2,1,0:T(8,128)(2,1)} %param.15) | copy-start | bytes 196612
  102.8 168.8 %all-gather.5.cloned.1.call-start = ((), (), s32[]{:S(2)}) async-start(), calls=%async_computation.4 | async-start | bytes 1114112 | tf_op jit(solution)/shard_map/all_gather | solution.py:81
  218.3 180.2 %reduce-scatter.5.cloned.1.call-start = ((), (), s32[]{:S(2)}) async-start(), calls=%async_computation.5 | async-start | bytes 1114112 | tf_op jit(solution)/shard_map/reduce_scatter | solution.py:93
  299.0 2.8 copy-start.3
  299.0 99.4 %copy-start.2 = (bf16[1,128,256]{2,1,0:T(8,128)(2,1)S(1)}, bf16[1,128,256]{2,1,0:T(8,128)(2,1)}, u32[]{:S(2)}) copy-start(bf16[1,128,256]{2,1,0:T(8,128)(2,1)} %param.14) | copy-start | bytes 196612
  299.0 101.2 %copy-start.1 = (bf16[256,256]{1,0:T(8,128)(2,1)S(1)}, bf16[256,256]{1,0:T(8,128)(2,1)}, u32[]{:S(2)}) copy-start(bf16[256,256]{1,0:T(8,128)(2,1)} %param.16) | copy-start | bytes 393220
  301.8 363.2 %all-reduce.3.cloned.1.call-start = ((), (), s32[]{:S(2)}) async-start(), calls=%async_computation.6 | async-start | bytes 1048576 | tf_op jit(solution)/shard_map/psum | solution.py:100
Sparse Core Ops, SparseCore 0:
  10.4 62.3 all-gather.2
  102.9 113.3 reduce-scatter.2
  220.0 51.5 all-gather.4
  301.9 96.5 reduce-scatter.4
  404.5 260.3 all-reduce.2
where the time goes:
time: 678 us; the launch traced here: 675 us
  waiting for transfers between devices  577 us (85%)
  other arithmetic  35.5 us (5%)
  local copies, waits for them, and re-layouts  29.5 us (4%)
  matrix products  18.4 us (3%)
  between operations  14.5 us (2%)
    psum x1, waiting for transfers between devices, per_device(): grad_w_msg = lax.psum(emit_partial, ('emit', 'recv'))  263 us
    reduce_scatter x1, waiting for transfers between devices, per_device(): lax.psum_scatter(message_terms.astype(jnp.bfloat16), 'emit', scatter_dime...  114 us
    reduce_scatter x1, waiting for transfers between devices, per_device(): lax.psum_scatter(emitter_terms.astype(jnp.bfloat16), 'recv', scatter_dime...  95.7 us
    all_gather x1, waiting for transfers between devices, per_device(): emitter_group = lax.all_gather(emitted, 'recv', axis=0, tiled=True)  63 us
    all_gather x1, waiting for transfers between devices, per_device(): grad_message = lax.all_gather(grad_share, 'emit', axis=0, tiled=True)  41.3 us
    scatter-add x6, other arithmetic, advance(): return running.at[targets].add(product)  25.2 us
    unnamed x17, local copies, waits for them, and re-layouts  15.4 us
  transfers between devices with their start and end apart: 5, of which 5 were waited for; matrix products, arithmetic and copies ran while one was open for 2% of the time, Pallas kernels for 0%

commit v1 on v0

v1 whole, which is shorter than its diff:
```python
import functools

import jax
import jax.numpy as jnp
from jax import lax
from jax.experimental import pallas as pl
from jax.experimental.pallas import tpu as pltpu
from jax.sharding import PartitionSpec as P

ring_depth = 16
f32 = jnp.float32
bf16 = jnp.bfloat16


def stream_tiles(live, tiles, ring, sems, consume):
    def copy(slot):
        place = lax.rem(slot, ring_depth)
        return pltpu.make_async_copy(tiles.at[slot], ring.at[place], sems.at[place])

    def begin(slot, carry):
        copy(slot).start()
        return carry

    lax.fori_loop(0, jnp.minimum(live, ring_depth), begin, 0)

    def step(slot, carry):
        copy(slot).wait()
        consume(slot, ring[lax.rem(slot, ring_depth)])

        @pl.when(slot + ring_depth < live)
        def _():
            copy(slot + ring_depth).start()

        return carry

    return lax.fori_loop(0, live, step, 0)


def forward_kernel(source, target, live, core, rows, tiles, kept, sent, acc, ring, sems):
    half = kept.shape[1]
    acc[...] = jnp.zeros_like(acc)

    def consume(slot, tile):
        block = target[slot]
        acc[block] += jnp.dot(tile, rows[source[slot]], preferred_element_type=f32)

    stream_tiles(live[0], tiles, ring, sems, consume)
    own = pl.multiple_of(core[0] * half, half)
    other = pl.multiple_of((1 - core[0]) * half, half)
    for block in range(acc.shape[0]):
        sent[block] = acc[block, pl.ds(other, half), :].astype(bf16)
        kept[block] = acc[block, pl.ds(own, half), :]


def middle_kernel(terms, cotangent, w_msg, w_out, payload):
    width = w_msg.shape[0]
    pieces = terms.shape[0]
    lanes = width // 2
    summed = terms[0].astype(f32)
    for piece in range(1, pieces):
        summed += terms[piece].astype(f32)
    summed = summed.astype(bf16)
    message = jnp.dot(summed, w_msg[...], preferred_element_type=f32).astype(bf16)
    preact = jnp.dot(message, w_out[...], preferred_element_type=f32)
    sigmoid_pre = jax.nn.sigmoid(preact)
    slope = sigmoid_pre * (1.0 + preact * (1.0 - sigmoid_pre))
    grad_preact = (cotangent[...].astype(f32) * slope).astype(bf16)
    across = (((1,), (1,)), ((), ()))
    along = (((0,), (0,)), ((), ()))
    grad_turned = lax.dot_general(w_out[...], grad_preact, across, preferred_element_type=f32).astype(bf16)
    grad = lax.dot_general(grad_preact, w_out[...], across, preferred_element_type=f32).astype(bf16)
    out_part = lax.dot_general(message, grad_preact, along, preferred_element_type=f32).astype(bf16)
    msg_part = lax.dot_general(summed, grad, along, preferred_element_type=f32).astype(bf16)
    parts = (
        out_part[:, :lanes],
        out_part[:, lanes:],
        msg_part[:, :lanes],
        msg_part[:, lanes:],
    )
    chunk = 4 * width // pieces
    for piece in range(pieces):
        payload[piece, :width, :] = grad_turned
        at = 0
        while at < chunk:
            quarter, row = divmod(piece * chunk + at, width)
            size = min(chunk - at, width - row)
            payload[piece, width + at : width + at + size, :] = parts[quarter][row : row + size]
            at += size


def backward_kernel(
    source, target, live, core, held, other, tiles, payload, grads, acc, ring, sems
):
    width, lanes = acc.shape[1], held.shape[2]
    blocks = acc.shape[0]
    acc[...] = jnp.zeros_like(acc)
    chunk = (held.shape[1] - width) // 2

    def place(first, second):
        for block in range(held.shape[0]):
            grads[block, :, :lanes] = first[block, :width, :]
            grads[block, :, lanes:] = second[block, :width, :]

    @pl.when(core[0] == 0)
    def _():
        place(held, other)

    @pl.when(core[0] == 1)
    def _():
        place(other, held)

    def consume(slot, tile):
        block = target[slot]
        acc[block] += jnp.dot(grads[source[slot]], tile, preferred_element_type=f32)

    stream_tiles(live[0], tiles, ring, sems, consume)
    own = pl.ds(pl.multiple_of(width + core[0] * chunk, chunk), chunk)
    weights = held[0, own, :].astype(f32) + other[0, own, :].astype(f32)
    for block in range(1, held.shape[0]):
        weights += held[block, own, :].astype(f32) + other[block, own, :].astype(f32)
    weights = weights.astype(bf16)
    for block in range(blocks):
        for part in range(width // lanes):
            piece = block * (width // lanes) + part
            payload[piece, :width, :] = acc[block, :, part * lanes : (part + 1) * lanes].astype(bf16)
            payload[piece, width:, :] = weights


def weights_kernel(terms, total):
    width = terms.shape[1] - total.shape[1]
    summed = terms[0, width:, :].astype(f32)
    for piece in range(1, terms.shape[0]):
        summed += terms[piece, width:, :].astype(f32)
    for piece in range(total.shape[0]):
        total[piece] = summed


def features_kernel(terms, w_msg, grad):
    width = w_msg.shape[0]
    summed = terms[0, :width, :].astype(f32)
    for piece in range(1, terms.shape[0]):
        summed += terms[piece, :width, :].astype(f32)
    grad[...] = lax.dot_general(
        summed.astype(bf16), w_msg[...], (((0,), (1,)), ((), ())), preferred_element_type=f32
    ).astype(bf16)


def in_vmem(count):
    return [pl.BlockSpec(memory_space=pltpu.VMEM)] * count


def in_smem(count):
    return [pl.BlockSpec(memory_space=pltpu.SMEM)] * count


def limits(mebibytes):
    return pltpu.CompilerParams(vmem_limit_bytes=mebibytes * 2**20)


def per_device(features, cotangent, w_msg, w_out, tile_vals, tile_emit, tile_recv, tile_count):
    own_rows = features[0]
    facet_rows, width = own_rows.shape
    tile_dim = tile_vals.shape[-1]
    emit_size = lax.axis_size("emit")
    recv_size = lax.axis_size("recv")
    recv_blocks = facet_rows * emit_size // tile_dim
    emit_blocks = facet_rows * recv_size // tile_dim
    chips = emit_size // 2
    lanes = width // 2
    values = tile_vals[0, 0]
    emit_slots = tile_emit[0, 0]
    recv_slots = tile_recv[0, 0]
    live = tile_count[0]
    core = lax.rem(lax.axis_index("emit"), 2)[None]
    same_core = [list(range(parity, emit_size, 2)) for parity in range(2)]
    swap = [(member, member ^ 1) for member in range(emit_size)]
    struct = jax.ShapeDtypeStruct
    any_space = pl.BlockSpec(memory_space=pl.ANY)
    sweep_scratch = [
        pltpu.VMEM((ring_depth, tile_dim, tile_dim), bf16),
        pltpu.SemaphoreType.DMA((ring_depth,)),
    ]

    group_rows = lax.all_to_all(
        jnp.broadcast_to(own_rows[None], (recv_size, facet_rows, width)), "recv", 0, 0, tiled=True
    )
    kept, sent = pl.pallas_call(
        forward_kernel,
        out_shape=(
            struct((recv_blocks, tile_dim // 2, width), f32),
            struct((recv_blocks, tile_dim // 2, width), bf16),
        ),
        in_specs=in_smem(4) + in_vmem(1) + [any_space],
        out_specs=tuple(in_vmem(2)),
        scratch_shapes=[pltpu.VMEM((recv_blocks, tile_dim, width), f32)] + sweep_scratch,
        compiler_params=limits(16),
        name="forward_sweep",
    )(emit_slots, recv_slots, live, core, group_rows.reshape(emit_blocks, tile_dim, width), values)
    arrived = lax.ppermute(sent, "emit", swap)
    pair_sum = (kept + arrived.astype(f32)).astype(bf16)
    terms = lax.all_to_all(pair_sum, "emit", 0, 0, tiled=True, axis_index_groups=same_core)

    chunk = 4 * width // chips
    payload = pl.pallas_call(
        middle_kernel,
        out_shape=struct((chips, width + chunk, lanes), bf16),
        in_specs=in_vmem(4),
        out_specs=in_vmem(1)[0],
        compiler_params=limits(16),
        name="middle",
    )(terms, cotangent[0], w_msg, w_out)
    held = lax.all_to_all(payload, "emit", 0, 0, tiled=True, axis_index_groups=same_core)
    other = lax.ppermute(held, "emit", swap)

    back = pl.pallas_call(
        backward_kernel,
        out_shape=struct((recv_size, width + chunk // 2, lanes), bf16),
        in_specs=in_smem(4) + in_vmem(2) + [any_space],
        out_specs=in_vmem(1)[0],
        scratch_shapes=[
            pltpu.VMEM((recv_blocks, width, tile_dim), bf16),
            pltpu.VMEM((emit_blocks, width, tile_dim), f32),
        ]
        + sweep_scratch,
        compiler_params=limits(16),
        name="backward_sweep",
    )(recv_slots, emit_slots, live, core, held, other, values)
    back_terms = lax.all_to_all(back, "recv", 0, 0, tiled=True)

    total = pl.pallas_call(
        weights_kernel,
        out_shape=struct((emit_size, chunk // 2, lanes), f32),
        in_specs=in_vmem(1),
        out_specs=in_vmem(1)[0],
        compiler_params=limits(8),
        name="weights_sum",
    )(back_terms)
    gathered = lax.all_to_all(total, "emit", 0, 0, tiled=True).reshape(4, width, lanes)
    grad_features = pl.pallas_call(
        features_kernel,
        out_shape=struct((facet_rows, width), bf16),
        in_specs=in_vmem(2),
        out_specs=in_vmem(1)[0],
        compiler_params=limits(8),
        name="features_grad",
    )(back_terms, w_msg)[None]
    grad_w_out = jnp.concatenate([gathered[0], gathered[1]], axis=1)
    grad_w_msg = jnp.concatenate([gathered[2], gathered[3]], axis=1)
    return (grad_features, grad_w_msg, grad_w_out)


def solution(mesh):
    in_specs = (
        P("emit", "recv", None),
        P("recv", "emit", None),
        P(),
        P(),
        P("emit", "recv", None, None, None),
        P("emit", "recv", None),
        P("emit", "recv", None),
        P("emit", "recv"),
    )
    out_specs = (P("emit", "recv", None), P(), P())
    return jax.shard_map(
        per_device, mesh=mesh, in_specs=in_specs, out_specs=out_specs, check_vma=False
    )
```

time: 678 us -> 175 us (0.26)
  waiting for transfers between devices: 577 us -> 38.3 us
  blocking collectives: 0 us -> 70.4 us
  other arithmetic: 35.5 us -> 0.98 us
  starting transfers between devices: 0.21 us -> 33.2 us
  Pallas kernels: 0 us -> 26.8 us
  local copies, waits for them, and re-layouts: 29.5 us -> 5.37 us
  matrix products: 18.4 us -> 0 us
  between operations: 14.5 us -> 1.34 us
    psum x1 -> x0, waiting for transfers between devices: 263 us -> none  [per_device(): grad_w_msg = lax.psum(emit_partial, ('emit', 'recv'))]
    reduce_scatter x2 -> x0, waiting for transfers between devices: 209 us -> none  [the longest x1 114 us: per_device(): lax.psum_scatter(message_terms.astype(jnp.bfloat16), 'emit', scatter_dime...]
    all_gather x2 -> x0, waiting for transfers between devices: 104 us -> none  [the longest x1 63 us: per_device(): emitter_group = lax.all_gather(emitted, 'recv', axis=0, tiled=True)]
    all_to_all x0 -> x3, blocking collectives: none -> 70.4 us  [the longest x1 40.5 us: per_device(): back_terms = lax.all_to_all(back, 'recv', 0, 0, tiled=True)]
    all_to_all x0 -> x2, waiting for transfers between devices: none -> 34.8 us  [the longest x1 24.6 us: per_device(): lax.all_to_all(jnp.broadcast_to(own_rows[None], (recv_size, facet_rows, w...]
    pallas_call x0 -> x5, Pallas kernels: none -> 26.8 us  [the longest x1 12.2 us: per_device(): pl.pallas_call(backward_kernel, out_shape=struct((recv_size, width + chun...]
    all_to_all x0 -> x2, starting transfers between devices: none -> 25.4 us  [the longest x1 15.1 us: per_device(): lax.all_to_all(total, 'emit', 0, 0, tiled=True).reshape(4, width, lanes)]
    scatter-add x6 -> x0, other arithmetic: 25.2 us -> none  [advance(): return running.at[targets].add(product)]
  transfers between devices with their start and end apart: 5 -> 4, of which waited for: 5 -> 4; matrix products, arithmetic and copies ran while one was open for 2% -> 0% of each run, Pallas kernels for 0% -> 1%
where the time goes in v1:
time: 175 us; the launch traced here: 176 us
  blocking collectives  70.4 us (40%)
  waiting for transfers between devices  38.3 us (22%)
  starting transfers between devices  33.2 us (19%)
  Pallas kernels  26.8 us (15%)
  local copies, waits for them, and re-layouts  5.37 us (3%)
    all_to_all x1, blocking collectives, per_device(): back_terms = lax.all_to_all(back, 'recv', 0, 0, tiled=True)  40.5 us
    all_to_all x1, waiting for transfers between devices, per_device(): lax.all_to_all(jnp.broadcast_to(own_rows[None], (recv_size, facet_rows, w...  24.6 us
    all_to_all x1, blocking collectives, per_device(): lax.all_to_all(payload, 'emit', 0, 0, tiled=True, axis_index_groups=same_...  16 us
    all_to_all x1, starting transfers between devices, per_device(): lax.all_to_all(total, 'emit', 0, 0, tiled=True).reshape(4, width, lanes)  15.1 us
    all_to_all x1, blocking collectives, per_device(): lax.all_to_all(pair_sum, 'emit', 0, 0, tiled=True, axis_index_groups=same...  13.9 us
    pallas_call x1, Pallas kernels, per_device(): pl.pallas_call(backward_kernel, out_shape=struct((recv_size, width + chun...  12.2 us
    pallas_call x1, Pallas kernels, per_device(): pl.pallas_call(forward_kernel, out_shape=(struct((recv_blocks, tile_dim /...  12.1 us
    all_to_all x1, starting transfers between devices, per_device(): lax.all_to_all(jnp.broadcast_to(own_rows[None], (recv_size, facet_rows, w...  10.3 us
  transfers between devices with their start and end apart: 4, of which 4 were waited for; matrix products, arithmetic and copies ran while one was open for 0% of the time, Pallas kernels for 1%

profile of v1, /device:TPU:1, one launch (start us, length us, event | category | flops | bytes accessed | tf_op | source)
XLA Modules:
  0.0 176.3 jit_solution(3059832524806245521)
XLA Ops:
  0.6 1.9 %broadcast_in_dim.15 = bf16[16,128,256]{2,1,0:T(8,128)(2,1)} broadcast(bf16[128,256]{1,0:T(8,128)(2,1)} %bitcast.27), dimensions={1,2} | broadcast | bytes 1114112 | tf_op jit(solution)/shard_map/broadcast_in_dim | solution.py:185
  2.6 0.0 copy-start.5
  2.6 0.0 copy-start.6
  2.6 10.3 %all-to-all-start = ((bf16[16,128,256]{2,1,0:T(8,128)(2,1)}), bf16[16,128,256]{2,1,0:T(8,128)(2,1)S(1)}, u32[]{:S(2)}, u32[]{:S(2)}) async-start(bf16[16,128,256]{2,1,0:T(8,128)(2,1)} %broadcast_in_dim.15), calls=%async_computation | async-start | bytes 2097152 | tf_op jit(solution)/shard_map/all_to_all | solution.py:184
  13.5 24.6 %all-to-all-done = bf16[16,128,256]{2,1,0:T(8,128)(2,1)S(1)} async-done(((bf16[16,128,256]{2,1,0:T(8,128)(2,1)}), bf16[16,128,256]{2,1,0:T(8,128)(2,1)S(1)}, u32[]{:S(2)}, u32[]{:S(2)}) %all-to-all-start) | async-done | bytes 1048608 | tf_op jit(solution)/shard_map/all_to_all | solution.py:184
  38.1 0.0 copy-done.5
  38.1 0.0 copy-done.6
  38.1 0.0 copy-start
  38.1 3.4 %copy-done = bf16[1,1,64,256,256]{4,3,2,1,0:T(8,128)(2,1)S(1)} copy-done((bf16[1,1,64,256,256]{4,3,2,1,0:T(8,128)(2,1)S(1)}, bf16[1,1,64,256,256]{4,3,2,1,0:T(8,128)(2,1)}, u32[]{:S(2)}) %copy-start) | copy-done | bytes 8388632
  41.5 0.0 copy-start.1
  41.5 12.1 %forward_sweep.1 = (f32[8,128,256]{2,1,0:T(8,128)S(1)}, bf16[8,128,256]{2,1,0:T(8,128)(2,1)S(1)}) custom-call(s32[64]{0:T(128)S(1)} %bitcast.21, s32[64]{0:T(128)S(1)} %bitcast.19, s32[1]{0:T(128)} %bitcast.13.live, s32[1]{0:T(128)} %bitcast.3.core, bf16[8,256,256]{2,1,0:T(8,128)(2,1)S(1)} %bitcast.17, bf16[64,256,256]{2,1,0:T(8,128)(2,1)S(1)} %bitcast.15), custom_call_target="tpu_custom_call" | custom-call | tf_op jit(solution)/shard_map/forward_sweep/pallas_call | solution.py:187
  53.7 5.2 %collective-permute-start = (bf16[8,128,256]{2,1,0:T(8,128)(2,1)S(1)}, bf16[8,128,256]{2,1,0:T(8,128)(2,1)S(1)}, u32[]{:S(2)}, u32[]{:S(2)}) collective-permute-start(bf16[8,128,256]{2,1,0:T(8,128)(2,1)S(1)} %get-tuple-element.6), channel_id=1, source_target_pairs={{0,16},{16,0},{32,48},{48,32},{64,80},{80,64},{96,112},{112,96},{1... | collective-permute-start | bytes 1572872 | tf_op jit(solution)/shard_map/ppermute | solution.py:199
  58.8 1.5 collective-permute-done
  60.4 0.0 copy-start.2
  60.4 0.0 copy-start.3
  60.4 0.0 copy-start.4
  60.4 0.2 add_convert_fusion
  60.5 13.9 %all_to_all.25.terms = bf16[8,128,256]{2,1,0:T(8,128)(2,1)S(1)} all-to-all(bf16[8,128,256]{2,1,0:T(8,128)(2,1)S(1)} %add_convert_fusion), channel_id=1, replica_groups={{0,32,64,96,128,160,192,224},{16,48,80,112,144,176,208,240},{1,33,65,97..., dimensions={0} | all-to-all | bytes 1048576 | tf_op jit(solution)/shard_map/all_to_all | solution.py:201
  74.4 0.0 copy-done.2
  74.4 0.0 copy-done.3
  74.4 0.0 copy-done.4
  74.4 0.6 middle.1
  75.0 16.0 %all_to_all.26.held = bf16[8,384,128]{2,1,0:T(8,128)(2,1)S(1)} all-to-all(bf16[8,384,128]{2,1,0:T(8,128)(2,1)S(1)} %middle.1), channel_id=1, replica_groups={{0,32,64,96,128,160,192,224},{16,48,80,112,144,176,208,240},{1,33,65,97..., dimensions={0} | all-to-all | bytes 1572864 | tf_op jit(solution)/shard_map/all_to_all | solution.py:212
  91.0 2.7 %collective-permute-start.1 = (bf16[8,384,128]{2,1,0:T(8,128)(2,1)S(1)}, bf16[8,384,128]{2,1,0:T(8,128)(2,1)S(1)}, u32[]{:S(2)}, u32[]{:S(2)}) collective-permute-start(bf16[8,384,128]{2,1,0:T(8,128)(2,1)S(1)} %all_to_all.26.held), channel_id=1, source_target_pairs={{0,16},{16,0},{32,48},{48,32},{64,80},{80,64},{96,112},{112,96},{1... | collective-permute-start | bytes 2359304 | tf_op jit(solution)/shard_map/ppermute | solution.py:213
  93.7 1.9 %collective-permute-done.1.other = bf16[8,384,128]{2,1,0:T(8,128)(2,1)S(1)} collective-permute-done((bf16[8,384,128]{2,1,0:T(8,128)(2,1)S(1)}, bf16[8,384,128]{2,1,0:T(8,128)(2,1)S(1)}, u32[]{:S(2)}, u32[]{:S(2)}) %collective-permute-start.1) | collective-permute-done | bytes 786464 | tf_op jit(solution)/shard_map/ppermute | solution.py:213
  95.6 0.0 copy-done.1
  95.6 12.2 %backward_sweep.1 = bf16[16,320,128]{2,1,0:T(8,128)(2,1)S(1)} custom-call(s32[64]{0:T(128)S(1)} %bitcast.20, s32[64]{0:T(128)S(1)} %bitcast.22, s32[1]{0:T(128)} %bitcast.14.live, s32[1]{0:T(128)} %bitcast.3.core, bf16[8,384,128]{2,1,0:T(8,128)(2,1)S(1)} %all_to_all.26.held, bf16[8,384,128]{2,1,0:T(8,128)(2,1)S(1)} %collective-permute-done.1.other, ...), custom_call_target="tpu_custom_call" | custom-call | tf_op jit(solution)/shard_map/backward_sweep/pallas_call | solution.py:215
  107.8 40.5 %all_to_all.27.terms = bf16[16,320,128]{2,1,0:T(8,128)(2,1)S(1)} all-to-all(bf16[16,320,128]{2,1,0:T(8,128)(2,1)S(1)} %backward_sweep.1), channel_id=1, replica_groups=mesh['emit'=16,'recv'=16] {'recv'}, dimensions={0} | all-to-all | bytes 2621440 | tf_op jit(solution)/shard_map/all_to_all | solution.py:228
  148.4 0.9 weights_sum.1
  149.2 15.1 %all-to-all-start.4 = ((f32[16,64,128]{2,1,0:T(8,128)}), f32[16,64,128]{2,1,0:T(8,128)S(1)}, u32[]{:S(2)}, u32[]{:S(2)}) async-start(f32[16,64,128]{2,1,0:T(8,128)} %weights_sum.1), calls=%async_computation.4 | async-start | bytes 1048576 | tf_op jit(solution)/shard_map/all_to_all | solution.py:238
  164.3 1.0 features_grad.1
  165.3 10.2 %all-to-all-done.4 = f32[16,64,128]{2,1,0:T(8,128)S(1)} async-done(((f32[16,64,128]{2,1,0:T(8,128)}), f32[16,64,128]{2,1,0:T(8,128)S(1)}, u32[]{:S(2)}, u32[]{:S(2)}) %all-to-all-start.4) | async-done | bytes 524320 | tf_op jit(solution)/shard_map/all_to_all | solution.py:238
  175.5 0.8 pad_maximum_fusion
  (1 shorter events, 0.0 us)
Async XLA Ops:
  2.6 35.6 %copy-start.5 = (s32[1,1,64]{2,1,0:T(1,128)S(1)}, s32[1,1,64]{2,1,0:T(1,128)}, u32[]{:S(2)}) copy-start(s32[1,1,64]{2,1,0:T(1,128)} %param.14) | copy-start | bytes 772
  2.6 35.6 %copy-start.6 = (s32[1,1,64]{2,1,0:T(1,128)S(1)}, s32[1,1,64]{2,1,0:T(1,128)}, u32[]{:S(2)}) copy-start(s32[1,1,64]{2,1,0:T(1,128)} %param.13) | copy-start | bytes 772
  2.6 35.6 %all-to-all-start = ((bf16[16,128,256]{2,1,0:T(8,128)(2,1)}), bf16[16,128,256]{2,1,0:T(8,128)(2,1)S(1)}, u32[]{:S(2)}, u32[]{:S(2)}) async-start(bf16[16,128,256]{2,1,0:T(8,128)(2,1)} %broadcast_in_dim.15), calls=%async_computation | async-start | bytes 2097152 | tf_op jit(solution)/shard_map/all_to_all | solution.py:184
  38.1 3.4 %copy-start = (bf16[1,1,64,256,256]{4,3,2,1,0:T(8,128)(2,1)S(1)}, bf16[1,1,64,256,256]{4,3,2,1,0:T(8,128)(2,1)}, u32[]{:S(2)}) copy-start(bf16[1,1,64,256,256]{4,3,2,1,0:T(8,128)(2,1)} %param.12) | copy-start | bytes 25165828
  41.5 54.1 %copy-start.1 = (bf16[1,1,64,256,256]{4,3,2,1,0:T(8,128)(2,1)S(1)}, bf16[1,1,64,256,256]{4,3,2,1,0:T(8,128)(2,1)}, u32[]{:S(2)}) copy-start(bf16[1,1,64,256,256]{4,3,2,1,0:T(8,128)(2,1)} %param.12) | copy-start | bytes 25165828
  53.7 6.7 %collective-permute-start = (bf16[8,128,256]{2,1,0:T(8,128)(2,1)S(1)}, bf16[8,128,256]{2,1,0:T(8,128)(2,1)S(1)}, u32[]{:S(2)}, u32[]{:S(2)}) collective-permute-start(bf16[8,128,256]{2,1,0:T(8,128)(2,1)S(1)} %get-tuple-element.6), channel_id=1, source_target_pairs={{0,16},{16,0},{32,48},{48,32},{64,80},{80,64},{96,112},{112,96},{1... | collective-permute-start | bytes 1572872 | tf_op jit(solution)/shard_map/ppermute | solution.py:199
  60.4 14.0 %copy-start.2 = (bf16[256,256]{1,0:T(8,128)(2,1)S(1)}, bf16[256,256]{1,0:T(8,128)(2,1)}, u32[]{:S(2)}) copy-start(bf16[256,256]{1,0:T(8,128)(2,1)} %w_msg.3) | copy-start | bytes 393220
  60.4 14.0 %copy-start.3 = (bf16[256,256]{1,0:T(8,128)(2,1)S(1)}, bf16[256,256]{1,0:T(8,128)(2,1)}, u32[]{:S(2)}) copy-start(bf16[256,256]{1,0:T(8,128)(2,1)} %w_out.1) | copy-start | bytes 393220
  60.4 14.0 %copy-start.4 = (bf16[1,128,256]{2,1,0:T(8,128)(2,1)S(1)}, bf16[1,128,256]{2,1,0:T(8,128)(2,1)}, u32[]{:S(2)}) copy-start(bf16[1,128,256]{2,1,0:T(8,128)(2,1)} %param.9) | copy-start | bytes 196612
  91.0 4.6 %collective-permute-start.1 = (bf16[8,384,128]{2,1,0:T(8,128)(2,1)S(1)}, bf16[8,384,128]{2,1,0:T(8,128)(2,1)S(1)}, u32[]{:S(2)}, u32[]{:S(2)}) collective-permute-start(bf16[8,384,128]{2,1,0:T(8,128)(2,1)S(1)} %all_to_all.26.held), channel_id=1, source_target_pairs={{0,16},{16,0},{32,48},{48,32},{64,80},{80,64},{96,112},{112,96},{1... | collective-permute-start | bytes 2359304 | tf_op jit(solution)/shard_map/ppermute | solution.py:213
  149.2 26.2 %all-to-all-start.4 = ((f32[16,64,128]{2,1,0:T(8,128)}), f32[16,64,128]{2,1,0:T(8,128)S(1)}, u32[]{:S(2)}, u32[]{:S(2)}) async-start(f32[16,64,128]{2,1,0:T(8,128)} %weights_sum.1), calls=%async_computation.4 | async-start | bytes 1048576 | tf_op jit(solution)/shard_map/all_to_all | solution.py:238

commit v2 on v1

--- a/solution.py
+++ b/solution.py
@@ -7,47 +7,56 @@
 from jax.experimental.pallas import tpu as pltpu
 from jax.sharding import PartitionSpec as P
 
-ring_depth = 16
+ring_depth = 8
+group_tiles = 8
 f32 = jnp.float32
 bf16 = jnp.bfloat16
 
 
-def stream_tiles(live, tiles, ring, sems, consume):
-    def copy(slot):
-        place = lax.rem(slot, ring_depth)
-        return pltpu.make_async_copy(tiles.at[slot], ring.at[place], sems.at[place])
-
-    def begin(slot, carry):
-        copy(slot).start()
-        return carry
-
-    lax.fori_loop(0, jnp.minimum(live, ring_depth), begin, 0)
-
-    def step(slot, carry):
-        copy(slot).wait()
-        consume(slot, ring[lax.rem(slot, ring_depth)])
-
-        @pl.when(slot + ring_depth < live)
-        def _():
-            copy(slot + ring_depth).start()
-
-        return carry
-
-    return lax.fori_loop(0, live, step, 0)
+def add_group(first, live, tiles, product, target, acc):
+    spare = acc.shape[0] - 1
+    slots = [first + at for at in range(group_tiles)]
+    products = [product(slot, tiles[at]) for at, slot in enumerate(slots)]
+    for slot, term in zip(slots, products):
+        acc[jnp.where(slot < live, target[slot], spare)] += term
 
 
 def forward_kernel(source, target, live, core, rows, tiles, kept, sent, acc, ring, sems):
     half = kept.shape[1]
+    depth = ring.shape[0]
+    steps = lax.div(live[0] + group_tiles - 1, group_tiles)
+
+    def copy(step):
+        place = lax.rem(step, depth)
+        return pltpu.make_async_copy(
+            tiles.at[pl.ds(step * group_tiles, group_tiles)], ring.at[place], sems.at[place]
+        )
+
+    def begin(step, carry):
+        copy(step).start()
+        return carry
+
+    lax.fori_loop(0, jnp.minimum(steps, depth), begin, 0)
     acc[...] = jnp.zeros_like(acc)
 
-    def consume(slot, tile):
-        block = target[slot]
-        acc[block] += jnp.dot(tile, rows[source[slot]], preferred_element_type=f32)
-
-    stream_tiles(live[0], tiles, ring, sems, consume)
+    def product(slot, tile):
+        return jnp.dot(tile, rows[source[slot]], preferred_element_type=f32)
+
+    def advance(step, carry):
+        copy(step).wait()
+        held = ring.at[lax.rem(step, depth)]
+        add_group(step * group_tiles, live[0], held, product, target, acc)
+
+        @pl.when(step + depth < steps)
+        def _():
+            copy(step + depth).start()
+
+        return carry
+
+    lax.fori_loop(0, steps, advance, 0)
     own = pl.multiple_of(core[0] * half, half)
     other = pl.multiple_of((1 - core[0]) * half, half)
-    for block in range(acc.shape[0]):
+    for block in range(kept.shape[0]):
         sent[block] = acc[block, pl.ds(other, half), :].astype(bf16)
         kept[block] = acc[block, pl.ds(own, half), :]
 
@@ -89,11 +98,10 @@
 
 
 def backward_kernel(
-    source, target, live, core, held, other, tiles, payload, grads, acc, ring, sems
+    source, target, live, core, held, other, tiles, payload, grads, acc
 ):
     width, lanes = acc.shape[1], held.shape[2]
-    blocks = acc.shape[0]
-    acc[...] = jnp.zeros_like(acc)
+    blocks = acc.shape[0] - 1
     chunk = (held.shape[1] - width) // 2
 
     def place(first, second):
@@ -109,11 +117,17 @@
     def _():
         place(other, held)
 
-    def consume(slot, tile):
-        block = target[slot]
-        acc[block] += jnp.dot(grads[source[slot]], tile, preferred_element_type=f32)
-
-    stream_tiles(live[0], tiles, ring, sems, consume)
+    acc[...] = jnp.zeros_like(acc)
+
+    def product(slot, tile):
+        return jnp.dot(grads[source[slot]], tile, preferred_element_type=f32)
+
+    def advance(step, carry):
+        first = step * group_tiles
+        add_group(first, live[0], tiles.at[pl.ds(first, group_tiles)], product, target, acc)
+        return carry
+
+    lax.fori_loop(0, lax.div(live[0] + group_tiles - 1, group_tiles), advance, 0)
     own = pl.ds(pl.multiple_of(width + core[0] * chunk, chunk), chunk)
     weights = held[0, own, :].astype(f32) + other[0, own, :].astype(f32)
     for block in range(1, held.shape[0]):
@@ -175,14 +189,13 @@
     same_core = [list(range(parity, emit_size, 2)) for parity in range(2)]
     swap = [(member, member ^ 1) for member in range(emit_size)]
     struct = jax.ShapeDtypeStruct
-    any_space = pl.BlockSpec(memory_space=pl.ANY)
-    sweep_scratch = [
-        pltpu.VMEM((ring_depth, tile_dim, tile_dim), bf16),
-        pltpu.SemaphoreType.DMA((ring_depth,)),
-    ]
+    in_hbm = pl.BlockSpec(memory_space=pltpu.HBM)
 
     group_rows = lax.all_to_all(
         jnp.broadcast_to(own_rows[None], (recv_size, facet_rows, width)), "recv", 0, 0, tiled=True
+    )
+    group_rows, emit_slots, recv_slots, live, core = lax.optimization_barrier(
+        (group_rows, emit_slots, recv_slots, live, core)
     )
     kept, sent = pl.pallas_call(
         forward_kernel,
@@ -190,10 +203,14 @@
             struct((recv_blocks, tile_dim // 2, width), f32),
             struct((recv_blocks, tile_dim // 2, width), bf16),
         ),
-        in_specs=in_smem(4) + in_vmem(1) + [any_space],
+        in_specs=in_smem(4) + in_vmem(1) + [in_hbm],
         out_specs=tuple(in_vmem(2)),
-        scratch_shapes=[pltpu.VMEM((recv_blocks, tile_dim, width), f32)] + sweep_scratch,
-        compiler_params=limits(16),
+        scratch_shapes=[
+            pltpu.VMEM((recv_blocks + 1, tile_dim, width), f32),
+            pltpu.VMEM((ring_depth, group_tiles, tile_dim, tile_dim), bf16),
+            pltpu.SemaphoreType.DMA((ring_depth,)),
+        ],
+        compiler_params=limits(48),
         name="forward_sweep",
     )(emit_slots, recv_slots, live, core, group_rows.reshape(emit_blocks, tile_dim, width), values)
     arrived = lax.ppermute(sent, "emit", swap)
@@ -215,14 +232,13 @@
     back = pl.pallas_call(
         backward_kernel,
         out_shape=struct((recv_size, width + chunk // 2, lanes), bf16),
-        in_specs=in_smem(4) + in_vmem(2) + [any_space],
+        in_specs=in_smem(4) + in_vmem(3),
         out_specs=in_vmem(1)[0],
         scratch_shapes=[
             pltpu.VMEM((recv_blocks, width, tile_dim), bf16),
-            pltpu.VMEM((emit_blocks, width, tile_dim), f32),
-        ]
-        + sweep_scratch,
-        compiler_params=limits(16),
+            pltpu.VMEM((emit_blocks + 1, width, tile_dim), f32),
+        ],
+        compiler_params=limits(20),
         name="backward_sweep",
     )(recv_slots, emit_slots, live, core, held, other, values)
     back_terms = lax.all_to_all(back, "recv", 0, 0, tiled=True)

time: 175 us -> 148 us (0.85)
  Pallas kernels: 26.8 us -> 7.38 us
  starting transfers between devices: 33.2 us -> 21.6 us
  blocking collectives: 70.4 us -> 72.6 us
    all_to_all x1, starting transfers between devices: 15.1 us -> 3.76 us  [per_device(): lax.all_to_all(total, 'emit', 0, 0, tiled=True).reshape(4, width, lanes)]
    pallas_call x1, Pallas kernels: 12.2 us -> 2.01 us  [per_device(): pl.pallas_call(backward_kernel, out_shape=struct((recv_size, width + chun...]
    pallas_call x1, Pallas kernels: 12.1 us -> 2.93 us  [per_device(): pl.pallas_call(forward_kernel, out_shape=(struct((recv_blocks, tile_dim /...]
    all_to_all x1, blocking collectives: 13.9 us -> 16.3 us  [per_device(): lax.all_to_all(pair_sum, 'emit', 0, 0, tiled=True, axis_index_groups=same...]
where the time goes in v2:
time: 148 us
  blocking collectives  72.6 us (49%)
  waiting for transfers between devices  38.3 us (26%)
  starting transfers between devices  21.6 us (15%)
  Pallas kernels  7.38 us (5%)
  local copies, waits for them, and re-layouts  5.36 us (4%)
    all_to_all x1, blocking collectives, per_device(): back_terms = lax.all_to_all(back, 'recv', 0, 0, tiled=True)  40.3 us
    all_to_all x1, waiting for transfers between devices, per_device(): lax.all_to_all(jnp.broadcast_to(own_rows[None], (recv_size, facet_rows, w...  24.6 us
    all_to_all x1, blocking collectives, per_device(): lax.all_to_all(pair_sum, 'emit', 0, 0, tiled=True, axis_index_groups=same...  16.3 us
    all_to_all x1, blocking collectives, per_device(): lax.all_to_all(payload, 'emit', 0, 0, tiled=True, axis_index_groups=same_...  16 us
    all_to_all x1, starting transfers between devices, per_device(): lax.all_to_all(jnp.broadcast_to(own_rows[None], (recv_size, facet_rows, w...  10.3 us
    all_to_all x1, waiting for transfers between devices, per_device(): lax.all_to_all(total, 'emit', 0, 0, tiled=True).reshape(4, width, lanes)  10.2 us
    ppermute x1, starting transfers between devices, per_device(): arrived = lax.ppermute(sent, 'emit', swap)  4.9 us
    all_to_all x1, starting transfers between devices, per_device(): lax.all_to_all(total, 'emit', 0, 0, tiled=True).reshape(4, width, lanes)  3.76 us
  transfers between devices with their start and end apart: 4, of which 4 were waited for; matrix products, arithmetic and copies ran while one was open for 0% of the time, Pallas kernels for 1%

profile of v2, /device:TPU:1, one launch (start us, length us, event | category | flops | bytes accessed | tf_op | source)
XLA Modules:
  0.0 147.6 jit_solution(13329909656981413930)
XLA Ops:
  0.6 1.9 %broadcast_in_dim.14 = bf16[16,128,256]{2,1,0:T(8,128)(2,1)} broadcast(bf16[128,256]{1,0:T(8,128)(2,1)} %bitcast.27), dimensions={1,2} | broadcast | bytes 1114112 | tf_op jit(solution)/shard_map/broadcast_in_dim | solution.py:195
  2.6 0.0 copy-start.4
  2.6 0.0 copy-start.5
  2.6 10.3 %all-to-all-start = ((bf16[16,128,256]{2,1,0:T(8,128)(2,1)}), bf16[16,128,256]{2,1,0:T(8,128)(2,1)S(1)}, u32[]{:S(2)}, u32[]{:S(2)}) async-start(bf16[16,128,256]{2,1,0:T(8,128)(2,1)} %broadcast_in_dim.14), calls=%async_computation | async-start | bytes 2097152 | tf_op jit(solution)/shard_map/all_to_all | solution.py:194
  13.5 24.6 %all-to-all-done = bf16[16,128,256]{2,1,0:T(8,128)(2,1)S(1)} async-done(((bf16[16,128,256]{2,1,0:T(8,128)(2,1)}), bf16[16,128,256]{2,1,0:T(8,128)(2,1)S(1)}, u32[]{:S(2)}, u32[]{:S(2)}) %all-to-all-start) | async-done | bytes 1048608 | tf_op jit(solution)/shard_map/all_to_all | solution.py:194
  38.1 0.0 copy-done.4
  38.1 0.0 copy-done.5
  38.1 2.9 %forward_sweep.1 = (f32[8,128,256]{2,1,0:T(8,128)S(1)}, bf16[8,128,256]{2,1,0:T(8,128)(2,1)S(1)}) custom-call(s32[64]{0:T(128)S(1)} %bitcast.21, s32[64]{0:T(128)S(1)} %bitcast.19, s32[1]{0:T(128)} %bitcast.13.live, s32[1]{0:T(128)} %bitcast.4.core, bf16[8,256,256]{2,1,0:T(8,128)(2,1)S(1)} %bitcast.17, bf16[64,256,256]{2,1,0:T(8,128)(2,1)} %bitcast.15), custom_call_target="tpu_custom_call" | custom-call | tf_op jit(solution)/shard_map/forward_sweep/pallas_call | solution.py:200
  41.1 4.9 %collective-permute-start = (bf16[8,128,256]{2,1,0:T(8,128)(2,1)S(1)}, bf16[8,128,256]{2,1,0:T(8,128)(2,1)S(1)}, u32[]{:S(2)}, u32[]{:S(2)}) collective-permute-start(bf16[8,128,256]{2,1,0:T(8,128)(2,1)S(1)} %get-tuple-element.16), channel_id=1, source_target_pairs={{0,16},{16,0},{32,48},{48,32},{64,80},{80,64},{96,112},{112,96},{1... | collective-permute-start | bytes 1572872 | tf_op jit(solution)/shard_map/ppermute | solution.py:216
  46.0 1.5 %collective-permute-done = bf16[8,128,256]{2,1,0:T(8,128)(2,1)S(1)} collective-permute-done((bf16[8,128,256]{2,1,0:T(8,128)(2,1)S(1)}, bf16[8,128,256]{2,1,0:T(8,128)(2,1)S(1)}, u32[]{:S(2)}, u32[]{:S(2)}) %collective-permute-start) | collective-permute-done | bytes 524320 | tf_op jit(solution)/shard_map/ppermute | solution.py:216
  47.5 0.0 copy-start.1
  47.5 0.0 copy-start.2
  47.5 0.0 copy-start.3
  47.5 0.2 add_convert_fusion
  47.7 16.3 %all_to_all.25.terms = bf16[8,128,256]{2,1,0:T(8,128)(2,1)S(1)} all-to-all(bf16[8,128,256]{2,1,0:T(8,128)(2,1)S(1)} %add_convert_fusion), channel_id=1, replica_groups={{0,32,64,96,128,160,192,224},{16,48,80,112,144,176,208,240},{1,33,65,97..., dimensions={0} | all-to-all | bytes 1048576 | tf_op jit(solution)/shard_map/all_to_all | solution.py:218
  64.0 0.0 copy-done.1
  64.0 0.0 copy-done.2
  64.0 0.0 copy-done.3
  64.0 0.6 middle.1
  64.7 16.0 %all_to_all.26.held = bf16[8,384,128]{2,1,0:T(8,128)(2,1)S(1)} all-to-all(bf16[8,384,128]{2,1,0:T(8,128)(2,1)S(1)} %middle.1), channel_id=1, replica_groups={{0,32,64,96,128,160,192,224},{16,48,80,112,144,176,208,240},{1,33,65,97..., dimensions={0} | all-to-all | bytes 1572864 | tf_op jit(solution)/shard_map/all_to_all | solution.py:229
  80.6 2.7 %collective-permute-start.1 = (bf16[8,384,128]{2,1,0:T(8,128)(2,1)S(1)}, bf16[8,384,128]{2,1,0:T(8,128)(2,1)S(1)}, u32[]{:S(2)}, u32[]{:S(2)}) collective-permute-start(bf16[8,384,128]{2,1,0:T(8,128)(2,1)S(1)} %all_to_all.26.held), channel_id=1, source_target_pairs={{0,16},{16,0},{32,48},{48,32},{64,80},{80,64},{96,112},{112,96},{1... | collective-permute-start | bytes 2359304 | tf_op jit(solution)/shard_map/ppermute | solution.py:230
  83.3 1.9 %collective-permute-done.1.other = bf16[8,384,128]{2,1,0:T(8,128)(2,1)S(1)} collective-permute-done((bf16[8,384,128]{2,1,0:T(8,128)(2,1)S(1)}, bf16[8,384,128]{2,1,0:T(8,128)(2,1)S(1)}, u32[]{:S(2)}, u32[]{:S(2)}) %collective-permute-start.1) | collective-permute-done | bytes 786464 | tf_op jit(solution)/shard_map/ppermute | solution.py:230
  85.2 0.0 copy-start
  85.2 3.4 %copy-done = bf16[1,1,64,256,256]{4,3,2,1,0:T(8,128)(2,1)S(1)} copy-done((bf16[1,1,64,256,256]{4,3,2,1,0:T(8,128)(2,1)S(1)}, bf16[1,1,64,256,256]{4,3,2,1,0:T(8,128)(2,1)}, u32[]{:S(2)}) %copy-start) | copy-done | bytes 8388632
  88.6 2.0 %backward_sweep.1 = bf16[16,320,128]{2,1,0:T(8,128)(2,1)S(1)} custom-call(s32[64]{0:T(128)S(1)} %bitcast.20, s32[64]{0:T(128)S(1)} %bitcast.22, s32[1]{0:T(128)} %bitcast.14.live, s32[1]{0:T(128)} %bitcast.4.core, bf16[8,384,128]{2,1,0:T(8,128)(2,1)S(1)} %all_to_all.26.held, bf16[8,384,128]{2,1,0:T(8,128)(2,1)S(1)} %collective-permute-done.1.other, ...), custom_call_target="tpu_custom_call" | custom-call | tf_op jit(solution)/shard_map/backward_sweep/pallas_call | solution.py:232
  90.6 40.3 %all_to_all.27.terms = bf16[16,320,128]{2,1,0:T(8,128)(2,1)S(1)} all-to-all(bf16[16,320,128]{2,1,0:T(8,128)(2,1)S(1)} %backward_sweep.1), channel_id=1, replica_groups=mesh['emit'=16,'recv'=16] {'recv'}, dimensions={0} | all-to-all | bytes 2621440 | tf_op jit(solution)/shard_map/all_to_all | solution.py:244
  130.9 0.9 weights_sum.1
  131.8 3.8 %all-to-all-start.4 = ((f32[16,64,128]{2,1,0:T(8,128)}), f32[16,64,128]{2,1,0:T(8,128)S(1)}, u32[]{:S(2)}, u32[]{:S(2)}) async-start(f32[16,64,128]{2,1,0:T(8,128)} %weights_sum.1), calls=%async_computation.4 | async-start | bytes 1048576 | tf_op jit(solution)/shard_map/all_to_all | solution.py:254
  135.6 1.0 features_grad.1
  136.5 10.2 %all-to-all-done.4 = f32[16,64,128]{2,1,0:T(8,128)S(1)} async-done(((f32[16,64,128]{2,1,0:T(8,128)}), f32[16,64,128]{2,1,0:T(8,128)S(1)}, u32[]{:S(2)}, u32[]{:S(2)}) %all-to-all-start.4) | async-done | bytes 524320 | tf_op jit(solution)/shard_map/all_to_all | solution.py:254
  146.8 0.8 pad_maximum_fusion
  (1 shorter events, 0.0 us)
Async XLA Ops:
  2.6 35.6 %copy-start.4 = (s32[1,1,64]{2,1,0:T(1,128)S(1)}, s32[1,1,64]{2,1,0:T(1,128)}, u32[]{:S(2)}) copy-start(s32[1,1,64]{2,1,0:T(1,128)} %param.14) | copy-start | bytes 772
  2.6 35.6 %copy-start.5 = (s32[1,1,64]{2,1,0:T(1,128)S(1)}, s32[1,1,64]{2,1,0:T(1,128)}, u32[]{:S(2)}) copy-start(s32[1,1,64]{2,1,0:T(1,128)} %param.13) | copy-start | bytes 772
  2.6 35.6 %all-to-all-start = ((bf16[16,128,256]{2,1,0:T(8,128)(2,1)}), bf16[16,128,256]{2,1,0:T(8,128)(2,1)S(1)}, u32[]{:S(2)}, u32[]{:S(2)}) async-start(bf16[16,128,256]{2,1,0:T(8,128)(2,1)} %broadcast_in_dim.14), calls=%async_computation | async-start | bytes 2097152 | tf_op jit(solution)/shard_map/all_to_all | solution.py:194
  41.1 6.4 %collective-permute-start = (bf16[8,128,256]{2,1,0:T(8,128)(2,1)S(1)}, bf16[8,128,256]{2,1,0:T(8,128)(2,1)S(1)}, u32[]{:S(2)}, u32[]{:S(2)}) collective-permute-start(bf16[8,128,256]{2,1,0:T(8,128)(2,1)S(1)} %get-tuple-element.16), channel_id=1, source_target_pairs={{0,16},{16,0},{32,48},{48,32},{64,80},{80,64},{96,112},{112,96},{1... | collective-permute-start | bytes 1572872 | tf_op jit(solution)/shard_map/ppermute | solution.py:216
  47.5 16.5 %copy-start.1 = (bf16[256,256]{1,0:T(8,128)(2,1)S(1)}, bf16[256,256]{1,0:T(8,128)(2,1)}, u32[]{:S(2)}) copy-start(bf16[256,256]{1,0:T(8,128)(2,1)} %w_msg.3) | copy-start | bytes 393220
  47.5 16.5 %copy-start.2 = (bf16[256,256]{1,0:T(8,128)(2,1)S(1)}, bf16[256,256]{1,0:T(8,128)(2,1)}, u32[]{:S(2)}) copy-start(bf16[256,256]{1,0:T(8,128)(2,1)} %w_out.1) | copy-start | bytes 393220
  47.5 16.5 %copy-start.3 = (bf16[1,128,256]{2,1,0:T(8,128)(2,1)S(1)}, bf16[1,128,256]{2,1,0:T(8,128)(2,1)}, u32[]{:S(2)}) copy-start(bf16[1,128,256]{2,1,0:T(8,128)(2,1)} %param.9) | copy-start | bytes 196612
  80.6 4.6 %collective-permute-start.1 = (bf16[8,384,128]{2,1,0:T(8,128)(2,1)S(1)}, bf16[8,384,128]{2,1,0:T(8,128)(2,1)S(1)}, u32[]{:S(2)}, u32[]{:S(2)}) collective-permute-start(bf16[8,384,128]{2,1,0:T(8,128)(2,1)S(1)} %all_to_all.26.held), channel_id=1, source_target_pairs={{0,16},{16,0},{32,48},{48,32},{64,80},{80,64},{96,112},{112,96},{1... | collective-permute-start | bytes 2359304 | tf_op jit(solution)/shard_map/ppermute | solution.py:230
  85.2 3.4 %copy-start = (bf16[1,1,64,256,256]{4,3,2,1,0:T(8,128)(2,1)S(1)}, bf16[1,1,64,256,256]{4,3,2,1,0:T(8,128)(2,1)}, u32[]{:S(2)}) copy-start(bf16[1,1,64,256,256]{4,3,2,1,0:T(8,128)(2,1)} %param.12) | copy-start | bytes 25165828
  131.8 15.0 %all-to-all-start.4 = ((f32[16,64,128]{2,1,0:T(8,128)}), f32[16,64,128]{2,1,0:T(8,128)S(1)}, u32[]{:S(2)}, u32[]{:S(2)}) async-start(f32[16,64,128]{2,1,0:T(8,128)} %weights_sum.1), calls=%async_computation.4 | async-start | bytes 1048576 | tf_op jit(solution)/shard_map/all_to_all | solution.py:254

commit v3 on v2

--- a/solution.py
+++ b/solution.py
@@ -21,10 +21,9 @@
         acc[jnp.where(slot < live, target[slot], spare)] += term
 
 
-def forward_kernel(source, target, live, core, rows, tiles, kept, sent, acc, ring, sems):
-    half = kept.shape[1]
+def sweep(live, tiles, ring, sems, prepare, product, target, acc):
     depth = ring.shape[0]
-    steps = lax.div(live[0] + group_tiles - 1, group_tiles)
+    steps = lax.div(live + group_tiles - 1, group_tiles)
 
     def copy(step):
         place = lax.rem(step, depth)
@@ -38,14 +37,12 @@
 
     lax.fori_loop(0, jnp.minimum(steps, depth), begin, 0)
     acc[...] = jnp.zeros_like(acc)
-
-    def product(slot, tile):
-        return jnp.dot(tile, rows[source[slot]], preferred_element_type=f32)
+    prepare()
 
     def advance(step, carry):
         copy(step).wait()
         held = ring.at[lax.rem(step, depth)]
-        add_group(step * group_tiles, live[0], held, product, target, acc)
+        add_group(step * group_tiles, live, held, product, target, acc)
 
         @pl.when(step + depth < steps)
         def _():
@@ -54,11 +51,35 @@
         return carry
 
     lax.fori_loop(0, steps, advance, 0)
-    own = pl.multiple_of(core[0] * half, half)
-    other = pl.multiple_of((1 - core[0]) * half, half)
+
+
+def forward_kernel(
+    source, target, live, place, own, pair, beside, across, tiles, kept, sent, rows, acc, ring, sems
+):
+    half = kept.shape[1]
+    core, column, height = place[0], place[1], place[2]
+    heights = rows.shape[0]
+
+    def prepare():
+        for held, base, side in (
+            (own, height, column),
+            (pair, height ^ 1, column),
+            (beside, height, 1 - column),
+            (across, height ^ 1, 1 - column),
+        ):
+            at = pl.ds(pl.multiple_of(side * half, half), half)
+            for step in range(held.shape[0]):
+                rows[lax.rem(base + heights - 2 * step, heights), at, :] = held[step]
+
+    def product(slot, tile):
+        return jnp.dot(tile, rows[source[slot]], preferred_element_type=f32)
+
+    sweep(live[0], tiles, ring, sems, prepare, product, target, acc)
+    mine = pl.multiple_of(core * half, half)
+    other = pl.multiple_of((1 - core) * half, half)
     for block in range(kept.shape[0]):
         sent[block] = acc[block, pl.ds(other, half), :].astype(bf16)
-        kept[block] = acc[block, pl.ds(own, half), :]
+        kept[block] = acc[block, pl.ds(mine, half), :]
 
 
 def middle_kernel(terms, cotangent, w_msg, w_out, payload):
@@ -98,62 +119,95 @@
 
 
 def backward_kernel(
-    source, target, live, core, held, other, tiles, payload, grads, acc
+    source, target, live, place, held, other, tiles, own, pair, beside, across, grads, acc, ring, sems
 ):
+    core, column, height = place[0], place[1], place[2]
     width, lanes = acc.shape[1], held.shape[2]
-    blocks = acc.shape[0] - 1
+    heights = acc.shape[0] - 1
     chunk = (held.shape[1] - width) // 2
 
-    def place(first, second):
+    def lay(first, second):
         for block in range(held.shape[0]):
             grads[block, :, :lanes] = first[block, :width, :]
             grads[block, :, lanes:] = second[block, :width, :]
 
-    @pl.when(core[0] == 0)
-    def _():
-        place(held, other)
-
-    @pl.when(core[0] == 1)
-    def _():
-        place(other, held)
-
-    acc[...] = jnp.zeros_like(acc)
+    def prepare():
+        @pl.when(core == 0)
+        def _():
+            lay(held, other)
+
+        @pl.when(core == 1)
+        def _():
+            lay(other, held)
 
     def product(slot, tile):
         return jnp.dot(grads[source[slot]], tile, preferred_element_type=f32)
 
-    def advance(step, carry):
-        first = step * group_tiles
-        add_group(first, live[0], tiles.at[pl.ds(first, group_tiles)], product, target, acc)
-        return carry
-
-    lax.fori_loop(0, lax.div(live[0] + group_tiles - 1, group_tiles), advance, 0)
-    own = pl.ds(pl.multiple_of(width + core[0] * chunk, chunk), chunk)
-    weights = held[0, own, :].astype(f32) + other[0, own, :].astype(f32)
+    sweep(live[0], tiles, ring, sems, prepare, product, target, acc)
+    mine = pl.ds(pl.multiple_of(width + core * chunk, chunk), chunk)
+    weights = held[0, mine, :].astype(f32) + other[0, mine, :].astype(f32)
     for block in range(1, held.shape[0]):
-        weights += held[block, own, :].astype(f32) + other[block, own, :].astype(f32)
+        weights += held[block, mine, :].astype(f32) + other[block, mine, :].astype(f32)
     weights = weights.astype(bf16)
-    for block in range(blocks):
-        for part in range(width // lanes):
-            piece = block * (width // lanes) + part
-            payload[piece, :width, :] = acc[block, :, part * lanes : (part + 1) * lanes].astype(bf16)
-            payload[piece, width:, :] = weights
-
-
-def weights_kernel(terms, total):
-    width = terms.shape[1] - total.shape[1]
-    summed = terms[0, width:, :].astype(f32)
-    for piece in range(1, terms.shape[0]):
-        summed += terms[piece, width:, :].astype(f32)
+    steps = heights // 2
+
+    def hand_out(column):
+        for out, base, side in (
+            (own, height, column),
+            (pair, height ^ 1, column),
+            (beside, height, 1 - column),
+            (across, height ^ 1, 1 - column),
+        ):
+            for step in range(steps):
+                block = acc[lax.rem(base + 2 * step, heights), :, side * lanes : (side + 1) * lanes]
+                out[step * width : (step + 1) * width, :] = block.astype(bf16)
+
+    @pl.when(column == 0)
+    def _():
+        hand_out(0)
+
+    @pl.when(column == 1)
+    def _():
+        hand_out(1)
+
+    for out in (own, pair, beside, across):
+        out[steps * width :, :] = weights
+
+
+def quad_kernel(width, own, pair, beside, across, *outs):
+    chunk = outs[0].shape[0] - width
+
+    def total(at, size):
+        rows = pl.ds(at, size)
+        near = own[rows, :].astype(f32) + pair[rows, :].astype(f32)
+        far = beside[rows, :].astype(f32) + across[rows, :].astype(f32)
+        return (near + far).astype(bf16)
+
+    weights = total(width * len(outs), chunk)
+    for step, out in enumerate(outs):
+        out[:width, :] = total(step * width, width)
+        out[width:, :] = weights
+
+
+def ring_sum(terms, rows):
+    parts = [term[rows, :].astype(f32) for term in terms]
+    while len(parts) > 1:
+        half = len(parts) // 2
+        parts = [near + far for near, far in zip(parts[:half], parts[half:])]
+    return parts[0]
+
+
+def weights_kernel(*refs):
+    terms, total = refs[:-1], refs[-1]
+    chunk = total.shape[1]
+    summed = ring_sum(terms, pl.ds(terms[0].shape[0] - chunk, chunk))
     for piece in range(total.shape[0]):
         total[piece] = summed
 
 
-def features_kernel(terms, w_msg, grad):
-    width = w_msg.shape[0]
-    summed = terms[0, :width, :].astype(f32)
-    for piece in range(1, terms.shape[0]):
-        summed += terms[piece, :width, :].astype(f32)
+def features_kernel(*refs):
+    terms, w_msg, grad = refs[:-2], refs[-2], refs[-1]
+    summed = ring_sum(terms, pl.ds(0, w_msg.shape[0]))
     grad[...] = lax.dot_general(
         summed.astype(bf16), w_msg[...], (((0,), (1,)), ((), ())), preferred_element_type=f32
     ).astype(bf16)
@@ -185,34 +239,54 @@
     emit_slots = tile_emit[0, 0]
     recv_slots = tile_recv[0, 0]
     live = tile_count[0]
-    core = lax.rem(lax.axis_index("emit"), 2)[None]
+    heights = recv_size // 2
+    steps = heights // 2
+    recv_at = lax.axis_index("recv")
+    place = jnp.stack([lax.rem(lax.axis_index("emit"), 2), lax.rem(recv_at, 2), lax.div(recv_at, 2)])
     same_core = [list(range(parity, emit_size, 2)) for parity in range(2)]
     swap = [(member, member ^ 1) for member in range(emit_size)]
     struct = jax.ShapeDtypeStruct
     in_hbm = pl.BlockSpec(memory_space=pltpu.HBM)
-
-    group_rows = lax.all_to_all(
-        jnp.broadcast_to(own_rows[None], (recv_size, facet_rows, width)), "recv", 0, 0, tiled=True
-    )
-    group_rows, emit_slots, recv_slots, live, core = lax.optimization_barrier(
-        (group_rows, emit_slots, recv_slots, live, core)
-    )
+    sweep_scratch = [
+        pltpu.VMEM((ring_depth, group_tiles, tile_dim, tile_dim), bf16),
+        pltpu.SemaphoreType.DMA((ring_depth,)),
+    ]
+
+    def to_quad(array, bits):
+        return lax.ppermute(array, "recv", [(member, member ^ bits) for member in range(recv_size)])
+
+    def along_z(array, step):
+        return lax.ppermute(
+            array, "recv", [(member, (member + 4 * step) % recv_size) for member in range(recv_size)]
+        )
+
+    column_rows = jnp.stack([own_rows] + [along_z(own_rows, step) for step in range(1, steps)])
     kept, sent = pl.pallas_call(
         forward_kernel,
         out_shape=(
             struct((recv_blocks, tile_dim // 2, width), f32),
             struct((recv_blocks, tile_dim // 2, width), bf16),
         ),
-        in_specs=in_smem(4) + in_vmem(1) + [in_hbm],
+        in_specs=in_smem(4) + in_vmem(4) + [in_hbm],
         out_specs=tuple(in_vmem(2)),
         scratch_shapes=[
+            pltpu.VMEM((emit_blocks, tile_dim, width), bf16),
             pltpu.VMEM((recv_blocks + 1, tile_dim, width), f32),
-            pltpu.VMEM((ring_depth, group_tiles, tile_dim, tile_dim), bf16),
-            pltpu.SemaphoreType.DMA((ring_depth,)),
-        ],
+        ]
+        + sweep_scratch,
         compiler_params=limits(48),
         name="forward_sweep",
-    )(emit_slots, recv_slots, live, core, group_rows.reshape(emit_blocks, tile_dim, width), values)
+    )(
+        emit_slots,
+        recv_slots,
+        live,
+        place,
+        column_rows,
+        to_quad(column_rows, 2),
+        to_quad(column_rows, 1),
+        to_quad(column_rows, 3),
+        values,
+    )
     arrived = lax.ppermute(sent, "emit", swap)
     pair_sum = (kept + arrived.astype(f32)).astype(bf16)
     terms = lax.all_to_all(pair_sum, "emit", 0, 0, tiled=True, axis_index_groups=same_core)
@@ -229,37 +303,47 @@
     held = lax.all_to_all(payload, "emit", 0, 0, tiled=True, axis_index_groups=same_core)
     other = lax.ppermute(held, "emit", swap)
 
-    back = pl.pallas_call(
+    spread = struct((steps * width + chunk // 2, lanes), bf16)
+    own, pair, beside, across = pl.pallas_call(
         backward_kernel,
-        out_shape=struct((recv_size, width + chunk // 2, lanes), bf16),
-        in_specs=in_smem(4) + in_vmem(3),
-        out_specs=in_vmem(1)[0],
+        out_shape=(spread,) * 4,
+        in_specs=in_smem(4) + in_vmem(2) + [in_hbm],
+        out_specs=tuple(in_vmem(4)),
         scratch_shapes=[
             pltpu.VMEM((recv_blocks, width, tile_dim), bf16),
             pltpu.VMEM((emit_blocks + 1, width, tile_dim), f32),
-        ],
-        compiler_params=limits(20),
+        ]
+        + sweep_scratch,
+        compiler_params=limits(48),
         name="backward_sweep",
-    )(recv_slots, emit_slots, live, core, held, other, values)
-    back_terms = lax.all_to_all(back, "recv", 0, 0, tiled=True)
+    )(recv_slots, emit_slots, live, place, held, other, values)
+    terms = pl.pallas_call(
+        functools.partial(quad_kernel, width),
+        out_shape=(struct((width + chunk // 2, lanes), bf16),) * steps,
+        in_specs=in_vmem(4),
+        out_specs=tuple(in_vmem(steps)),
+        compiler_params=limits(8),
+        name="quad_sum",
+    )(own, to_quad(pair, 2), to_quad(beside, 1), to_quad(across, 3))
+    terms = [terms[0]] + [along_z(terms[step], step) for step in range(1, steps)]
 
     total = pl.pallas_call(
         weights_kernel,
         out_shape=struct((emit_size, chunk // 2, lanes), f32),
-        in_specs=in_vmem(1),
+        in_specs=in_vmem(steps),
         out_specs=in_vmem(1)[0],
         compiler_params=limits(8),
         name="weights_sum",
-    )(back_terms)
+    )(*terms)
     gathered = lax.all_to_all(total, "emit", 0, 0, tiled=True).reshape(4, width, lanes)
     grad_features = pl.pallas_call(
         features_kernel,
         out_shape=struct((facet_rows, width), bf16),
-        in_specs=in_vmem(2),
+        in_specs=in_vmem(steps + 1),
         out_specs=in_vmem(1)[0],
         compiler_params=limits(8),
         name="features_grad",
-    )(back_terms, w_msg)[None]
+    )(*terms, w_msg)[None]
     grad_w_out = jnp.concatenate([gathered[0], gathered[1]], axis=1)
     grad_w_msg = jnp.concatenate([gathered[2], gathered[3]], axis=1)
     return (grad_features, grad_w_msg, grad_w_out)

time: 148 us -> 129 us (0.87)
  blocking collectives: 72.6 us -> 33.3 us
  waiting for transfers between devices: 38.3 us -> 49 us
  starting transfers between devices: 21.6 us -> 29.9 us
  local copies, waits for them, and re-layouts: 5.36 us -> 1.37 us
  Pallas kernels: 7.38 us -> 11.3 us
    all_to_all x1 -> x0, blocking collectives: 40.3 us -> none  [per_device(): back_terms = lax.all_to_all(back, 'recv', 0, 0, tiled=True)]
    ppermute x0 -> x12, waiting for transfers between devices: none -> 34.9 us  [the longest x6 22.7 us: to_quad(): lax.ppermute(array, 'recv', [(member, member ^ bits) for member in range(...]
    all_to_all x1 -> x0, waiting for transfers between devices: 24.6 us -> none  [per_device(): lax.all_to_all(jnp.broadcast_to(own_rows[None], (recv_size, facet_rows, w...]
    ppermute x0 -> x12, starting transfers between devices: none -> 23.1 us  [the longest x6 17.6 us: along_z(): lax.ppermute(array, 'recv', [(member, (member + 4 * step) % recv_size) fo...]
    all_to_all x1 -> x0, starting transfers between devices: 10.3 us -> none  [per_device(): lax.all_to_all(jnp.broadcast_to(own_rows[None], (recv_size, facet_rows, w...]
    ppermute x1, starting transfers between devices: 4.9 us -> 0.09 us  [per_device(): arrived = lax.ppermute(sent, 'emit', swap)]
    pallas_call x1 -> x2, Pallas kernels: 2.01 us -> 4.57 us  [the longest x1 4.42 us: per_device(): pl.pallas_call(backward_kernel, out_shape=(spread,) * 4, in_specs=in_smem...]
    unnamed x12 -> x14, local copies, waits for them, and re-layouts: 3.4 us -> 1.34 us
  transfers between devices with their start and end apart: 4 -> 15, of which waited for: 4 -> 11; matrix products, arithmetic and copies ran while one was open for 0% -> 0% of each run, Pallas kernels for 1% -> 1%
where the time goes in v3:
time: 129 us; the launch traced here: 128 us
  waiting for transfers between devices  49 us (38%)
  blocking collectives  33.3 us (26%)
  starting transfers between devices  29.9 us (23%)
  Pallas kernels  11.3 us (9%)
  other arithmetic  1.92 us (1%)
  between operations  1.39 us (1%)
  local copies, waits for them, and re-layouts  1.37 us (1%)
    ppermute x6, waiting for transfers between devices, to_quad(): lax.ppermute(array, 'recv', [(member, member ^ bits) for member in range(...  22.7 us
    ppermute x6, starting transfers between devices, along_z(): lax.ppermute(array, 'recv', [(member, (member + 4 * step) % recv_size) fo...  17.6 us
    all_to_all x1, blocking collectives, per_device(): lax.all_to_all(pair_sum, 'emit', 0, 0, tiled=True, axis_index_groups=same...  17.3 us
    all_to_all x1, blocking collectives, per_device(): lax.all_to_all(payload, 'emit', 0, 0, tiled=True, axis_index_groups=same_...  16 us
    ppermute x6, waiting for transfers between devices, along_z(): lax.ppermute(array, 'recv', [(member, (member + 4 * step) % recv_size) fo...  12.1 us
    all_to_all x1, waiting for transfers between devices, per_device(): lax.all_to_all(total, 'emit', 0, 0, tiled=True).reshape(4, width, lanes)  10.3 us
    ppermute x6, starting transfers between devices, to_quad(): lax.ppermute(array, 'recv', [(member, member ^ bits) for member in range(...  5.47 us
    pallas_call x1, Pallas kernels, per_device(): pl.pallas_call(backward_kernel, out_shape=(spread,) * 4, in_specs=in_smem...  4.42 us
  transfers between devices with their start and end apart: 15, of which 11 were waited for; matrix products, arithmetic and copies ran while one was open for 0% of the time, Pallas kernels for 1%

profile of v3, /device:TPU:1, one launch (start us, length us, event | category | flops | bytes accessed | tf_op | source)
XLA Modules:
  0.0 128.2 jit_solution(4630739221719289574)
XLA Ops:
  0.6 0.0 copy-start.4
  0.6 0.0 copy-start.6
  0.7 0.0 copy-start
  0.7 0.0 copy-start.1
  0.7 0.0 copy-start.2
  0.7 6.9 %collective-permute-start.2 = (bf16[128,256]{1,0:T(8,128)(2,1)}, bf16[128,256]{1,0:T(8,128)(2,1)S(1)}, u32[]{:S(2)}, u32[]{:S(2)}) collective-permute-start(bf16[128,256]{1,0:T(8,128)(2,1)} %bitcast.30), channel_id=1, source_target_pairs={{0,12},{1,13},{2,14},{3,15},{4,0},{5,1},{6,2},{7,3},{8,4},{9,5},{1... | collective-permute-start | bytes 196616 | tf_op jit(solution)/shard_map/ppermute | solution.py:259
  7.6 1.0 collective-permute-start.1
  8.6 2.3 %collective-permute-start = (bf16[128,256]{1,0:T(8,128)(2,1)}, bf16[128,256]{1,0:T(8,128)(2,1)S(1)}, u32[]{:S(2)}, u32[]{:S(2)}) collective-permute-start(bf16[128,256]{1,0:T(8,128)(2,1)} %bitcast.32), channel_id=1, source_target_pairs={{0,4},{1,5},{2,6},{3,7},{4,8},{5,9},{6,10},{7,11},{8,12},{9,13},{1... | collective-permute-start | bytes 196616 | tf_op jit(solution)/shard_map/ppermute | solution.py:259
  10.9 0.0 collective-permute-done.2
  10.9 4.2 %collective-permute-done.1 = bf16[128,256]{1,0:T(8,128)(2,1)S(1)} collective-permute-done((bf16[128,256]{1,0:T(8,128)(2,1)}, bf16[128,256]{1,0:T(8,128)(2,1)S(1)}, u32[]{:S(2)}, u32[]{:S(2)}) %collective-permute-start.1) | collective-permute-done | bytes 65568 | tf_op jit(solution)/shard_map/ppermute | solution.py:259
  15.0 0.6 collective-permute-done
  15.7 0.9 pad_maximum_fusion.own
  16.6 2.1 %collective-permute-start.5 = (bf16[4,128,256]{2,1,0:T(8,128)(2,1)S(1)}, bf16[4,128,256]{2,1,0:T(8,128)(2,1)S(1)}, u32[]{:S(2)}, u32[]{:S(2)}) collective-permute-start(bf16[4,128,256]{2,1,0:T(8,128)(2,1)S(1)} %pad_maximum_fusion.own), channel_id=1, source_target_pairs={{0,3},{1,2},{2,1},{3,0},{4,7},{5,6},{6,5},{7,4},{8,11},{9,10},{10,... | collective-permute-start | bytes 786440 | tf_op jit(solution)/shard_map/ppermute | solution.py:256
  18.7 0.2 collective-permute-start.4
  18.9 0.4 collective-permute-start.3
  20.0 0.1 pad_add_fusion.place
  20.0 2.8 %collective-permute-done.5.across = bf16[4,128,256]{2,1,0:T(8,128)(2,1)S(1)} collective-permute-done((bf16[4,128,256]{2,1,0:T(8,128)(2,1)S(1)}, bf16[4,128,256]{2,1,0:T(8,128)(2,1)S(1)}, u32[]{:S(2)}, u32[]{:S(2)}) %collective-permute-start.5) | collective-permute-done | bytes 262176 | tf_op jit(solution)/shard_map/ppermute | solution.py:256
  22.9 7.7 %collective-permute-done.4.beside = bf16[4,128,256]{2,1,0:T(8,128)(2,1)S(1)} collective-permute-done((bf16[4,128,256]{2,1,0:T(8,128)(2,1)S(1)}, bf16[4,128,256]{2,1,0:T(8,128)(2,1)S(1)}, u32[]{:S(2)}, u32[]{:S(2)}) %collective-permute-start.4) | collective-permute-done | bytes 262176 | tf_op jit(solution)/shard_map/ppermute | solution.py:256
  30.6 0.0 collective-permute-done.3.pair
  30.6 0.0 copy-start.3
  30.6 0.7 copy-done.3
  31.3 0.0 copy-start.5
  31.3 0.7 copy-done.5
  31.9 4.4 %forward_sweep.1 = (f32[8,128,256]{2,1,0:T(8,128)S(1)}, bf16[8,128,256]{2,1,0:T(8,128)(2,1)S(1)}) custom-call(s32[64]{0:T(128)S(1)} %bitcast.22, s32[64]{0:T(128)S(1)} %bitcast.20, s32[1]{0:T(128)} %bitcast.17.live, s32[3]{0:T(128)S(1)} %pad_add_fusion.place, bf16[4,128,256]{2,1,0:T(8,128)(2,1)S(1)} %pad_maximum_fusion.own, ...), custom_call_target="tpu_custom_call" | custom-call | tf_op jit(solution)/shard_map/forward_sweep/pallas_call | solution.py:264
  36.3 0.1 collective-permute-start.6
  36.4 1.9 %collective-permute-done.6 = bf16[8,128,256]{2,1,0:T(8,128)(2,1)S(1)} collective-permute-done((bf16[8,128,256]{2,1,0:T(8,128)(2,1)S(1)}, bf16[8,128,256]{2,1,0:T(8,128)(2,1)S(1)}, u32[]{:S(2)}, u32[]{:S(2)}) %collective-permute-start.6) | collective-permute-done | bytes 524320 | tf_op jit(solution)/shard_map/ppermute | solution.py:290
  38.3 0.1 add_convert_fusion
  38.5 17.3 %all_to_all.15.terms = bf16[8,128,256]{2,1,0:T(8,128)(2,1)S(1)} all-to-all(bf16[8,128,256]{2,1,0:T(8,128)(2,1)S(1)} %add_convert_fusion), channel_id=1, replica_groups={{0,32,64,96,128,160,192,224},{16,48,80,112,144,176,208,240},{1,33,65,97..., dimensions={0} | all-to-all | bytes 1048576 | tf_op jit(solution)/shard_map/all_to_all | solution.py:292
  55.8 0.0 copy-done
  55.8 0.0 copy-done.1
  55.8 0.0 copy-done.2
  55.8 0.6 middle.1
  56.4 16.0 %all_to_all.16.held = bf16[8,384,128]{2,1,0:T(8,128)(2,1)S(1)} all-to-all(bf16[8,384,128]{2,1,0:T(8,128)(2,1)S(1)} %middle.1), channel_id=1, replica_groups={{0,32,64,96,128,160,192,224},{16,48,80,112,144,176,208,240},{1,33,65,97..., dimensions={0} | all-to-all | bytes 1572864 | tf_op jit(solution)/shard_map/all_to_all | solution.py:303
  72.4 2.7 %collective-permute-start.7 = (bf16[8,384,128]{2,1,0:T(8,128)(2,1)S(1)}, bf16[8,384,128]{2,1,0:T(8,128)(2,1)S(1)}, u32[]{:S(2)}, u32[]{:S(2)}) collective-permute-start(bf16[8,384,128]{2,1,0:T(8,128)(2,1)S(1)} %all_to_all.16.held), channel_id=1, source_target_pairs={{0,16},{16,0},{32,48},{48,32},{64,80},{80,64},{96,112},{112,96},{1... | collective-permute-start | bytes 2359304 | tf_op jit(solution)/shard_map/ppermute | solution.py:304
  75.1 1.9 %collective-permute-done.7.other = bf16[8,384,128]{2,1,0:T(8,128)(2,1)S(1)} collective-permute-done((bf16[8,384,128]{2,1,0:T(8,128)(2,1)S(1)}, bf16[8,384,128]{2,1,0:T(8,128)(2,1)S(1)}, u32[]{:S(2)}, u32[]{:S(2)}) %collective-permute-start.7) | collective-permute-done | bytes 786464 | tf_op jit(solution)/shard_map/ppermute | solution.py:304
  77.0 0.0 copy-done.4
  77.0 0.0 copy-done.6
  77.0 4.4 %backward_sweep.1 = (bf16[1088,128]{1,0:T(8,128)(2,1)S(1)}, bf16[1088,128]{1,0:T(8,128)(2,1)S(1)}, bf16[1088,128]{1,0:T(8,128)(2,1)S(1)}, bf16[1088,128]{1,0:T(8,128)(2,1)S(1)}) custom-call(s32[64]{0:T(128)S(1)} %bitcast.21, s32[64]{0:T(128)S(1)} %bitcast.23, s32[1]{0:T(128)} %bitcast.18.live, s32[3]{0:T(128)S(1)} %pad_add_fusion.place, ...), custom_call_target="tpu_custom_call" | custom-call | tf_op jit(solution)/shard_map/backward_sweep/pallas_call | solution.py:307
  81.4 0.3 collective-permute-start.8
  81.7 0.0 collective-permute-start.9
  81.7 2.4 %collective-permute-start.10 = (bf16[1088,128]{1,0:T(8,128)(2,1)S(1)}, bf16[1088,128]{1,0:T(8,128)(2,1)S(1)}, u32[]{:S(2)}, u32[]{:S(2)}) collective-permute-start(bf16[1088,128]{1,0:T(8,128)(2,1)S(1)} %get-tuple-element.18), channel_id=1, source_target_pairs={{0,3},{1,2},{2,1},{3,0},{4,7},{5,6},{6,5},{7,4},{8,11},{9,10},{10,... | collective-permute-start | bytes 835592 | tf_op jit(solution)/shard_map/ppermute | solution.py:256
  84.2 6.0 %collective-permute-done.8.pair = bf16[1088,128]{1,0:T(8,128)(2,1)S(1)} collective-permute-done((bf16[1088,128]{1,0:T(8,128)(2,1)S(1)}, bf16[1088,128]{1,0:T(8,128)(2,1)S(1)}, u32[]{:S(2)}, u32[]{:S(2)}) %collective-permute-start.8) | collective-permute-done | bytes 278560 | tf_op jit(solution)/shard_map/ppermute | solution.py:256
  90.1 6.2 %collective-permute-done.9.beside = bf16[1088,128]{1,0:T(8,128)(2,1)S(1)} collective-permute-done((bf16[1088,128]{1,0:T(8,128)(2,1)S(1)}, bf16[1088,128]{1,0:T(8,128)(2,1)S(1)}, u32[]{:S(2)}, u32[]{:S(2)}) %collective-permute-start.9) | collective-permute-done | bytes 278560 | tf_op jit(solution)/shard_map/ppermute | solution.py:256
  96.3 0.0 collective-permute-done.10.across
  96.3 0.1 quad_sum.1
  96.5 2.6 %collective-permute-start.11 = (bf16[320,128]{1,0:T(8,128)(2,1)S(1)}, bf16[320,128]{1,0:T(8,128)(2,1)S(1)}, u32[]{:S(2)}, u32[]{:S(2)}) collective-permute-start(bf16[320,128]{1,0:T(8,128)(2,1)S(1)} %get-tuple-element.20), channel_id=1, source_target_pairs={{0,4},{1,5},{2,6},{3,7},{4,8},{5,9},{6,10},{7,11},{8,12},{9,13},{1... | collective-permute-start | bytes 245768 | tf_op jit(solution)/shard_map/ppermute | solution.py:259
  99.1 3.8 %collective-permute-start.12 = (bf16[320,128]{1,0:T(8,128)(2,1)S(1)}, bf16[320,128]{1,0:T(8,128)(2,1)S(1)}, u32[]{:S(2)}, u32[]{:S(2)}) collective-permute-start(bf16[320,128]{1,0:T(8,128)(2,1)S(1)} %get-tuple-element.21), channel_id=1, source_target_pairs={{0,8},{1,9},{2,10},{3,11},{4,12},{5,13},{6,14},{7,15},{8,0},{9,1},... | collective-permute-start | bytes 245768 | tf_op jit(solution)/shard_map/ppermute | solution.py:259
  102.8 1.1 collective-permute-start.13
  103.9 0.0 collective-permute-done.11.refs_1_
  103.9 5.8 %collective-permute-done.12.refs_2_ = bf16[320,128]{1,0:T(8,128)(2,1)S(1)} collective-permute-done((bf16[320,128]{1,0:T(8,128)(2,1)S(1)}, bf16[320,128]{1,0:T(8,128)(2,1)S(1)}, u32[]{:S(2)}, u32[]{:S(2)}) %collective-permute-start.12) | collective-permute-done | bytes 81952 | tf_op jit(solution)/shard_map/ppermute | solution.py:259
  109.7 1.5 %collective-permute-done.13.refs_3_ = bf16[320,128]{1,0:T(8,128)(2,1)S(1)} collective-permute-done((bf16[320,128]{1,0:T(8,128)(2,1)S(1)}, bf16[320,128]{1,0:T(8,128)(2,1)S(1)}, u32[]{:S(2)}, u32[]{:S(2)}) %collective-permute-start.13) | collective-permute-done | bytes 81952 | tf_op jit(solution)/shard_map/ppermute | solution.py:259
  111.2 0.9 weights_sum.1
  112.1 4.0 %all-to-all-start.2 = ((f32[16,64,128]{2,1,0:T(8,128)}), f32[16,64,128]{2,1,0:T(8,128)S(1)}, u32[]{:S(2)}, u32[]{:S(2)}) async-start(f32[16,64,128]{2,1,0:T(8,128)} %weights_sum.1), calls=%async_computation.2 | async-start | bytes 1048576 | tf_op jit(solution)/shard_map/all_to_all | solution.py:338
  116.1 0.8 features_grad.1
  117.0 10.3 %all-to-all-done.2 = f32[16,64,128]{2,1,0:T(8,128)S(1)} async-done(((f32[16,64,128]{2,1,0:T(8,128)}), f32[16,64,128]{2,1,0:T(8,128)S(1)}, u32[]{:S(2)}, u32[]{:S(2)}) %all-to-all-start.2) | async-done | bytes 524320 | tf_op jit(solution)/shard_map/all_to_all | solution.py:338
  127.3 0.8 pad_maximum_fusion.1
  (1 shorter events, 0.0 us)
Async XLA Ops:
  0.6 76.4 %copy-start.4 = (s32[1,1,64]{2,1,0:T(1,128)S(1)}, s32[1,1,64]{2,1,0:T(1,128)}, u32[]{:S(2)}) copy-start(s32[1,1,64]{2,1,0:T(1,128)} %param.14) | copy-start | bytes 772
  0.6 76.4 %copy-start.6 = (s32[1,1,64]{2,1,0:T(1,128)S(1)}, s32[1,1,64]{2,1,0:T(1,128)}, u32[]{:S(2)}) copy-start(s32[1,1,64]{2,1,0:T(1,128)} %param.13) | copy-start | bytes 772
  0.7 55.1 %copy-start = (bf16[256,256]{1,0:T(8,128)(2,1)S(1)}, bf16[256,256]{1,0:T(8,128)(2,1)}, u32[]{:S(2)}) copy-start(bf16[256,256]{1,0:T(8,128)(2,1)} %refs_4_.1) | copy-start | bytes 393220
  0.7 55.1 %copy-start.1 = (bf16[256,256]{1,0:T(8,128)(2,1)S(1)}, bf16[256,256]{1,0:T(8,128)(2,1)}, u32[]{:S(2)}) copy-start(bf16[256,256]{1,0:T(8,128)(2,1)} %w_out.1) | copy-start | bytes 393220
  0.7 55.1 %copy-start.2 = (bf16[1,128,256]{2,1,0:T(8,128)(2,1)S(1)}, bf16[1,128,256]{2,1,0:T(8,128)(2,1)}, u32[]{:S(2)}) copy-start(bf16[1,128,256]{2,1,0:T(8,128)(2,1)} %param.9) | copy-start | bytes 196612
  0.7 10.2 %collective-permute-start.2 = (bf16[128,256]{1,0:T(8,128)(2,1)}, bf16[128,256]{1,0:T(8,128)(2,1)S(1)}, u32[]{:S(2)}, u32[]{:S(2)}) collective-permute-start(bf16[128,256]{1,0:T(8,128)(2,1)} %bitcast.30), channel_id=1, source_target_pairs={{0,12},{1,13},{2,14},{3,15},{4,0},{5,1},{6,2},{7,3},{8,4},{9,5},{1... | collective-permute-start | bytes 196616 | tf_op jit(solution)/shard_map/ppermute | solution.py:259
  7.6 7.4 %collective-permute-start.1 = (bf16[128,256]{1,0:T(8,128)(2,1)}, bf16[128,256]{1,0:T(8,128)(2,1)S(1)}, u32[]{:S(2)}, u32[]{:S(2)}) collective-permute-start(bf16[128,256]{1,0:T(8,128)(2,1)} %bitcast.31), channel_id=1, source_target_pairs={{0,8},{1,9},{2,10},{3,11},{4,12},{5,13},{6,14},{7,15},{8,0},{9,1},... | collective-permute-start | bytes 196616 | tf_op jit(solution)/shard_map/ppermute | solution.py:259
  8.6 7.1 %collective-permute-start = (bf16[128,256]{1,0:T(8,128)(2,1)}, bf16[128,256]{1,0:T(8,128)(2,1)S(1)}, u32[]{:S(2)}, u32[]{:S(2)}) collective-permute-start(bf16[128,256]{1,0:T(8,128)(2,1)} %bitcast.32), channel_id=1, source_target_pairs={{0,4},{1,5},{2,6},{3,7},{4,8},{5,9},{6,10},{7,11},{8,12},{9,13},{1... | collective-permute-start | bytes 196616 | tf_op jit(solution)/shard_map/ppermute | solution.py:259
  16.6 6.3 %collective-permute-start.5 = (bf16[4,128,256]{2,1,0:T(8,128)(2,1)S(1)}, bf16[4,128,256]{2,1,0:T(8,128)(2,1)S(1)}, u32[]{:S(2)}, u32[]{:S(2)}) collective-permute-start(bf16[4,128,256]{2,1,0:T(8,128)(2,1)S(1)} %pad_maximum_fusion.own), channel_id=1, source_target_pairs={{0,3},{1,2},{2,1},{3,0},{4,7},{5,6},{6,5},{7,4},{8,11},{9,10},{10,... | collective-permute-start | bytes 786440 | tf_op jit(solution)/shard_map/ppermute | solution.py:256
  18.7 11.9 %collective-permute-start.4 = (bf16[4,128,256]{2,1,0:T(8,128)(2,1)S(1)}, bf16[4,128,256]{2,1,0:T(8,128)(2,1)S(1)}, u32[]{:S(2)}, u32[]{:S(2)}) collective-permute-start(bf16[4,128,256]{2,1,0:T(8,128)(2,1)S(1)} %pad_maximum_fusion.own), channel_id=1, source_target_pairs={{0,1},{1,0},{2,3},{3,2},{4,5},{5,4},{6,7},{7,6},{8,9},{9,8},{10,11... | collective-permute-start | bytes 786440 | tf_op jit(solution)/shard_map/ppermute | solution.py:256
  18.9 11.7 %collective-permute-start.3 = (bf16[4,128,256]{2,1,0:T(8,128)(2,1)S(1)}, bf16[4,128,256]{2,1,0:T(8,128)(2,1)S(1)}, u32[]{:S(2)}, u32[]{:S(2)}) collective-permute-start(bf16[4,128,256]{2,1,0:T(8,128)(2,1)S(1)} %pad_maximum_fusion.own), channel_id=1, source_target_pairs={{0,2},{1,3},{2,0},{3,1},{4,6},{5,7},{6,4},{7,5},{8,10},{9,11},{10,... | collective-permute-start | bytes 786440 | tf_op jit(solution)/shard_map/ppermute | solution.py:256
  30.6 0.7 copy-start.3
  31.3 0.7 copy-start.5
  36.3 2.0 %collective-permute-start.6 = (bf16[8,128,256]{2,1,0:T(8,128)(2,1)S(1)}, bf16[8,128,256]{2,1,0:T(8,128)(2,1)S(1)}, u32[]{:S(2)}, u32[]{:S(2)}) collective-permute-start(bf16[8,128,256]{2,1,0:T(8,128)(2,1)S(1)} %get-tuple-element.14), channel_id=1, source_target_pairs={{0,16},{16,0},{32,48},{48,32},{64,80},{80,64},{96,112},{112,96},{1... | collective-permute-start | bytes 1572872 | tf_op jit(solution)/shard_map/ppermute | solution.py:290
  72.4 4.6 %collective-permute-start.7 = (bf16[8,384,128]{2,1,0:T(8,128)(2,1)S(1)}, bf16[8,384,128]{2,1,0:T(8,128)(2,1)S(1)}, u32[]{:S(2)}, u32[]{:S(2)}) collective-permute-start(bf16[8,384,128]{2,1,0:T(8,128)(2,1)S(1)} %all_to_all.16.held), channel_id=1, source_target_pairs={{0,16},{16,0},{32,48},{48,32},{64,80},{80,64},{96,112},{112,96},{1... | collective-permute-start | bytes 2359304 | tf_op jit(solution)/shard_map/ppermute | solution.py:304
  81.4 8.7 %collective-permute-start.8 = (bf16[1088,128]{1,0:T(8,128)(2,1)S(1)}, bf16[1088,128]{1,0:T(8,128)(2,1)S(1)}, u32[]{:S(2)}, u32[]{:S(2)}) collective-permute-start(bf16[1088,128]{1,0:T(8,128)(2,1)S(1)} %get-tuple-element.16), channel_id=1, source_target_pairs={{0,2},{1,3},{2,0},{3,1},{4,6},{5,7},{6,4},{7,5},{8,10},{9,11},{10,... | collective-permute-start | bytes 835592 | tf_op jit(solution)/shard_map/ppermute | solution.py:256
  81.7 14.6 %collective-permute-start.9 = (bf16[1088,128]{1,0:T(8,128)(2,1)S(1)}, bf16[1088,128]{1,0:T(8,128)(2,1)S(1)}, u32[]{:S(2)}, u32[]{:S(2)}) collective-permute-start(bf16[1088,128]{1,0:T(8,128)(2,1)S(1)} %get-tuple-element.17), channel_id=1, source_target_pairs={{0,1},{1,0},{2,3},{3,2},{4,5},{5,4},{6,7},{7,6},{8,9},{9,8},{10,11... | collective-permute-start | bytes 835592 | tf_op jit(solution)/shard_map/ppermute | solution.py:256
  81.7 14.6 %collective-permute-start.10 = (bf16[1088,128]{1,0:T(8,128)(2,1)S(1)}, bf16[1088,128]{1,0:T(8,128)(2,1)S(1)}, u32[]{:S(2)}, u32[]{:S(2)}) collective-permute-start(bf16[1088,128]{1,0:T(8,128)(2,1)S(1)} %get-tuple-element.18), channel_id=1, source_target_pairs={{0,3},{1,2},{2,1},{3,0},{4,7},{5,6},{6,5},{7,4},{8,11},{9,10},{10,... | collective-permute-start | bytes 835592 | tf_op jit(solution)/shard_map/ppermute | solution.py:256
  96.5 7.4 %collective-permute-start.11 = (bf16[320,128]{1,0:T(8,128)(2,1)S(1)}, bf16[320,128]{1,0:T(8,128)(2,1)S(1)}, u32[]{:S(2)}, u32[]{:S(2)}) collective-permute-start(bf16[320,128]{1,0:T(8,128)(2,1)S(1)} %get-tuple-element.20), channel_id=1, source_target_pairs={{0,4},{1,5},{2,6},{3,7},{4,8},{5,9},{6,10},{7,11},{8,12},{9,13},{1... | collective-permute-start | bytes 245768 | tf_op jit(solution)/shard_map/ppermute | solution.py:259
  99.1 10.6 %collective-permute-start.12 = (bf16[320,128]{1,0:T(8,128)(2,1)S(1)}, bf16[320,128]{1,0:T(8,128)(2,1)S(1)}, u32[]{:S(2)}, u32[]{:S(2)}) collective-permute-start(bf16[320,128]{1,0:T(8,128)(2,1)S(1)} %get-tuple-element.21), channel_id=1, source_target_pairs={{0,8},{1,9},{2,10},{3,11},{4,12},{5,13},{6,14},{7,15},{8,0},{9,1},... | collective-permute-start | bytes 245768 | tf_op jit(solution)/shard_map/ppermute | solution.py:259
  102.8 8.4 %collective-permute-start.13 = (bf16[320,128]{1,0:T(8,128)(2,1)S(1)}, bf16[320,128]{1,0:T(8,128)(2,1)S(1)}, u32[]{:S(2)}, u32[]{:S(2)}) collective-permute-start(bf16[320,128]{1,0:T(8,128)(2,1)S(1)} %get-tuple-element.22), channel_id=1, source_target_pairs={{0,12},{1,13},{2,14},{3,15},{4,0},{5,1},{6,2},{7,3},{8,4},{9,5},{1... | collective-permute-start | bytes 245768 | tf_op jit(solution)/shard_map/ppermute | solution.py:259
  112.1 15.2 %all-to-all-start.2 = ((f32[16,64,128]{2,1,0:T(8,128)}), f32[16,64,128]{2,1,0:T(8,128)S(1)}, u32[]{:S(2)}, u32[]{:S(2)}) async-start(f32[16,64,128]{2,1,0:T(8,128)} %weights_sum.1), calls=%async_computation.2 | async-start | bytes 1048576 | tf_op jit(solution)/shard_map/all_to_all | solution.py:338

commit v4 on v3

--- a/solution.py
+++ b/solution.py
@@ -1,5 +1,3 @@
-import functools
-
 import jax
 import jax.numpy as jnp
 from jax import lax
@@ -18,7 +16,7 @@
     slots = [first + at for at in range(group_tiles)]
     products = [product(slot, tiles[at]) for at, slot in enumerate(slots)]
     for slot, term in zip(slots, products):
-        acc[jnp.where(slot < live, target[slot], spare)] += term
+        acc[jnp.where(slot < live, target(slot), spare)] += term
 
 
 def sweep(live, tiles, ring, sems, prepare, product, target, acc):
@@ -53,28 +51,32 @@
     lax.fori_loop(0, steps, advance, 0)
 
 
+def unpack(numbers, slots):
+    live, core, column, parity = (numbers[at] for at in range(4))
+    return live, core, column, parity, lambda slot: numbers[4 + slot], lambda slot: numbers[4 + slots + slot]
+
+
 def forward_kernel(
-    source, target, live, place, own, pair, beside, across, tiles, kept, sent, rows, acc, ring, sems
+    numbers, own, pair, beside, across, tiles, kept, sent, rows, acc, ring, sems
 ):
     half = kept.shape[1]
-    core, column, height = place[0], place[1], place[2]
-    heights = rows.shape[0]
+    live, core, column, parity, emit_block, recv_block = unpack(numbers, tiles.shape[0])
 
     def prepare():
-        for held, base, side in (
-            (own, height, column),
-            (pair, height ^ 1, column),
-            (beside, height, 1 - column),
-            (across, height ^ 1, 1 - column),
+        for held, side, odd in (
+            (own, column, parity),
+            (pair, column, 1 - parity),
+            (beside, 1 - column, parity),
+            (across, 1 - column, 1 - parity),
         ):
             at = pl.ds(pl.multiple_of(side * half, half), half)
             for step in range(held.shape[0]):
-                rows[lax.rem(base + heights - 2 * step, heights), at, :] = held[step]
+                rows[2 * step + odd, at, :] = held[step]
 
     def product(slot, tile):
-        return jnp.dot(tile, rows[source[slot]], preferred_element_type=f32)
-
-    sweep(live[0], tiles, ring, sems, prepare, product, target, acc)
+        return jnp.dot(tile, rows[emit_block(slot)], preferred_element_type=f32)
+
+    sweep(live, tiles, ring, sems, prepare, product, recv_block, acc)
     mine = pl.multiple_of(core * half, half)
     other = pl.multiple_of((1 - core) * half, half)
     for block in range(kept.shape[0]):
@@ -119,12 +121,12 @@
 
 
 def backward_kernel(
-    source, target, live, place, held, other, tiles, own, pair, beside, across, grads, acc, ring, sems
+    numbers, held, other, tiles, own, pair, beside, across, grads, acc, ring, sems
 ):
-    core, column, height = place[0], place[1], place[2]
+    live, core, column, parity, emit_block, recv_block = unpack(numbers, tiles.shape[0])
     width, lanes = acc.shape[1], held.shape[2]
-    heights = acc.shape[0] - 1
     chunk = (held.shape[1] - width) // 2
+    steps = own.shape[0] // width
 
     def lay(first, second):
         for block in range(held.shape[0]):
@@ -141,26 +143,26 @@
             lay(other, held)
 
     def product(slot, tile):
-        return jnp.dot(grads[source[slot]], tile, preferred_element_type=f32)
-
-    sweep(live[0], tiles, ring, sems, prepare, product, target, acc)
+        return jnp.dot(grads[recv_block(slot)], tile, preferred_element_type=f32)
+
+    sweep(live, tiles, ring, sems, prepare, product, emit_block, acc)
     mine = pl.ds(pl.multiple_of(width + core * chunk, chunk), chunk)
     weights = held[0, mine, :].astype(f32) + other[0, mine, :].astype(f32)
     for block in range(1, held.shape[0]):
         weights += held[block, mine, :].astype(f32) + other[block, mine, :].astype(f32)
     weights = weights.astype(bf16)
-    steps = heights // 2
-
-    def hand_out(column):
-        for out, base, side in (
-            (own, height, column),
-            (pair, height ^ 1, column),
-            (beside, height, 1 - column),
-            (across, height ^ 1, 1 - column),
+
+    def hand_out(near):
+        for out, side, odd in (
+            (own, near, parity),
+            (pair, near, 1 - parity),
+            (beside, 1 - near, parity),
+            (across, 1 - near, 1 - parity),
         ):
             for step in range(steps):
-                block = acc[lax.rem(base + 2 * step, heights), :, side * lanes : (side + 1) * lanes]
+                block = acc[2 * step + odd, :, side * lanes : (side + 1) * lanes]
                 out[step * width : (step + 1) * width, :] = block.astype(bf16)
+            out[steps * width :, :] = weights
 
     @pl.when(column == 0)
     def _():
@@ -170,46 +172,42 @@
     def _():
         hand_out(1)
 
-    for out in (own, pair, beside, across):
-        out[steps * width :, :] = weights
-
-
-def quad_kernel(width, own, pair, beside, across, *outs):
-    chunk = outs[0].shape[0] - width
-
-    def total(at, size):
-        rows = pl.ds(at, size)
+
+def quad_kernel(own, pair, beside, across, out):
+    steps = out.shape[0]
+    width = (own.shape[0] - out.shape[1]) // (steps - 1)
+
+    def total(rows):
         near = own[rows, :].astype(f32) + pair[rows, :].astype(f32)
         far = beside[rows, :].astype(f32) + across[rows, :].astype(f32)
         return (near + far).astype(bf16)
 
-    weights = total(width * len(outs), chunk)
-    for step, out in enumerate(outs):
-        out[:width, :] = total(step * width, width)
-        out[width:, :] = weights
-
-
-def ring_sum(terms, rows):
-    parts = [term[rows, :].astype(f32) for term in terms]
-    while len(parts) > 1:
-        half = len(parts) // 2
-        parts = [near + far for near, far in zip(parts[:half], parts[half:])]
-    return parts[0]
-
-
-def weights_kernel(*refs):
-    terms, total = refs[:-1], refs[-1]
+    weights = total(slice(steps * width, None))
+    for step in range(steps):
+        out[step, :width, :] = total(slice(step * width, (step + 1) * width))
+        out[step, width:, :] = weights
+
+
+def step_sum(terms, rows):
+    summed = terms[0, rows, :].astype(f32)
+    for step in range(1, terms.shape[0]):
+        summed += terms[step, rows, :].astype(f32)
+    return summed
+
+
+def weights_kernel(terms, total):
     chunk = total.shape[1]
-    summed = ring_sum(terms, pl.ds(terms[0].shape[0] - chunk, chunk))
+    summed = step_sum(terms, pl.ds(terms.shape[1] - chunk, chunk))
     for piece in range(total.shape[0]):
         total[piece] = summed
 
 
-def features_kernel(*refs):
-    terms, w_msg, grad = refs[:-2], refs[-2], refs[-1]
-    summed = ring_sum(terms, pl.ds(0, w_msg.shape[0]))
+def features_kernel(terms, w_msg, grad):
     grad[...] = lax.dot_general(
-        summed.astype(bf16), w_msg[...], (((0,), (1,)), ((), ())), preferred_element_type=f32
+        step_sum(terms, pl.ds(0, w_msg.shape[0])).astype(bf16),
+        w_msg[...],
+        (((0,), (1,)), ((), ())),
+        preferred_element_type=f32,
     ).astype(bf16)
 
 
@@ -236,13 +234,13 @@
     chips = emit_size // 2
     lanes = width // 2
     values = tile_vals[0, 0]
-    emit_slots = tile_emit[0, 0]
-    recv_slots = tile_recv[0, 0]
-    live = tile_count[0]
-    heights = recv_size // 2
-    steps = heights // 2
+    steps = recv_size // 4
     recv_at = lax.axis_index("recv")
-    place = jnp.stack([lax.rem(lax.axis_index("emit"), 2), lax.rem(recv_at, 2), lax.div(recv_at, 2)])
+    column, parity = lax.rem(recv_at, 2), lax.rem(lax.div(recv_at, 2), 2)
+    core = lax.rem(lax.axis_index("emit"), 2)
+    numbers = jnp.concatenate(
+        [tile_count[0], core[None], column[None], parity[None], tile_emit[0, 0], tile_recv[0, 0]]
+    )
     same_core = [list(range(parity, emit_size, 2)) for parity in range(2)]
     swap = [(member, member ^ 1) for member in range(emit_size)]
     struct = jax.ShapeDtypeStruct
@@ -255,19 +253,18 @@
     def to_quad(array, bits):
         return lax.ppermute(array, "recv", [(member, member ^ bits) for member in range(recv_size)])
 
-    def along_z(array, step):
-        return lax.ppermute(
-            array, "recv", [(member, (member + 4 * step) % recv_size) for member in range(recv_size)]
-        )
-
-    column_rows = jnp.stack([own_rows] + [along_z(own_rows, step) for step in range(1, steps)])
+    def along_z(array):
+        groups = [list(range(first, recv_size, 4)) for first in range(4)]
+        return lax.all_to_all(array, "recv", 0, 0, tiled=True, axis_index_groups=groups)
+
+    column_rows = along_z(jnp.broadcast_to(own_rows[None], (steps, facet_rows, width)))
     kept, sent = pl.pallas_call(
         forward_kernel,
         out_shape=(
             struct((recv_blocks, tile_dim // 2, width), f32),
             struct((recv_blocks, tile_dim // 2, width), bf16),
         ),
-        in_specs=in_smem(4) + in_vmem(4) + [in_hbm],
+        in_specs=in_smem(1) + in_vmem(4) + [in_hbm],
         out_specs=tuple(in_vmem(2)),
         scratch_shapes=[
             pltpu.VMEM((emit_blocks, tile_dim, width), bf16),
@@ -277,10 +274,7 @@
         compiler_params=limits(48),
         name="forward_sweep",
     )(
-        emit_slots,
-        recv_slots,
-        live,
-        place,
+        numbers,
         column_rows,
         to_quad(column_rows, 2),
         to_quad(column_rows, 1),
@@ -307,7 +301,7 @@
     own, pair, beside, across = pl.pallas_call(
         backward_kernel,
         out_shape=(spread,) * 4,
-        in_specs=in_smem(4) + in_vmem(2) + [in_hbm],
+        in_specs=in_smem(1) + in_vmem(2) + [in_hbm],
         out_specs=tuple(in_vmem(4)),
         scratch_shapes=[
             pltpu.VMEM((recv_blocks, width, tile_dim), bf16),
@@ -316,34 +310,34 @@
         + sweep_scratch,
         compiler_params=limits(48),
         name="backward_sweep",
-    )(recv_slots, emit_slots, live, place, held, other, values)
+    )(numbers, held, other, values)
     terms = pl.pallas_call(
-        functools.partial(quad_kernel, width),
-        out_shape=(struct((width + chunk // 2, lanes), bf16),) * steps,
+        quad_kernel,
+        out_shape=struct((steps, width + chunk // 2, lanes), bf16),
         in_specs=in_vmem(4),
-        out_specs=tuple(in_vmem(steps)),
+        out_specs=in_vmem(1)[0],
         compiler_params=limits(8),
         name="quad_sum",
     )(own, to_quad(pair, 2), to_quad(beside, 1), to_quad(across, 3))
-    terms = [terms[0]] + [along_z(terms[step], step) for step in range(1, steps)]
+    terms = along_z(terms)
 
     total = pl.pallas_call(
         weights_kernel,
         out_shape=struct((emit_size, chunk // 2, lanes), f32),
-        in_specs=in_vmem(steps),
+        in_specs=in_vmem(1),
         out_specs=in_vmem(1)[0],
         compiler_params=limits(8),
         name="weights_sum",
-    )(*terms)
+    )(terms)
     gathered = lax.all_to_all(total, "emit", 0, 0, tiled=True).reshape(4, width, lanes)
     grad_features = pl.pallas_call(
         features_kernel,
         out_shape=struct((facet_rows, width), bf16),
-        in_specs=in_vmem(steps + 1),
+        in_specs=in_vmem(2),
         out_specs=in_vmem(1)[0],
         compiler_params=limits(8),
         name="features_grad",
-    )(*terms, w_msg)[None]
+    )(terms, w_msg)[None]
     grad_w_out = jnp.concatenate([gathered[0], gathered[1]], axis=1)
     grad_w_msg = jnp.concatenate([gathered[2], gathered[3]], axis=1)
     return (grad_features, grad_w_msg, grad_w_out)

time: 129 us -> 131 us (1.016)
  blocking collectives: 33.3 us -> 65 us
  waiting for transfers between devices: 49 us -> 34.1 us
  starting transfers between devices: 29.9 us -> 18.3 us
  Pallas kernels: 11.3 us -> 8.36 us
    all_to_all x0 -> x2, blocking collectives: none -> 33.7 us  [along_z(): lax.all_to_all(array, 'recv', 0, 0, tiled=True, axis_index_groups=groups)]
    ppermute x6 -> x0, starting transfers between devices: 17.6 us -> none  [along_z(): lax.ppermute(array, 'recv', [(member, (member + 4 * step) % recv_size) fo...]
    ppermute x6 -> x0, waiting for transfers between devices: 12.1 us -> none  [along_z(): lax.ppermute(array, 'recv', [(member, (member + 4 * step) % recv_size) fo...]
    ppermute x1, starting transfers between devices: 0.09 us -> 3.36 us  [per_device(): arrived = lax.ppermute(sent, 'emit', swap)]
    ppermute x6, waiting for transfers between devices: 22.7 us -> 20.4 us  [to_quad(): lax.ppermute(array, 'recv', [(member, member ^ bits) for member in range(...]
    all_to_all x1, blocking collectives: 17.3 us -> 15.3 us  [per_device(): lax.all_to_all(pair_sum, 'emit', 0, 0, tiled=True, axis_index_groups=same...]
    all_to_all x1, starting transfers between devices: 4.01 us -> 5.54 us  [per_device(): lax.all_to_all(total, 'emit', 0, 0, tiled=True).reshape(4, width, lanes)]
    pallas_call x1, Pallas kernels: 4.39 us -> 2.93 us  [per_device(): pl.pallas_call(forward_kernel, out_shape=(struct((recv_blocks, tile_dim /...]
  transfers between devices with their start and end apart: 15 -> 9, of which waited for: 11 -> 8; matrix products, arithmetic and copies ran while one was open for 0% -> 1% of each run, Pallas kernels for 1% -> 1%
where the time goes in v4:
time: 131 us; the launch traced here: 130 us
  blocking collectives  65 us (50%)
  waiting for transfers between devices  34.1 us (26%)
  starting transfers between devices  18.3 us (14%)
  Pallas kernels  8.36 us (6%)
  local copies, waits for them, and re-layouts  1.71 us (1%)
  between operations  1.36 us (1%)
    all_to_all x2, blocking collectives, along_z(): lax.all_to_all(array, 'recv', 0, 0, tiled=True, axis_index_groups=groups)  33.7 us
    ppermute x6, waiting for transfers between devices, to_quad(): lax.ppermute(array, 'recv', [(member, member ^ bits) for member in range(...  20.4 us
    all_to_all x1, blocking collectives, per_device(): lax.all_to_all(payload, 'emit', 0, 0, tiled=True, axis_index_groups=same_...  16 us
    all_to_all x1, blocking collectives, per_device(): lax.all_to_all(pair_sum, 'emit', 0, 0, tiled=True, axis_index_groups=same...  15.3 us
    all_to_all x1, waiting for transfers between devices, per_device(): lax.all_to_all(total, 'emit', 0, 0, tiled=True).reshape(4, width, lanes)  10.3 us
    ppermute x6, starting transfers between devices, to_quad(): lax.ppermute(array, 'recv', [(member, member ^ bits) for member in range(...  6.72 us
    all_to_all x1, starting transfers between devices, per_device(): lax.all_to_all(total, 'emit', 0, 0, tiled=True).reshape(4, width, lanes)  5.54 us
    ppermute x1, starting transfers between devices, per_device(): arrived = lax.ppermute(sent, 'emit', swap)  3.36 us
  transfers between devices with their start and end apart: 9, of which 8 were waited for; matrix products, arithmetic and copies ran while one was open for 1% of the time, Pallas kernels for 1%

profile of v4, /device:TPU:1, one launch (start us, length us, event | category | flops | bytes accessed | tf_op | source)
XLA Modules:
  0.0 129.8 jit_solution(15764319627137110005)
XLA Ops:
  0.6 0.0 copy-start
  0.6 0.0 copy-start.1
  0.7 0.0 copy-start.2
  0.7 0.9 broadcast_in_dim.23
  1.6 17.9 %all_to_all.25.own = bf16[4,128,256]{2,1,0:T(8,128)(2,1)S(1)} all-to-all(bf16[4,128,256]{2,1,0:T(8,128)(2,1)S(1)} %broadcast_in_dim.23), channel_id=1, replica_groups={{0,4,8,12},{1,5,9,13},{2,6,10,14},{3,7,11,15},{16,20,24,28},{17,21,25,2..., dimensions={0} | all-to-all | bytes 524288 | tf_op jit(solution)/shard_map/all_to_all | solution.py:258
  19.4 2.2 %collective-permute-start.2 = (bf16[4,128,256]{2,1,0:T(8,128)(2,1)S(1)}, bf16[4,128,256]{2,1,0:T(8,128)(2,1)S(1)}, u32[]{:S(2)}, u32[]{:S(2)}) collective-permute-start(bf16[4,128,256]{2,1,0:T(8,128)(2,1)S(1)} %all_to_all.25.own), channel_id=1, source_target_pairs={{0,3},{1,2},{2,1},{3,0},{4,7},{5,6},{6,5},{7,4},{8,11},{9,10},{10,... | collective-permute-start | bytes 786440 | tf_op jit(solution)/shard_map/ppermute | solution.py:254
  21.6 0.2 collective-permute-start.1
  21.8 0.3 collective-permute-start
  22.7 0.8 concatenate.9.numbers
  23.5 2.2 %collective-permute-done.2.across = bf16[4,128,256]{2,1,0:T(8,128)(2,1)S(1)} collective-permute-done((bf16[4,128,256]{2,1,0:T(8,128)(2,1)S(1)}, bf16[4,128,256]{2,1,0:T(8,128)(2,1)S(1)}, u32[]{:S(2)}, u32[]{:S(2)}) %collective-permute-start.2) | collective-permute-done | bytes 262176 | tf_op jit(solution)/shard_map/ppermute | solution.py:254
  25.7 7.3 %collective-permute-done.1.beside = bf16[4,128,256]{2,1,0:T(8,128)(2,1)S(1)} collective-permute-done((bf16[4,128,256]{2,1,0:T(8,128)(2,1)S(1)}, bf16[4,128,256]{2,1,0:T(8,128)(2,1)S(1)}, u32[]{:S(2)}, u32[]{:S(2)}) %collective-permute-start.1) | collective-permute-done | bytes 262176 | tf_op jit(solution)/shard_map/ppermute | solution.py:254
  33.0 0.0 collective-permute-done.pair
  33.0 2.9 %forward_sweep.1 = (f32[8,128,256]{2,1,0:T(8,128)S(1)}, bf16[8,128,256]{2,1,0:T(8,128)(2,1)S(1)}) custom-call(s32[132]{0:T(256)S(1)} %concatenate.9.numbers, bf16[4,128,256]{2,1,0:T(8,128)(2,1)S(1)} %all_to_all.25.own, bf16[4,128,256]{2,1,0:T(8,128)(2,1)S(1)} %collective-permute-done.pair, bf16[4,128,256]{2,1,0:T(8,128)(2,1)S(1)} %collective-permute-done.1.beside, ...), custom_call_target="tpu_custom_call" | custom-call | tf_op jit(solution)/shard_map/forward_sweep/pallas_call | solution.py:261
  35.9 3.4 %collective-permute-start.3 = (bf16[8,128,256]{2,1,0:T(8,128)(2,1)S(1)}, bf16[8,128,256]{2,1,0:T(8,128)(2,1)S(1)}, u32[]{:S(2)}, u32[]{:S(2)}) collective-permute-start(bf16[8,128,256]{2,1,0:T(8,128)(2,1)S(1)} %get-tuple-element.10), channel_id=1, source_target_pairs={{0,16},{16,0},{32,48},{48,32},{64,80},{80,64},{96,112},{112,96},{1... | collective-permute-start | bytes 1572872 | tf_op jit(solution)/shard_map/ppermute | solution.py:284
  39.3 1.5 %collective-permute-done.3 = bf16[8,128,256]{2,1,0:T(8,128)(2,1)S(1)} collective-permute-done((bf16[8,128,256]{2,1,0:T(8,128)(2,1)S(1)}, bf16[8,128,256]{2,1,0:T(8,128)(2,1)S(1)}, u32[]{:S(2)}, u32[]{:S(2)}) %collective-permute-start.3) | collective-permute-done | bytes 524320 | tf_op jit(solution)/shard_map/ppermute | solution.py:284
  40.8 0.2 add_convert_fusion
  41.0 15.3 %all_to_all.26.terms = bf16[8,128,256]{2,1,0:T(8,128)(2,1)S(1)} all-to-all(bf16[8,128,256]{2,1,0:T(8,128)(2,1)S(1)} %add_convert_fusion), channel_id=1, replica_groups={{0,32,64,96,128,160,192,224},{16,48,80,112,144,176,208,240},{1,33,65,97..., dimensions={0} | all-to-all | bytes 1048576 | tf_op jit(solution)/shard_map/all_to_all | solution.py:286
  56.3 0.0 copy-done
  56.3 0.0 copy-done.1
  56.3 0.0 copy-done.2
  56.3 0.6 middle.1
  56.9 16.0 %all_to_all.27.held = bf16[8,384,128]{2,1,0:T(8,128)(2,1)S(1)} all-to-all(bf16[8,384,128]{2,1,0:T(8,128)(2,1)S(1)} %middle.1), channel_id=1, replica_groups={{0,32,64,96,128,160,192,224},{16,48,80,112,144,176,208,240},{1,33,65,97..., dimensions={0} | all-to-all | bytes 1572864 | tf_op jit(solution)/shard_map/all_to_all | solution.py:297
  72.9 2.7 %collective-permute-start.4 = (bf16[8,384,128]{2,1,0:T(8,128)(2,1)S(1)}, bf16[8,384,128]{2,1,0:T(8,128)(2,1)S(1)}, u32[]{:S(2)}, u32[]{:S(2)}) collective-permute-start(bf16[8,384,128]{2,1,0:T(8,128)(2,1)S(1)} %all_to_all.27.held), channel_id=1, source_target_pairs={{0,16},{16,0},{32,48},{48,32},{64,80},{80,64},{96,112},{112,96},{1... | collective-permute-start | bytes 2359304 | tf_op jit(solution)/shard_map/ppermute | solution.py:298
  75.6 1.9 %collective-permute-done.4.other = bf16[8,384,128]{2,1,0:T(8,128)(2,1)S(1)} collective-permute-done((bf16[8,384,128]{2,1,0:T(8,128)(2,1)S(1)}, bf16[8,384,128]{2,1,0:T(8,128)(2,1)S(1)}, u32[]{:S(2)}, u32[]{:S(2)}) %collective-permute-start.4) | collective-permute-done | bytes 786464 | tf_op jit(solution)/shard_map/ppermute | solution.py:298
  77.5 3.0 %backward_sweep.1 = (bf16[1088,128]{1,0:T(8,128)(2,1)S(1)}, bf16[1088,128]{1,0:T(8,128)(2,1)S(1)}, bf16[1088,128]{1,0:T(8,128)(2,1)S(1)}, bf16[1088,128]{1,0:T(8,128)(2,1)S(1)}) custom-call(s32[132]{0:T(256)S(1)} %concatenate.9.numbers, bf16[8,384,128]{2,1,0:T(8,128)(2,1)S(1)} %all_to_all.27.held, bf16[8,384,128]{2,1,0:T(8,128)(2,1)S(1)} %collective-permute-done.4.other, ...), custom_call_target="tpu_custom_call" | custom-call | tf_op jit(solution)/shard_map/backward_sweep/pallas_call | solution.py:301
  80.5 2.2 %collective-permute-start.5 = (bf16[1088,128]{1,0:T(8,128)(2,1)S(1)}, bf16[1088,128]{1,0:T(8,128)(2,1)S(1)}, u32[]{:S(2)}, u32[]{:S(2)}) collective-permute-start(bf16[1088,128]{1,0:T(8,128)(2,1)S(1)} %get-tuple-element.12), channel_id=1, source_target_pairs={{0,2},{1,3},{2,0},{3,1},{4,6},{5,7},{6,4},{7,5},{8,10},{9,11},{10,... | collective-permute-start | bytes 835592 | tf_op jit(solution)/shard_map/ppermute | solution.py:254
  82.7 0.8 collective-permute-start.6
  83.5 1.1 collective-permute-start.7
  84.6 4.4 %collective-permute-done.5.pair = bf16[1088,128]{1,0:T(8,128)(2,1)S(1)} collective-permute-done((bf16[1088,128]{1,0:T(8,128)(2,1)S(1)}, bf16[1088,128]{1,0:T(8,128)(2,1)S(1)}, u32[]{:S(2)}, u32[]{:S(2)}) %collective-permute-start.5) | collective-permute-done | bytes 278560 | tf_op jit(solution)/shard_map/ppermute | solution.py:254
  88.9 1.7 %collective-permute-done.6.beside = bf16[1088,128]{1,0:T(8,128)(2,1)S(1)} collective-permute-done((bf16[1088,128]{1,0:T(8,128)(2,1)S(1)}, bf16[1088,128]{1,0:T(8,128)(2,1)S(1)}, u32[]{:S(2)}, u32[]{:S(2)}) %collective-permute-start.6) | collective-permute-done | bytes 278560 | tf_op jit(solution)/shard_map/ppermute | solution.py:254
  90.7 4.7 %collective-permute-done.7.across = bf16[1088,128]{1,0:T(8,128)(2,1)S(1)} collective-permute-done((bf16[1088,128]{1,0:T(8,128)(2,1)S(1)}, bf16[1088,128]{1,0:T(8,128)(2,1)S(1)}, u32[]{:S(2)}, u32[]{:S(2)}) %collective-permute-start.7) | collective-permute-done | bytes 278560 | tf_op jit(solution)/shard_map/ppermute | solution.py:254
  95.4 0.1 quad_sum.1
  95.6 15.8 %all_to_all.28.terms = bf16[4,320,128]{2,1,0:T(8,128)(2,1)S(1)} all-to-all(bf16[4,320,128]{2,1,0:T(8,128)(2,1)S(1)} %quad_sum.1), channel_id=1, replica_groups={{0,4,8,12},{1,5,9,13},{2,6,10,14},{3,7,11,15},{16,20,24,28},{17,21,25,2..., dimensions={0} | all-to-all | bytes 655360 | tf_op jit(solution)/shard_map/all_to_all | solution.py:258
  111.4 0.8 weights_sum.1
  112.2 5.5 %all-to-all-start.4 = ((f32[16,64,128]{2,1,0:T(8,128)}), f32[16,64,128]{2,1,0:T(8,128)S(1)}, u32[]{:S(2)}, u32[]{:S(2)}) async-start(f32[16,64,128]{2,1,0:T(8,128)} %weights_sum.1), calls=%async_computation.4 | async-start | bytes 1048576 | tf_op jit(solution)/shard_map/all_to_all | solution.py:332
  117.8 0.8 features_grad.1
  118.6 10.3 %all-to-all-done.4 = f32[16,64,128]{2,1,0:T(8,128)S(1)} async-done(((f32[16,64,128]{2,1,0:T(8,128)}), f32[16,64,128]{2,1,0:T(8,128)S(1)}, u32[]{:S(2)}, u32[]{:S(2)}) %all-to-all-start.4) | async-done | bytes 524320 | tf_op jit(solution)/shard_map/all_to_all | solution.py:332
  129.0 0.8 pad_maximum_fusion
  (1 shorter events, 0.0 us)
Async XLA Ops:
  0.6 55.7 %copy-start = (bf16[256,256]{1,0:T(8,128)(2,1)S(1)}, bf16[256,256]{1,0:T(8,128)(2,1)}, u32[]{:S(2)}) copy-start(bf16[256,256]{1,0:T(8,128)(2,1)} %w_msg.3) | copy-start | bytes 393220
  0.6 55.7 %copy-start.1 = (bf16[256,256]{1,0:T(8,128)(2,1)S(1)}, bf16[256,256]{1,0:T(8,128)(2,1)}, u32[]{:S(2)}) copy-start(bf16[256,256]{1,0:T(8,128)(2,1)} %w_out.1) | copy-start | bytes 393220
  0.7 55.6 %copy-start.2 = (bf16[1,128,256]{2,1,0:T(8,128)(2,1)S(1)}, bf16[1,128,256]{2,1,0:T(8,128)(2,1)}, u32[]{:S(2)}) copy-start(bf16[1,128,256]{2,1,0:T(8,128)(2,1)} %param.9) | copy-start | bytes 196612
  19.4 6.2 %collective-permute-start.2 = (bf16[4,128,256]{2,1,0:T(8,128)(2,1)S(1)}, bf16[4,128,256]{2,1,0:T(8,128)(2,1)S(1)}, u32[]{:S(2)}, u32[]{:S(2)}) collective-permute-start(bf16[4,128,256]{2,1,0:T(8,128)(2,1)S(1)} %all_to_all.25.own), channel_id=1, source_target_pairs={{0,3},{1,2},{2,1},{3,0},{4,7},{5,6},{6,5},{7,4},{8,11},{9,10},{10,... | collective-permute-start | bytes 786440 | tf_op jit(solution)/shard_map/ppermute | solution.py:254
  21.6 11.4 %collective-permute-start.1 = (bf16[4,128,256]{2,1,0:T(8,128)(2,1)S(1)}, bf16[4,128,256]{2,1,0:T(8,128)(2,1)S(1)}, u32[]{:S(2)}, u32[]{:S(2)}) collective-permute-start(bf16[4,128,256]{2,1,0:T(8,128)(2,1)S(1)} %all_to_all.25.own), channel_id=1, source_target_pairs={{0,1},{1,0},{2,3},{3,2},{4,5},{5,4},{6,7},{7,6},{8,9},{9,8},{10,11... | collective-permute-start | bytes 786440 | tf_op jit(solution)/shard_map/ppermute | solution.py:254
  21.8 11.2 %collective-permute-start = (bf16[4,128,256]{2,1,0:T(8,128)(2,1)S(1)}, bf16[4,128,256]{2,1,0:T(8,128)(2,1)S(1)}, u32[]{:S(2)}, u32[]{:S(2)}) collective-permute-start(bf16[4,128,256]{2,1,0:T(8,128)(2,1)S(1)} %all_to_all.25.own), channel_id=1, source_target_pairs={{0,2},{1,3},{2,0},{3,1},{4,6},{5,7},{6,4},{7,5},{8,10},{9,11},{10,... | collective-permute-start | bytes 786440 | tf_op jit(solution)/shard_map/ppermute | solution.py:254
  35.9 4.9 %collective-permute-start.3 = (bf16[8,128,256]{2,1,0:T(8,128)(2,1)S(1)}, bf16[8,128,256]{2,1,0:T(8,128)(2,1)S(1)}, u32[]{:S(2)}, u32[]{:S(2)}) collective-permute-start(bf16[8,128,256]{2,1,0:T(8,128)(2,1)S(1)} %get-tuple-element.10), channel_id=1, source_target_pairs={{0,16},{16,0},{32,48},{48,32},{64,80},{80,64},{96,112},{112,96},{1... | collective-permute-start | bytes 1572872 | tf_op jit(solution)/shard_map/ppermute | solution.py:284
  72.9 4.6 %collective-permute-start.4 = (bf16[8,384,128]{2,1,0:T(8,128)(2,1)S(1)}, bf16[8,384,128]{2,1,0:T(8,128)(2,1)S(1)}, u32[]{:S(2)}, u32[]{:S(2)}) collective-permute-start(bf16[8,384,128]{2,1,0:T(8,128)(2,1)S(1)} %all_to_all.27.held), channel_id=1, source_target_pairs={{0,16},{16,0},{32,48},{48,32},{64,80},{80,64},{96,112},{112,96},{1... | collective-permute-start | bytes 2359304 | tf_op jit(solution)/shard_map/ppermute | solution.py:298
  80.5 8.4 %collective-permute-start.5 = (bf16[1088,128]{1,0:T(8,128)(2,1)S(1)}, bf16[1088,128]{1,0:T(8,128)(2,1)S(1)}, u32[]{:S(2)}, u32[]{:S(2)}) collective-permute-start(bf16[1088,128]{1,0:T(8,128)(2,1)S(1)} %get-tuple-element.12), channel_id=1, source_target_pairs={{0,2},{1,3},{2,0},{3,1},{4,6},{5,7},{6,4},{7,5},{8,10},{9,11},{10,... | collective-permute-start | bytes 835592 | tf_op jit(solution)/shard_map/ppermute | solution.py:254
  82.7 8.0 %collective-permute-start.6 = (bf16[1088,128]{1,0:T(8,128)(2,1)S(1)}, bf16[1088,128]{1,0:T(8,128)(2,1)S(1)}, u32[]{:S(2)}, u32[]{:S(2)}) collective-permute-start(bf16[1088,128]{1,0:T(8,128)(2,1)S(1)} %get-tuple-element.13), channel_id=1, source_target_pairs={{0,1},{1,0},{2,3},{3,2},{4,5},{5,4},{6,7},{7,6},{8,9},{9,8},{10,11... | collective-permute-start | bytes 835592 | tf_op jit(solution)/shard_map/ppermute | solution.py:254
  83.5 11.9 %collective-permute-start.7 = (bf16[1088,128]{1,0:T(8,128)(2,1)S(1)}, bf16[1088,128]{1,0:T(8,128)(2,1)S(1)}, u32[]{:S(2)}, u32[]{:S(2)}) collective-permute-start(bf16[1088,128]{1,0:T(8,128)(2,1)S(1)} %get-tuple-element.14), channel_id=1, source_target_pairs={{0,3},{1,2},{2,1},{3,0},{4,7},{5,6},{6,5},{7,4},{8,11},{9,10},{10,... | collective-permute-start | bytes 835592 | tf_op jit(solution)/shard_map/ppermute | solution.py:254
  112.2 16.7 %all-to-all-start.4 = ((f32[16,64,128]{2,1,0:T(8,128)}), f32[16,64,128]{2,1,0:T(8,128)S(1)}, u32[]{:S(2)}, u32[]{:S(2)}) async-start(f32[16,64,128]{2,1,0:T(8,128)} %weights_sum.1), calls=%async_computation.4 | async-start | bytes 1048576 | tf_op jit(solution)/shard_map/all_to_all | solution.py:332

commit v5 on v4

--- a/solution.py
+++ b/solution.py
@@ -53,7 +53,7 @@
 
 def unpack(numbers, slots):
     live, core, column, parity = (numbers[at] for at in range(4))
-    return live, core, column, parity, lambda slot: numbers[4 + slot], lambda slot: numbers[4 + slots + slot]
+    return live, core, column, parity, lambda slot: numbers[5 + slot], lambda slot: numbers[5 + slots + slot]
 
 
 def forward_kernel(
@@ -125,8 +125,7 @@
 ):
     live, core, column, parity, emit_block, recv_block = unpack(numbers, tiles.shape[0])
     width, lanes = acc.shape[1], held.shape[2]
-    chunk = (held.shape[1] - width) // 2
-    steps = own.shape[0] // width
+    steps = own.shape[0]
 
     def lay(first, second):
         for block in range(held.shape[0]):
@@ -146,12 +145,6 @@
         return jnp.dot(grads[recv_block(slot)], tile, preferred_element_type=f32)
 
     sweep(live, tiles, ring, sems, prepare, product, emit_block, acc)
-    mine = pl.ds(pl.multiple_of(width + core * chunk, chunk), chunk)
-    weights = held[0, mine, :].astype(f32) + other[0, mine, :].astype(f32)
-    for block in range(1, held.shape[0]):
-        weights += held[block, mine, :].astype(f32) + other[block, mine, :].astype(f32)
-    weights = weights.astype(bf16)
-
     def hand_out(near):
         for out, side, odd in (
             (own, near, parity),
@@ -161,8 +154,7 @@
         ):
             for step in range(steps):
                 block = acc[2 * step + odd, :, side * lanes : (side + 1) * lanes]
-                out[step * width : (step + 1) * width, :] = block.astype(bf16)
-            out[steps * width :, :] = weights
+                out[step] = block.astype(bf16)
 
     @pl.when(column == 0)
     def _():
@@ -173,41 +165,41 @@
         hand_out(1)
 
 
-def quad_kernel(own, pair, beside, across, out):
-    steps = out.shape[0]
-    width = (own.shape[0] - out.shape[1]) // (steps - 1)
-
-    def total(rows):
-        near = own[rows, :].astype(f32) + pair[rows, :].astype(f32)
-        far = beside[rows, :].astype(f32) + across[rows, :].astype(f32)
-        return (near + far).astype(bf16)
-
-    weights = total(slice(steps * width, None))
-    for step in range(steps):
-        out[step, :width, :] = total(slice(step * width, (step + 1) * width))
-        out[step, width:, :] = weights
-
-
-def step_sum(terms, rows):
-    summed = terms[0, rows, :].astype(f32)
-    for step in range(1, terms.shape[0]):
-        summed += terms[step, rows, :].astype(f32)
-    return summed
+def chunk_kernel(numbers, held, other, out):
+    chunk = out.shape[1]
+    width = held.shape[1] - 2 * chunk
+    mine = pl.ds(pl.multiple_of(width + numbers[1] * chunk, chunk), chunk)
+    weights = held[0, mine, :].astype(f32) + other[0, mine, :].astype(f32)
+    for block in range(1, held.shape[0]):
+        weights += held[block, mine, :].astype(f32) + other[block, mine, :].astype(f32)
+    for piece in range(out.shape[0]):
+        out[piece] = weights.astype(bf16)
+
+
+def quad_kernel(numbers, own, pair, beside, across, *outs):
+    steps = own.shape[0]
+    for step, out in enumerate(outs):
+        block = lax.rem(numbers[4] + step, steps)
+        near = own[block].astype(f32) + pair[block].astype(f32)
+        far = beside[block].astype(f32) + across[block].astype(f32)
+        out[...] = (near + far).astype(bf16)
 
 
 def weights_kernel(terms, total):
-    chunk = total.shape[1]
-    summed = step_sum(terms, pl.ds(terms.shape[1] - chunk, chunk))
+    summed = terms[0].astype(f32)
+    for piece in range(1, terms.shape[0]):
+        summed += terms[piece].astype(f32)
     for piece in range(total.shape[0]):
         total[piece] = summed
 
 
-def features_kernel(terms, w_msg, grad):
+def features_kernel(*refs):
+    terms, w_msg, grad = refs[:-2], refs[-2], refs[-1]
+    summed = terms[0][...].astype(f32)
+    for term in terms[1:]:
+        summed += term[...].astype(f32)
     grad[...] = lax.dot_general(
-        step_sum(terms, pl.ds(0, w_msg.shape[0])).astype(bf16),
-        w_msg[...],
-        (((0,), (1,)), ((), ())),
-        preferred_element_type=f32,
+        summed.astype(bf16), w_msg[...], (((0,), (1,)), ((), ())), preferred_element_type=f32
     ).astype(bf16)
 
 
@@ -239,7 +231,12 @@
     column, parity = lax.rem(recv_at, 2), lax.rem(lax.div(recv_at, 2), 2)
     core = lax.rem(lax.axis_index("emit"), 2)
     numbers = jnp.concatenate(
-        [tile_count[0], core[None], column[None], parity[None], tile_emit[0, 0], tile_recv[0, 0]]
+        [
+            tile_count[0],
+            jnp.stack([core, column, parity, lax.div(recv_at, 4)]),
+            tile_emit[0, 0],
+            tile_recv[0, 0],
+        ]
     )
     same_core = [list(range(parity, emit_size, 2)) for parity in range(2)]
     swap = [(member, member ^ 1) for member in range(emit_size)]
@@ -250,14 +247,26 @@
         pltpu.SemaphoreType.DMA((ring_depth,)),
     ]
 
+    sweep_cost = pl.CostEstimate(
+        flops=2 * values.size * width, bytes_accessed=2 * values.size, transcendentals=0
+    )
+
     def to_quad(array, bits):
         return lax.ppermute(array, "recv", [(member, member ^ bits) for member in range(recv_size)])
 
-    def along_z(array):
-        groups = [list(range(first, recv_size, 4)) for first in range(4)]
-        return lax.all_to_all(array, "recv", 0, 0, tiled=True, axis_index_groups=groups)
-
-    column_rows = along_z(jnp.broadcast_to(own_rows[None], (steps, facet_rows, width)))
+    def along_z(array, step):
+        return lax.ppermute(
+            array, "recv", [(member, (member + 4 * step) % recv_size) for member in range(recv_size)]
+        )
+
+    column_rows = lax.all_to_all(
+        jnp.broadcast_to(own_rows[None], (steps, facet_rows, width)),
+        "recv",
+        0,
+        0,
+        tiled=True,
+        axis_index_groups=[list(range(first, recv_size, 4)) for first in range(4)],
+    )
     kept, sent = pl.pallas_call(
         forward_kernel,
         out_shape=(
@@ -272,6 +281,7 @@
         ]
         + sweep_scratch,
         compiler_params=limits(48),
+        cost_estimate=sweep_cost,
         name="forward_sweep",
     )(
         numbers,
@@ -297,10 +307,19 @@
     held = lax.all_to_all(payload, "emit", 0, 0, tiled=True, axis_index_groups=same_core)
     other = lax.ppermute(held, "emit", swap)
 
-    spread = struct((steps * width + chunk // 2, lanes), bf16)
+    chunks = pl.pallas_call(
+        chunk_kernel,
+        out_shape=struct((recv_size, chunk // 2, lanes), bf16),
+        in_specs=in_smem(1) + in_vmem(2),
+        out_specs=in_vmem(1)[0],
+        compiler_params=limits(8),
+        name="weights_chunk",
+    )(numbers, held, other)
+    chunks = lax.all_to_all(chunks, "recv", 0, 0, tiled=True)
+
     own, pair, beside, across = pl.pallas_call(
         backward_kernel,
-        out_shape=(spread,) * 4,
+        out_shape=(struct((steps, width, lanes), bf16),) * 4,
         in_specs=in_smem(1) + in_vmem(2) + [in_hbm],
         out_specs=tuple(in_vmem(4)),
         scratch_shapes=[
@@ -309,17 +328,18 @@
         ]
         + sweep_scratch,
         compiler_params=limits(48),
+        cost_estimate=sweep_cost,
         name="backward_sweep",
     )(numbers, held, other, values)
     terms = pl.pallas_call(
         quad_kernel,
-        out_shape=struct((steps, width + chunk // 2, lanes), bf16),
-        in_specs=in_vmem(4),
-        out_specs=in_vmem(1)[0],
+        out_shape=(struct((width, lanes), bf16),) * steps,
+        in_specs=in_smem(1) + in_vmem(4),
+        out_specs=tuple(in_vmem(steps)),
         compiler_params=limits(8),
         name="quad_sum",
-    )(own, to_quad(pair, 2), to_quad(beside, 1), to_quad(across, 3))
-    terms = along_z(terms)
+    )(numbers, own, to_quad(pair, 2), to_quad(beside, 1), to_quad(across, 3))
+    chunks, terms = lax.optimization_barrier((chunks, terms))
 
     total = pl.pallas_call(
         weights_kernel,
@@ -328,16 +348,17 @@
         out_specs=in_vmem(1)[0],
         compiler_params=limits(8),
         name="weights_sum",
-    )(terms)
+    )(chunks)
     gathered = lax.all_to_all(total, "emit", 0, 0, tiled=True).reshape(4, width, lanes)
+    terms = [terms[0]] + [along_z(terms[step], step) for step in range(1, steps)]
     grad_features = pl.pallas_call(
         features_kernel,
         out_shape=struct((facet_rows, width), bf16),
-        in_specs=in_vmem(2),
+        in_specs=in_vmem(steps + 1),
         out_specs=in_vmem(1)[0],
         compiler_params=limits(8),
         name="features_grad",
-    )(terms, w_msg)[None]
+    )(*terms, w_msg)[None]
     grad_w_out = jnp.concatenate([gathered[0], gathered[1]], axis=1)
     grad_w_msg = jnp.concatenate([gathered[2], gathered[3]], axis=1)
     return (grad_features, grad_w_msg, grad_w_out)

time: 131 us -> 125 us (0.954)
  blocking collectives: 65 us -> 49.1 us
  starting transfers between devices: 18.3 us -> 27.7 us
  Pallas kernels: 8.36 us -> 13.1 us
  waiting for transfers between devices: 34.1 us -> 30.4 us
    all_to_all x2 -> x1, blocking collectives: 33.7 us -> 17.9 us  [per_device(): lax.all_to_all(jnp.broadcast_to(own_rows[None], (steps, facet_rows, width...]
    all_to_all x1, waiting for transfers between devices: 10.3 us -> 0.01 us  [per_device(): lax.all_to_all(total, 'emit', 0, 0, tiled=True).reshape(4, width, lanes)]
    ppermute x0 -> x3, starting transfers between devices: none -> 7.74 us  [along_z(): lax.ppermute(array, 'recv', [(member, (member + 4 * step) % recv_size) fo...]
    ppermute x0 -> x3, waiting for transfers between devices: none -> 5.03 us  [along_z(): lax.ppermute(array, 'recv', [(member, (member + 4 * step) % recv_size) fo...]
    all_to_all x0 -> x1, starting transfers between devices: none -> 4.79 us  [per_device(): chunks = lax.all_to_all(chunks, 'recv', 0, 0, tiled=True)]
    pallas_call x2 -> x3, Pallas kernels: 3.11 us -> 6.37 us  [the longest x1 4.38 us: per_device(): pl.pallas_call(backward_kernel, out_shape=(struct((steps, width, lanes),...]
    ppermute x6, waiting for transfers between devices: 20.4 us -> 21.9 us  [to_quad(): lax.ppermute(array, 'recv', [(member, member ^ bits) for member in range(...]
    pallas_call x1, Pallas kernels: 2.93 us -> 4.4 us  [per_device(): pl.pallas_call(forward_kernel, out_shape=(struct((recv_blocks, tile_dim /...]
  transfers between devices with their start and end apart: 9 -> 13, of which waited for: 8 -> 8; matrix products, arithmetic and copies ran while one was open for 1% -> 1% of each run, Pallas kernels for 1% -> 5%
where the time goes in v5:
time: 125 us; the launch traced here: 124 us
  blocking collectives  49.1 us (39%)
  waiting for transfers between devices  30.4 us (24%)
  starting transfers between devices  27.7 us (22%)
  Pallas kernels  13.1 us (10%)
  local copies, waits for them, and re-layouts  1.71 us (1%)
  between operations  1.39 us (1%)
    ppermute x6, waiting for transfers between devices, to_quad(): lax.ppermute(array, 'recv', [(member, member ^ bits) for member in range(...  21.9 us
    all_to_all x1, blocking collectives, per_device(): lax.all_to_all(jnp.broadcast_to(own_rows[None], (steps, facet_rows, width...  17.9 us
    all_to_all x1, blocking collectives, per_device(): lax.all_to_all(payload, 'emit', 0, 0, tiled=True, axis_index_groups=same_...  16 us
    all_to_all x1, blocking collectives, per_device(): lax.all_to_all(pair_sum, 'emit', 0, 0, tiled=True, axis_index_groups=same...  15.3 us
    ppermute x3, starting transfers between devices, along_z(): lax.ppermute(array, 'recv', [(member, (member + 4 * step) % recv_size) fo...  7.74 us
    ppermute x6, starting transfers between devices, to_quad(): lax.ppermute(array, 'recv', [(member, member ^ bits) for member in range(...  5.38 us
    all_to_all x1, starting transfers between devices, per_device(): lax.all_to_all(total, 'emit', 0, 0, tiled=True).reshape(4, width, lanes)  5.14 us
    ppermute x3, waiting for transfers between devices, along_z(): lax.ppermute(array, 'recv', [(member, (member + 4 * step) % recv_size) fo...  5.03 us
  transfers between devices with their start and end apart: 13, of which 8 were waited for; matrix products, arithmetic and copies ran while one was open for 1% of the time, Pallas kernels for 5%

profile of v5, /device:TPU:1, one launch (start us, length us, event | category | flops | bytes accessed | tf_op | source)
XLA Modules:
  0.0 124.4 jit_solution(10854249404019358090)
XLA Ops:
  0.6 0.0 copy-start
  0.6 0.0 copy-start.1
  0.7 0.0 copy-start.2
  0.7 0.9 broadcast_in_dim.11
  1.6 17.9 %all_to_all.25.own = bf16[4,128,256]{2,1,0:T(8,128)(2,1)S(1)} all-to-all(bf16[4,128,256]{2,1,0:T(8,128)(2,1)S(1)} %broadcast_in_dim.11), channel_id=1, replica_groups={{0,4,8,12},{1,5,9,13},{2,6,10,14},{3,7,11,15},{16,20,24,28},{17,21,25,2..., dimensions={0} | all-to-all | bytes 524288 | tf_op jit(solution)/shard_map/all_to_all | solution.py:262
  19.4 2.2 %collective-permute-start.2 = (bf16[4,128,256]{2,1,0:T(8,128)(2,1)S(1)}, bf16[4,128,256]{2,1,0:T(8,128)(2,1)S(1)}, u32[]{:S(2)}, u32[]{:S(2)}) collective-permute-start(bf16[4,128,256]{2,1,0:T(8,128)(2,1)S(1)} %all_to_all.25.own), channel_id=1, source_target_pairs={{0,3},{1,2},{2,1},{3,0},{4,7},{5,6},{6,5},{7,4},{8,11},{9,10},{10,... | collective-permute-start | bytes 786440 | tf_op jit(solution)/shard_map/ppermute | solution.py:255
  21.6 0.2 collective-permute-start.1
  21.8 0.3 collective-permute-start
  22.7 0.8 concatenate.9.numbers
  23.5 2.2 %collective-permute-done.2.across = bf16[4,128,256]{2,1,0:T(8,128)(2,1)S(1)} collective-permute-done((bf16[4,128,256]{2,1,0:T(8,128)(2,1)S(1)}, bf16[4,128,256]{2,1,0:T(8,128)(2,1)S(1)}, u32[]{:S(2)}, u32[]{:S(2)}) %collective-permute-start.2) | collective-permute-done | bytes 262176 | tf_op jit(solution)/shard_map/ppermute | solution.py:255
  25.7 7.3 %collective-permute-done.1.beside = bf16[4,128,256]{2,1,0:T(8,128)(2,1)S(1)} collective-permute-done((bf16[4,128,256]{2,1,0:T(8,128)(2,1)S(1)}, bf16[4,128,256]{2,1,0:T(8,128)(2,1)S(1)}, u32[]{:S(2)}, u32[]{:S(2)}) %collective-permute-start.1) | collective-permute-done | bytes 262176 | tf_op jit(solution)/shard_map/ppermute | solution.py:255
  33.0 0.0 collective-permute-done.pair
  33.0 4.4 %forward_sweep.1 = (f32[8,128,256]{2,1,0:T(8,128)S(1)}, bf16[8,128,256]{2,1,0:T(8,128)(2,1)S(1)}) custom-call(s32[133]{0:T(256)S(1)} %concatenate.9.numbers, bf16[4,128,256]{2,1,0:T(8,128)(2,1)S(1)} %all_to_all.25.own, bf16[4,128,256]{2,1,0:T(8,128)(2,1)S(1)} %collective-permute-done.pair, bf16[4,128,256]{2,1,0:T(8,128)(2,1)S(1)} %collective-permute-done.1.beside, ...), custom_call_target="tpu_custom_call" | custom-call | flops 2147483648 | bytes 8388608 | tf_op jit(solution)/shard_map/forward_sweep/pallas_call | solution.py:270
  37.4 1.9 %collective-permute-start.3 = (bf16[8,128,256]{2,1,0:T(8,128)(2,1)S(1)}, bf16[8,128,256]{2,1,0:T(8,128)(2,1)S(1)}, u32[]{:S(2)}, u32[]{:S(2)}) collective-permute-start(bf16[8,128,256]{2,1,0:T(8,128)(2,1)S(1)} %get-tuple-element.19), channel_id=1, source_target_pairs={{0,16},{16,0},{32,48},{48,32},{64,80},{80,64},{96,112},{112,96},{1... | collective-permute-start | bytes 1572872 | tf_op jit(solution)/shard_map/ppermute | solution.py:294
  39.3 1.5 %collective-permute-done.3 = bf16[8,128,256]{2,1,0:T(8,128)(2,1)S(1)} collective-permute-done((bf16[8,128,256]{2,1,0:T(8,128)(2,1)S(1)}, bf16[8,128,256]{2,1,0:T(8,128)(2,1)S(1)}, u32[]{:S(2)}, u32[]{:S(2)}) %collective-permute-start.3) | collective-permute-done | bytes 524320 | tf_op jit(solution)/shard_map/ppermute | solution.py:294
  40.9 0.1 add_convert_fusion
  41.0 15.3 %all_to_all.26.terms = bf16[8,128,256]{2,1,0:T(8,128)(2,1)S(1)} all-to-all(bf16[8,128,256]{2,1,0:T(8,128)(2,1)S(1)} %add_convert_fusion), channel_id=1, replica_groups={{0,32,64,96,128,160,192,224},{16,48,80,112,144,176,208,240},{1,33,65,97..., dimensions={0} | all-to-all | bytes 1048576 | tf_op jit(solution)/shard_map/all_to_all | solution.py:296
  56.3 0.0 copy-done
  56.3 0.0 copy-done.1
  56.3 0.0 copy-done.2
  56.3 0.6 middle.1
  56.9 16.0 %all_to_all.27.held = bf16[8,384,128]{2,1,0:T(8,128)(2,1)S(1)} all-to-all(bf16[8,384,128]{2,1,0:T(8,128)(2,1)S(1)} %middle.1), channel_id=1, replica_groups={{0,32,64,96,128,160,192,224},{16,48,80,112,144,176,208,240},{1,33,65,97..., dimensions={0} | all-to-all | bytes 1572864 | tf_op jit(solution)/shard_map/all_to_all | solution.py:307
  72.9 2.7 %collective-permute-start.4 = (bf16[8,384,128]{2,1,0:T(8,128)(2,1)S(1)}, bf16[8,384,128]{2,1,0:T(8,128)(2,1)S(1)}, u32[]{:S(2)}, u32[]{:S(2)}) collective-permute-start(bf16[8,384,128]{2,1,0:T(8,128)(2,1)S(1)} %all_to_all.27.held), channel_id=1, source_target_pairs={{0,16},{16,0},{32,48},{48,32},{64,80},{80,64},{96,112},{112,96},{1... | collective-permute-start | bytes 2359304 | tf_op jit(solution)/shard_map/ppermute | solution.py:308
  75.6 1.9 %collective-permute-done.4.other = bf16[8,384,128]{2,1,0:T(8,128)(2,1)S(1)} collective-permute-done((bf16[8,384,128]{2,1,0:T(8,128)(2,1)S(1)}, bf16[8,384,128]{2,1,0:T(8,128)(2,1)S(1)}, u32[]{:S(2)}, u32[]{:S(2)}) %collective-permute-start.4) | collective-permute-done | bytes 786464 | tf_op jit(solution)/shard_map/ppermute | solution.py:308
  77.5 1.3 %weights_chunk.1 = bf16[16,64,128]{2,1,0:T(8,128)(2,1)} custom-call(s32[133]{0:T(256)S(1)} %concatenate.9.numbers, bf16[8,384,128]{2,1,0:T(8,128)(2,1)S(1)} %all_to_all.27.held, bf16[8,384,128]{2,1,0:T(8,128)(2,1)S(1)} %collective-permute-done.4.other), custom_call_target="tpu_custom_call" | custom-call | tf_op jit(solution)/shard_map/weights_chunk/pallas_call | solution.py:310
  78.8 4.8 %all-to-all-start.3 = ((bf16[16,64,128]{2,1,0:T(8,128)(2,1)}), bf16[16,64,128]{2,1,0:T(8,128)(2,1)S(1)}, u32[]{:S(2)}, u32[]{:S(2)}) async-start(bf16[16,64,128]{2,1,0:T(8,128)(2,1)} %weights_chunk.1), calls=%async_computation.3 | async-start | bytes 524288 | tf_op jit(solution)/shard_map/all_to_all | solution.py:318
  83.6 4.4 %backward_sweep.1 = (bf16[4,256,128]{2,1,0:T(8,128)(2,1)S(1)}, bf16[4,256,128]{2,1,0:T(8,128)(2,1)S(1)}, bf16[4,256,128]{2,1,0:T(8,128)(2,1)S(1)}, bf16[4,256,128]{2,1,0:T(8,128)(2,1)S(1)}) custom-call(s32[133]{0:T(256)S(1)} %concatenate.9.numbers, bf16[8,384,128]{2,1,0:T(8,128)(2,1)S(1)} %all_to_all.27.held, ...), custom_call_target="tpu_custom_call" | custom-call | flops 2147483648 | bytes 8388608 | tf_op jit(solution)/shard_map/backward_sweep/pallas_call | solution.py:320
  88.0 0.1 collective-permute-start.5
  88.1 0.6 collective-permute-start.6
  88.7 2.0 %collective-permute-start.7 = (bf16[4,256,128]{2,1,0:T(8,128)(2,1)S(1)}, bf16[4,256,128]{2,1,0:T(8,128)(2,1)S(1)}, u32[]{:S(2)}, u32[]{:S(2)}) collective-permute-start(bf16[4,256,128]{2,1,0:T(8,128)(2,1)S(1)} %get-tuple-element.23), channel_id=1, source_target_pairs={{0,3},{1,2},{2,1},{3,0},{4,7},{5,6},{6,5},{7,4},{8,11},{9,10},{10,... | collective-permute-start | bytes 786440 | tf_op jit(solution)/shard_map/ppermute | solution.py:255
  90.7 6.2 %collective-permute-done.5.pair = bf16[4,256,128]{2,1,0:T(8,128)(2,1)S(1)} collective-permute-done((bf16[4,256,128]{2,1,0:T(8,128)(2,1)S(1)}, bf16[4,256,128]{2,1,0:T(8,128)(2,1)S(1)}, u32[]{:S(2)}, u32[]{:S(2)}) %collective-permute-start.5) | collective-permute-done | bytes 262176 | tf_op jit(solution)/shard_map/ppermute | solution.py:255
  97.0 0.0 collective-permute-done.6.beside
  97.0 6.2 %collective-permute-done.7.across = bf16[4,256,128]{2,1,0:T(8,128)(2,1)S(1)} collective-permute-done((bf16[4,256,128]{2,1,0:T(8,128)(2,1)S(1)}, bf16[4,256,128]{2,1,0:T(8,128)(2,1)S(1)}, u32[]{:S(2)}, u32[]{:S(2)}) %collective-permute-start.7) | collective-permute-done | bytes 262176 | tf_op jit(solution)/shard_map/ppermute | solution.py:255
  103.2 0.7 quad_sum.1
  103.9 0.0 all-to-all-done.3.terms
  103.9 0.9 weights_sum.1
  104.7 5.1 %all-to-all-start.4 = ((f32[16,64,128]{2,1,0:T(8,128)}), f32[16,64,128]{2,1,0:T(8,128)S(1)}, u32[]{:S(2)}, u32[]{:S(2)}) async-start(f32[16,64,128]{2,1,0:T(8,128)} %weights_sum.1), calls=%async_computation.4 | async-start | bytes 1048576 | tf_op jit(solution)/shard_map/all_to_all | solution.py:352
  109.9 2.2 %collective-permute-start.8 = (bf16[256,128]{1,0:T(8,128)(2,1)S(1)}, bf16[256,128]{1,0:T(8,128)(2,1)S(1)}, u32[]{:S(2)}, u32[]{:S(2)}) collective-permute-start(bf16[256,128]{1,0:T(8,128)(2,1)S(1)} %get-tuple-element.29), channel_id=1, source_target_pairs={{0,4},{1,5},{2,6},{3,7},{4,8},{5,9},{6,10},{7,11},{8,12},{9,13},{1... | collective-permute-start | bytes 196616 | tf_op jit(solution)/shard_map/ppermute | solution.py:258
  112.1 2.7 %collective-permute-start.9 = (bf16[256,128]{1,0:T(8,128)(2,1)S(1)}, bf16[256,128]{1,0:T(8,128)(2,1)S(1)}, u32[]{:S(2)}, u32[]{:S(2)}) collective-permute-start(bf16[256,128]{1,0:T(8,128)(2,1)S(1)} %get-tuple-element.30), channel_id=1, source_target_pairs={{0,8},{1,9},{2,10},{3,11},{4,12},{5,13},{6,14},{7,15},{8,0},{9,1},... | collective-permute-start | bytes 196616 | tf_op jit(solution)/shard_map/ppermute | solution.py:258
  114.8 2.8 %collective-permute-start.10 = (bf16[256,128]{1,0:T(8,128)(2,1)S(1)}, bf16[256,128]{1,0:T(8,128)(2,1)S(1)}, u32[]{:S(2)}, u32[]{:S(2)}) collective-permute-start(bf16[256,128]{1,0:T(8,128)(2,1)S(1)} %get-tuple-element.31), channel_id=1, source_target_pairs={{0,12},{1,13},{2,14},{3,15},{4,0},{5,1},{6,2},{7,3},{8,4},{9,5},{1... | collective-permute-start | bytes 196616 | tf_op jit(solution)/shard_map/ppermute | solution.py:258
  117.6 0.0 collective-permute-done.8.refs_1_
  117.6 2.3 %collective-permute-done.9.refs_2_ = bf16[256,128]{1,0:T(8,128)(2,1)S(1)} collective-permute-done((bf16[256,128]{1,0:T(8,128)(2,1)S(1)}, bf16[256,128]{1,0:T(8,128)(2,1)S(1)}, u32[]{:S(2)}, u32[]{:S(2)}) %collective-permute-start.9) | collective-permute-done | bytes 65568 | tf_op jit(solution)/shard_map/ppermute | solution.py:258
  119.9 2.7 %collective-permute-done.10.refs_3_ = bf16[256,128]{1,0:T(8,128)(2,1)S(1)} collective-permute-done((bf16[256,128]{1,0:T(8,128)(2,1)S(1)}, bf16[256,128]{1,0:T(8,128)(2,1)S(1)}, u32[]{:S(2)}, u32[]{:S(2)}) %collective-permute-start.10) | collective-permute-done | bytes 65568 | tf_op jit(solution)/shard_map/ppermute | solution.py:258
  122.7 0.8 features_grad.1
  123.5 0.0 all-to-all-done.4
  123.6 0.8 pad_maximum_fusion
  (1 shorter events, 0.0 us)
Async XLA Ops:
  0.6 55.7 %copy-start = (bf16[256,256]{1,0:T(8,128)(2,1)S(1)}, bf16[256,256]{1,0:T(8,128)(2,1)}, u32[]{:S(2)}) copy-start(bf16[256,256]{1,0:T(8,128)(2,1)} %refs_4_.1) | copy-start | bytes 393220
  0.6 55.7 %copy-start.1 = (bf16[256,256]{1,0:T(8,128)(2,1)S(1)}, bf16[256,256]{1,0:T(8,128)(2,1)}, u32[]{:S(2)}) copy-start(bf16[256,256]{1,0:T(8,128)(2,1)} %w_out.1) | copy-start | bytes 393220
  0.7 55.6 %copy-start.2 = (bf16[1,128,256]{2,1,0:T(8,128)(2,1)S(1)}, bf16[1,128,256]{2,1,0:T(8,128)(2,1)}, u32[]{:S(2)}) copy-start(bf16[1,128,256]{2,1,0:T(8,128)(2,1)} %param.9) | copy-start | bytes 196612
  19.4 6.2 %collective-permute-start.2 = (bf16[4,128,256]{2,1,0:T(8,128)(2,1)S(1)}, bf16[4,128,256]{2,1,0:T(8,128)(2,1)S(1)}, u32[]{:S(2)}, u32[]{:S(2)}) collective-permute-start(bf16[4,128,256]{2,1,0:T(8,128)(2,1)S(1)} %all_to_all.25.own), channel_id=1, source_target_pairs={{0,3},{1,2},{2,1},{3,0},{4,7},{5,6},{6,5},{7,4},{8,11},{9,10},{10,... | collective-permute-start | bytes 786440 | tf_op jit(solution)/shard_map/ppermute | solution.py:255
  21.6 11.4 %collective-permute-start.1 = (bf16[4,128,256]{2,1,0:T(8,128)(2,1)S(1)}, bf16[4,128,256]{2,1,0:T(8,128)(2,1)S(1)}, u32[]{:S(2)}, u32[]{:S(2)}) collective-permute-start(bf16[4,128,256]{2,1,0:T(8,128)(2,1)S(1)} %all_to_all.25.own), channel_id=1, source_target_pairs={{0,1},{1,0},{2,3},{3,2},{4,5},{5,4},{6,7},{7,6},{8,9},{9,8},{10,11... | collective-permute-start | bytes 786440 | tf_op jit(solution)/shard_map/ppermute | solution.py:255
  21.8 11.2 %collective-permute-start = (bf16[4,128,256]{2,1,0:T(8,128)(2,1)S(1)}, bf16[4,128,256]{2,1,0:T(8,128)(2,1)S(1)}, u32[]{:S(2)}, u32[]{:S(2)}) collective-permute-start(bf16[4,128,256]{2,1,0:T(8,128)(2,1)S(1)} %all_to_all.25.own), channel_id=1, source_target_pairs={{0,2},{1,3},{2,0},{3,1},{4,6},{5,7},{6,4},{7,5},{8,10},{9,11},{10,... | collective-permute-start | bytes 786440 | tf_op jit(solution)/shard_map/ppermute | solution.py:255
  37.4 3.5 %collective-permute-start.3 = (bf16[8,128,256]{2,1,0:T(8,128)(2,1)S(1)}, bf16[8,128,256]{2,1,0:T(8,128)(2,1)S(1)}, u32[]{:S(2)}, u32[]{:S(2)}) collective-permute-start(bf16[8,128,256]{2,1,0:T(8,128)(2,1)S(1)} %get-tuple-element.19), channel_id=1, source_target_pairs={{0,16},{16,0},{32,48},{48,32},{64,80},{80,64},{96,112},{112,96},{1... | collective-permute-start | bytes 1572872 | tf_op jit(solution)/shard_map/ppermute | solution.py:294
  72.9 4.6 %collective-permute-start.4 = (bf16[8,384,128]{2,1,0:T(8,128)(2,1)S(1)}, bf16[8,384,128]{2,1,0:T(8,128)(2,1)S(1)}, u32[]{:S(2)}, u32[]{:S(2)}) collective-permute-start(bf16[8,384,128]{2,1,0:T(8,128)(2,1)S(1)} %all_to_all.27.held), channel_id=1, source_target_pairs={{0,16},{16,0},{32,48},{48,32},{64,80},{80,64},{96,112},{112,96},{1... | collective-permute-start | bytes 2359304 | tf_op jit(solution)/shard_map/ppermute | solution.py:308
  78.8 25.0 %all-to-all-start.3 = ((bf16[16,64,128]{2,1,0:T(8,128)(2,1)}), bf16[16,64,128]{2,1,0:T(8,128)(2,1)S(1)}, u32[]{:S(2)}, u32[]{:S(2)}) async-start(bf16[16,64,128]{2,1,0:T(8,128)(2,1)} %weights_chunk.1), calls=%async_computation.3 | async-start | bytes 524288 | tf_op jit(solution)/shard_map/all_to_all | solution.py:318
  88.0 9.0 %collective-permute-start.5 = (bf16[4,256,128]{2,1,0:T(8,128)(2,1)S(1)}, bf16[4,256,128]{2,1,0:T(8,128)(2,1)S(1)}, u32[]{:S(2)}, u32[]{:S(2)}) collective-permute-start(bf16[4,256,128]{2,1,0:T(8,128)(2,1)S(1)} %get-tuple-element.21), channel_id=1, source_target_pairs={{0,2},{1,3},{2,0},{3,1},{4,6},{5,7},{6,4},{7,5},{8,10},{9,11},{10,... | collective-permute-start | bytes 786440 | tf_op jit(solution)/shard_map/ppermute | solution.py:255
  88.1 8.9 %collective-permute-start.6 = (bf16[4,256,128]{2,1,0:T(8,128)(2,1)S(1)}, bf16[4,256,128]{2,1,0:T(8,128)(2,1)S(1)}, u32[]{:S(2)}, u32[]{:S(2)}) collective-permute-start(bf16[4,256,128]{2,1,0:T(8,128)(2,1)S(1)} %get-tuple-element.22), channel_id=1, source_target_pairs={{0,1},{1,0},{2,3},{3,2},{4,5},{5,4},{6,7},{7,6},{8,9},{9,8},{10,11... | collective-permute-start | bytes 786440 | tf_op jit(solution)/shard_map/ppermute | solution.py:255
  88.7 14.4 %collective-permute-start.7 = (bf16[4,256,128]{2,1,0:T(8,128)(2,1)S(1)}, bf16[4,256,128]{2,1,0:T(8,128)(2,1)S(1)}, u32[]{:S(2)}, u32[]{:S(2)}) collective-permute-start(bf16[4,256,128]{2,1,0:T(8,128)(2,1)S(1)} %get-tuple-element.23), channel_id=1, source_target_pairs={{0,3},{1,2},{2,1},{3,0},{4,7},{5,6},{6,5},{7,4},{8,11},{9,10},{10,... | collective-permute-start | bytes 786440 | tf_op jit(solution)/shard_map/ppermute | solution.py:255
  104.7 18.8 %all-to-all-start.4 = ((f32[16,64,128]{2,1,0:T(8,128)}), f32[16,64,128]{2,1,0:T(8,128)S(1)}, u32[]{:S(2)}, u32[]{:S(2)}) async-start(f32[16,64,128]{2,1,0:T(8,128)} %weights_sum.1), calls=%async_computation.4 | async-start | bytes 1048576 | tf_op jit(solution)/shard_map/all_to_all | solution.py:352
  109.9 7.7 %collective-permute-start.8 = (bf16[256,128]{1,0:T(8,128)(2,1)S(1)}, bf16[256,128]{1,0:T(8,128)(2,1)S(1)}, u32[]{:S(2)}, u32[]{:S(2)}) collective-permute-start(bf16[256,128]{1,0:T(8,128)(2,1)S(1)} %get-tuple-element.29), channel_id=1, source_target_pairs={{0,4},{1,5},{2,6},{3,7},{4,8},{5,9},{6,10},{7,11},{8,12},{9,13},{1... | collective-permute-start | bytes 196616 | tf_op jit(solution)/shard_map/ppermute | solution.py:258
  112.1 7.8 %collective-permute-start.9 = (bf16[256,128]{1,0:T(8,128)(2,1)S(1)}, bf16[256,128]{1,0:T(8,128)(2,1)S(1)}, u32[]{:S(2)}, u32[]{:S(2)}) collective-permute-start(bf16[256,128]{1,0:T(8,128)(2,1)S(1)} %get-tuple-element.30), channel_id=1, source_target_pairs={{0,8},{1,9},{2,10},{3,11},{4,12},{5,13},{6,14},{7,15},{8,0},{9,1},... | collective-permute-start | bytes 196616 | tf_op jit(solution)/shard_map/ppermute | solution.py:258
  114.8 7.9 %collective-permute-start.10 = (bf16[256,128]{1,0:T(8,128)(2,1)S(1)}, bf16[256,128]{1,0:T(8,128)(2,1)S(1)}, u32[]{:S(2)}, u32[]{:S(2)}) collective-permute-start(bf16[256,128]{1,0:T(8,128)(2,1)S(1)} %get-tuple-element.31), channel_id=1, source_target_pairs={{0,12},{1,13},{2,14},{3,15},{4,0},{5,1},{6,2},{7,3},{8,4},{9,5},{1... | collective-permute-start | bytes 196616 | tf_op jit(solution)/shard_map/ppermute | solution.py:258

commit v6 on v5

--- a/solution.py
+++ b/solution.py
@@ -52,15 +52,14 @@
 
 
 def unpack(numbers, slots):
-    live, core, column, parity = (numbers[at] for at in range(4))
-    return live, core, column, parity, lambda slot: numbers[5 + slot], lambda slot: numbers[5 + slots + slot]
+    return *(numbers[at] for at in range(5)), lambda slot: numbers[5 + slot], lambda slot: numbers[5 + slots + slot]
 
 
 def forward_kernel(
     numbers, own, pair, beside, across, tiles, kept, sent, rows, acc, ring, sems
 ):
     half = kept.shape[1]
-    live, core, column, parity, emit_block, recv_block = unpack(numbers, tiles.shape[0])
+    live, core, column, parity, height, emit_block, recv_block = unpack(numbers, tiles.shape[0])
 
     def prepare():
         for held, side, odd in (
@@ -70,8 +69,9 @@
             (across, 1 - column, 1 - parity),
         ):
             at = pl.ds(pl.multiple_of(side * half, half), half)
-            for step in range(held.shape[0]):
-                rows[2 * step + odd, at, :] = held[step]
+            steps = held.shape[0]
+            for step in range(steps):
+                rows[2 * lax.rem(height + steps - step, steps) + odd, at, :] = held[step]
 
     def product(slot, tile):
         return jnp.dot(tile, rows[emit_block(slot)], preferred_element_type=f32)
@@ -121,9 +121,9 @@
 
 
 def backward_kernel(
-    numbers, held, other, tiles, own, pair, beside, across, grads, acc, ring, sems
+    numbers, held, other, tiles, own, pair, beside, across, weights, grads, acc, ring, sems
 ):
-    live, core, column, parity, emit_block, recv_block = unpack(numbers, tiles.shape[0])
+    live, core, column, parity, height, emit_block, recv_block = unpack(numbers, tiles.shape[0])
     width, lanes = acc.shape[1], held.shape[2]
     steps = own.shape[0]
 
@@ -145,6 +145,14 @@
         return jnp.dot(grads[recv_block(slot)], tile, preferred_element_type=f32)
 
     sweep(live, tiles, ring, sems, prepare, product, emit_block, acc)
+    chunk = weights.shape[1]
+    mine = pl.ds(pl.multiple_of(width + core * chunk, chunk), chunk)
+    summed = held[0, mine, :].astype(f32) + other[0, mine, :].astype(f32)
+    for block in range(1, held.shape[0]):
+        summed += held[block, mine, :].astype(f32) + other[block, mine, :].astype(f32)
+    for piece in range(weights.shape[0]):
+        weights[piece] = summed.astype(bf16)
+
     def hand_out(near):
         for out, side, odd in (
             (own, near, parity),
@@ -153,7 +161,8 @@
             (across, 1 - near, 1 - parity),
         ):
             for step in range(steps):
-                block = acc[2 * step + odd, :, side * lanes : (side + 1) * lanes]
+                at = 2 * lax.rem(height + step, steps) + odd
+                block = acc[at, :, side * lanes : (side + 1) * lanes]
                 out[step] = block.astype(bf16)
 
     @pl.when(column == 0)
@@ -165,24 +174,15 @@
         hand_out(1)
 
 
-def chunk_kernel(numbers, held, other, out):
-    chunk = out.shape[1]
-    width = held.shape[1] - 2 * chunk
-    mine = pl.ds(pl.multiple_of(width + numbers[1] * chunk, chunk), chunk)
-    weights = held[0, mine, :].astype(f32) + other[0, mine, :].astype(f32)
-    for block in range(1, held.shape[0]):
-        weights += held[block, mine, :].astype(f32) + other[block, mine, :].astype(f32)
-    for piece in range(out.shape[0]):
-        out[piece] = weights.astype(bf16)
-
-
-def quad_kernel(numbers, own, pair, beside, across, *outs):
-    steps = own.shape[0]
+def quad_kernel(own, pair, beside, across, *outs):
     for step, out in enumerate(outs):
-        block = lax.rem(numbers[4] + step, steps)
-        near = own[block].astype(f32) + pair[block].astype(f32)
-        far = beside[block].astype(f32) + across[block].astype(f32)
+        near = own[step].astype(f32) + pair[step].astype(f32)
+        far = beside[step].astype(f32) + across[step].astype(f32)
         out[...] = (near + far).astype(bf16)
+
+
+def copy_kernel(source, out):
+    out[...] = source[...]
 
 
 def weights_kernel(terms, total):
@@ -259,14 +259,16 @@
             array, "recv", [(member, (member + 4 * step) % recv_size) for member in range(recv_size)]
         )
 
-    column_rows = lax.all_to_all(
-        jnp.broadcast_to(own_rows[None], (steps, facet_rows, width)),
-        "recv",
-        0,
-        0,
-        tiled=True,
-        axis_index_groups=[list(range(first, recv_size, 4)) for first in range(4)],
-    )
+    arrivals = {step: along_z(own_rows, step) for step in sorted(range(1, steps), key=lambda step: abs(2 * step - steps))}
+    held_rows = pl.pallas_call(
+        copy_kernel,
+        out_shape=struct(own_rows.shape, bf16),
+        in_specs=in_vmem(1),
+        out_specs=in_vmem(1)[0],
+        compiler_params=limits(8),
+        name="own_rows",
+    )(own_rows)
+    column_rows = jnp.stack([held_rows] + [arrivals[step] for step in range(1, steps)])
     kept, sent = pl.pallas_call(
         forward_kernel,
         out_shape=(
@@ -307,21 +309,12 @@
     held = lax.all_to_all(payload, "emit", 0, 0, tiled=True, axis_index_groups=same_core)
     other = lax.ppermute(held, "emit", swap)
 
-    chunks = pl.pallas_call(
-        chunk_kernel,
-        out_shape=struct((recv_size, chunk // 2, lanes), bf16),
-        in_specs=in_smem(1) + in_vmem(2),
-        out_specs=in_vmem(1)[0],
-        compiler_params=limits(8),
-        name="weights_chunk",
-    )(numbers, held, other)
-    chunks = lax.all_to_all(chunks, "recv", 0, 0, tiled=True)
-
-    own, pair, beside, across = pl.pallas_call(
+    own, pair, beside, across, weights = pl.pallas_call(
         backward_kernel,
-        out_shape=(struct((steps, width, lanes), bf16),) * 4,
+        out_shape=(struct((steps, width, lanes), bf16),) * 4
+        + (struct((recv_size, chunk // 2, lanes), bf16),),
         in_specs=in_smem(1) + in_vmem(2) + [in_hbm],
-        out_specs=tuple(in_vmem(4)),
+        out_specs=tuple(in_vmem(5)),
         scratch_shapes=[
             pltpu.VMEM((recv_blocks, width, tile_dim), bf16),
             pltpu.VMEM((emit_blocks + 1, width, tile_dim), f32),
@@ -331,15 +324,18 @@
         cost_estimate=sweep_cost,
         name="backward_sweep",
     )(numbers, held, other, values)
+    pair, weights = lax.optimization_barrier((to_quad(pair, 2), weights))
+    chunks = lax.all_to_all(weights, "recv", 0, 0, tiled=True)
     terms = pl.pallas_call(
         quad_kernel,
         out_shape=(struct((width, lanes), bf16),) * steps,
-        in_specs=in_smem(1) + in_vmem(4),
+        in_specs=in_vmem(4),
         out_specs=tuple(in_vmem(steps)),
         compiler_params=limits(8),
         name="quad_sum",
-    )(numbers, own, to_quad(pair, 2), to_quad(beside, 1), to_quad(across, 3))
-    chunks, terms = lax.optimization_barrier((chunks, terms))
+    )(own, pair, to_quad(beside, 1), to_quad(across, 3))
+    terms = [terms[0]] + [along_z(terms[step], step) for step in range(1, steps)]
+    chunks, terms[1] = lax.optimization_barrier((chunks, terms[1]))
 
     total = pl.pallas_call(
         weights_kernel,
@@ -350,7 +346,6 @@
         name="weights_sum",
     )(chunks)
     gathered = lax.all_to_all(total, "emit", 0, 0, tiled=True).reshape(4, width, lanes)
-    terms = [terms[0]] + [along_z(terms[step], step) for step in range(1, steps)]
     grad_features = pl.pallas_call(
         features_kernel,
         out_shape=struct((facet_rows, width), bf16),

time: 125 us -> 136 us (1.088)
  starting transfers between devices: 27.7 us -> 44.3 us
  waiting for transfers between devices: 30.4 us -> 45.5 us
  blocking collectives: 49.1 us -> 34.1 us
  Pallas kernels: 13.1 us -> 8.16 us
    all_to_all x1 -> x0, blocking collectives: 17.9 us -> none  [per_device(): lax.all_to_all(jnp.broadcast_to(own_rows[None], (steps, facet_rows, width...]
    ppermute x3 -> x6, starting transfers between devices: 7.74 us -> 17.8 us  [along_z(): lax.ppermute(array, 'recv', [(member, (member + 4 * step) % recv_size) fo...]
    ppermute x3 -> x6, waiting for transfers between devices: 5.03 us -> 14.8 us  [along_z(): lax.ppermute(array, 'recv', [(member, (member + 4 * step) % recv_size) fo...]
    ppermute x6, waiting for transfers between devices: 21.9 us -> 27.2 us  [to_quad(): lax.ppermute(array, 'recv', [(member, member ^ bits) for member in range(...]
    all_to_all x1, starting transfers between devices: 5.14 us -> 8.85 us  [per_device(): lax.all_to_all(total, 'emit', 0, 0, tiled=True).reshape(4, width, lanes)]
    all_to_all x1, blocking collectives: 15.3 us -> 18.7 us  [per_device(): lax.all_to_all(pair_sum, 'emit', 0, 0, tiled=True, axis_index_groups=same...]
    pallas_call x1, Pallas kernels: 4.4 us -> 2.46 us  [per_device(): pl.pallas_call(forward_kernel, out_shape=(struct((recv_blocks, tile_dim /...]
    all_to_all x1, starting transfers between devices: 4.79 us -> 6.68 us  [per_device(): chunks = lax.all_to_all(weights, 'recv', 0, 0, tiled=True)]
  transfers between devices with their start and end apart: 13 -> 16, of which waited for: 8 -> 12; matrix products, arithmetic and copies ran while one was open for 1% -> 1% of each run, Pallas kernels for 5% -> 1%
where the time goes in v6:
time: 136 us
  waiting for transfers between devices  45.5 us (33%)
  starting transfers between devices  44.3 us (33%)
  blocking collectives  34.1 us (25%)
  Pallas kernels  8.16 us (6%)
  local copies, waits for them, and re-layouts  1.68 us (1%)
  between operations  1.38 us (1%)
    ppermute x6, waiting for transfers between devices, to_quad(): lax.ppermute(array, 'recv', [(member, member ^ bits) for member in range(...  27.2 us
    all_to_all x1, blocking collectives, per_device(): lax.all_to_all(pair_sum, 'emit', 0, 0, tiled=True, axis_index_groups=same...  18.7 us
    ppermute x6, starting transfers between devices, along_z(): lax.ppermute(array, 'recv', [(member, (member + 4 * step) % recv_size) fo...  17.8 us
    all_to_all x1, blocking collectives, per_device(): lax.all_to_all(payload, 'emit', 0, 0, tiled=True, axis_index_groups=same_...  15.3 us
    ppermute x6, waiting for transfers between devices, along_z(): lax.ppermute(array, 'recv', [(member, (member + 4 * step) % recv_size) fo...  14.8 us
    all_to_all x1, starting transfers between devices, per_device(): lax.all_to_all(total, 'emit', 0, 0, tiled=True).reshape(4, width, lanes)  8.85 us
    ppermute x6, starting transfers between devices, to_quad(): lax.ppermute(array, 'recv', [(member, member ^ bits) for member in range(...  6.8 us
    all_to_all x1, starting transfers between devices, per_device(): chunks = lax.all_to_all(weights, 'recv', 0, 0, tiled=True)  6.68 us
  transfers between devices with their start and end apart: 16, of which 12 were waited for; matrix products, arithmetic and copies ran while one was open for 1% of the time, Pallas kernels for 1%

profile of v6, /device:TPU:1, one launch (start us, length us, event | category | flops | bytes accessed | tf_op | source)
XLA Modules:
  0.0 136.0 jit_solution(16474022695191400716)
XLA Ops:
  0.6 0.0 copy-start
  0.6 0.0 copy-start.1
  0.7 0.0 copy-start.2
  0.7 6.9 %collective-permute-start.2 = (bf16[128,256]{1,0:T(8,128)(2,1)}, bf16[128,256]{1,0:T(8,128)(2,1)S(1)}, u32[]{:S(2)}, u32[]{:S(2)}) collective-permute-start(bf16[128,256]{1,0:T(8,128)(2,1)} %bitcast.22), channel_id=1, source_target_pairs={{0,12},{1,13},{2,14},{3,15},{4,0},{5,1},{6,2},{7,3},{8,4},{9,5},{1... | collective-permute-start | bytes 196616 | tf_op jit(solution)/shard_map/ppermute | solution.py:258
  7.6 1.0 collective-permute-start.1
  8.6 2.3 %collective-permute-start = (bf16[128,256]{1,0:T(8,128)(2,1)}, bf16[128,256]{1,0:T(8,128)(2,1)S(1)}, u32[]{:S(2)}, u32[]{:S(2)}) collective-permute-start(bf16[128,256]{1,0:T(8,128)(2,1)} %bitcast.24), channel_id=1, source_target_pairs={{0,4},{1,5},{2,6},{3,7},{4,8},{5,9},{6,10},{7,11},{8,12},{9,13},{1... | collective-permute-start | bytes 196616 | tf_op jit(solution)/shard_map/ppermute | solution.py:258
  10.8 0.0 copy-start.3
  10.8 0.9 copy-done.3
  11.7 0.0 collective-permute-done.2
  11.7 3.3 %collective-permute-done.1 = bf16[128,256]{1,0:T(8,128)(2,1)S(1)} collective-permute-done((bf16[128,256]{1,0:T(8,128)(2,1)}, bf16[128,256]{1,0:T(8,128)(2,1)S(1)}, u32[]{:S(2)}, u32[]{:S(2)}) %collective-permute-start.1) | collective-permute-done | bytes 65568 | tf_op jit(solution)/shard_map/ppermute | solution.py:258
  15.0 0.6 collective-permute-done
  15.7 2.1 %collective-permute-start.5 = (bf16[4,128,256]{2,1,0:T(8,128)(2,1)S(1)}, bf16[4,128,256]{2,1,0:T(8,128)(2,1)S(1)}, u32[]{:S(2)}, u32[]{:S(2)}) collective-permute-start(bf16[4,128,256]{2,1,0:T(8,128)(2,1)S(1)} %pad_maximum_fusion.own), channel_id=1, source_target_pairs={{0,3},{1,2},{2,1},{3,0},{4,7},{5,6},{6,5},{7,4},{8,11},{9,10},{10,... | collective-permute-start | bytes 786440 | tf_op jit(solution)/shard_map/ppermute | solution.py:255
  17.8 0.2 collective-permute-start.4
  18.0 0.4 collective-permute-start.3
  19.1 0.8 concatenate.9.numbers
  19.9 2.2 %collective-permute-done.5.across = bf16[4,128,256]{2,1,0:T(8,128)(2,1)S(1)} collective-permute-done((bf16[4,128,256]{2,1,0:T(8,128)(2,1)S(1)}, bf16[4,128,256]{2,1,0:T(8,128)(2,1)S(1)}, u32[]{:S(2)}, u32[]{:S(2)}) %collective-permute-start.5) | collective-permute-done | bytes 262176 | tf_op jit(solution)/shard_map/ppermute | solution.py:255
  22.0 7.7 %collective-permute-done.4.beside = bf16[4,128,256]{2,1,0:T(8,128)(2,1)S(1)} collective-permute-done((bf16[4,128,256]{2,1,0:T(8,128)(2,1)S(1)}, bf16[4,128,256]{2,1,0:T(8,128)(2,1)S(1)}, u32[]{:S(2)}, u32[]{:S(2)}) %collective-permute-start.4) | collective-permute-done | bytes 262176 | tf_op jit(solution)/shard_map/ppermute | solution.py:255
  29.8 0.0 collective-permute-done.3.pair
  29.8 2.5 %forward_sweep.1 = (f32[8,128,256]{2,1,0:T(8,128)S(1)}, bf16[8,128,256]{2,1,0:T(8,128)(2,1)S(1)}) custom-call(s32[133]{0:T(256)S(1)} %concatenate.9.numbers, bf16[4,128,256]{2,1,0:T(8,128)(2,1)S(1)} %pad_maximum_fusion.own, bf16[4,128,256]{2,1,0:T(8,128)(2,1)S(1)} %collective-permute-done.3.pair, bf16[4,128,256]{2,1,0:T(8,128)(2,1)S(1)} %collective-permute-done.4.beside, ...), custom_call_target="tpu_custom_call" | custom-call | flops 2147483648 | bytes 8388608 | tf_op jit(solution)/shard_map/forward_sweep/pallas_call | solution.py:272
  32.2 1.5 %collective-permute-start.6 = (bf16[8,128,256]{2,1,0:T(8,128)(2,1)S(1)}, bf16[8,128,256]{2,1,0:T(8,128)(2,1)S(1)}, u32[]{:S(2)}, u32[]{:S(2)}) collective-permute-start(bf16[8,128,256]{2,1,0:T(8,128)(2,1)S(1)} %get-tuple-element.19), channel_id=1, source_target_pairs={{0,16},{16,0},{32,48},{48,32},{64,80},{80,64},{96,112},{112,96},{1... | collective-permute-start | bytes 1572872 | tf_op jit(solution)/shard_map/ppermute | solution.py:296
  33.7 1.5 %collective-permute-done.6 = bf16[8,128,256]{2,1,0:T(8,128)(2,1)S(1)} collective-permute-done((bf16[8,128,256]{2,1,0:T(8,128)(2,1)S(1)}, bf16[8,128,256]{2,1,0:T(8,128)(2,1)S(1)}, u32[]{:S(2)}, u32[]{:S(2)}) %collective-permute-start.6) | collective-permute-done | bytes 524320 | tf_op jit(solution)/shard_map/ppermute | solution.py:296
  35.3 0.2 add_convert_fusion
  35.4 18.7 %all_to_all.20.terms = bf16[8,128,256]{2,1,0:T(8,128)(2,1)S(1)} all-to-all(bf16[8,128,256]{2,1,0:T(8,128)(2,1)S(1)} %add_convert_fusion), channel_id=1, replica_groups={{0,32,64,96,128,160,192,224},{16,48,80,112,144,176,208,240},{1,33,65,97..., dimensions={0} | all-to-all | bytes 1048576 | tf_op jit(solution)/shard_map/all_to_all | solution.py:298
  54.2 0.0 copy-done
  54.2 0.0 copy-done.1
  54.2 0.0 copy-done.2
  54.2 0.6 middle.1
  54.8 15.3 %all_to_all.21.held = bf16[8,384,128]{2,1,0:T(8,128)(2,1)S(1)} all-to-all(bf16[8,384,128]{2,1,0:T(8,128)(2,1)S(1)} %middle.1), channel_id=1, replica_groups={{0,32,64,96,128,160,192,224},{16,48,80,112,144,176,208,240},{1,33,65,97..., dimensions={0} | all-to-all | bytes 1572864 | tf_op jit(solution)/shard_map/all_to_all | solution.py:309
  70.1 2.6 %collective-permute-start.7 = (bf16[8,384,128]{2,1,0:T(8,128)(2,1)S(1)}, bf16[8,384,128]{2,1,0:T(8,128)(2,1)S(1)}, u32[]{:S(2)}, u32[]{:S(2)}) collective-permute-start(bf16[8,384,128]{2,1,0:T(8,128)(2,1)S(1)} %all_to_all.21.held), channel_id=1, source_target_pairs={{0,16},{16,0},{32,48},{48,32},{64,80},{80,64},{96,112},{112,96},{1... | collective-permute-start | bytes 2359304 | tf_op jit(solution)/shard_map/ppermute | solution.py:310
  72.8 1.9 %collective-permute-done.7.other = bf16[8,384,128]{2,1,0:T(8,128)(2,1)S(1)} collective-permute-done((bf16[8,384,128]{2,1,0:T(8,128)(2,1)S(1)}, bf16[8,384,128]{2,1,0:T(8,128)(2,1)S(1)}, u32[]{:S(2)}, u32[]{:S(2)}) %collective-permute-start.7) | collective-permute-done | bytes 786464 | tf_op jit(solution)/shard_map/ppermute | solution.py:310
  74.7 3.2 %backward_sweep.1 = (bf16[4,256,128]{2,1,0:T(8,128)(2,1)S(1)}, bf16[4,256,128]{2,1,0:T(8,128)(2,1)S(1)}, bf16[4,256,128]{2,1,0:T(8,128)(2,1)S(1)}, bf16[4,256,128]{2,1,0:T(8,128)(2,1)S(1)}, bf16[16,64,128]{2,1,0:T(8,128)(2,1)}) custom-call(s32[133]{0:T(256)S(1)} %concatenate.9.numbers, bf16[8,384,128]{2,1,0:T(8,128)(2,1)S(1)} %all_to_all.21.held, ...), custom_call_target="tpu_custom_call" | custom-call | flops 2147483648 | bytes 8388608 | tf_op jit(solution)/shard_map/backward_sweep/pallas_call | solution.py:312
  77.9 1.5 %collective-permute-start.8 = (bf16[4,256,128]{2,1,0:T(8,128)(2,1)S(1)}, bf16[4,256,128]{2,1,0:T(8,128)(2,1)S(1)}, u32[]{:S(2)}, u32[]{:S(2)}) collective-permute-start(bf16[4,256,128]{2,1,0:T(8,128)(2,1)S(1)} %get-tuple-element.21), channel_id=1, source_target_pairs={{0,2},{1,3},{2,0},{3,1},{4,6},{5,7},{6,4},{7,5},{8,10},{9,11},{10,... | collective-permute-start | bytes 786440 | tf_op jit(solution)/shard_map/ppermute | solution.py:255
  79.4 5.9 %collective-permute-done.8.pair = bf16[4,256,128]{2,1,0:T(8,128)(2,1)S(1)} collective-permute-done((bf16[4,256,128]{2,1,0:T(8,128)(2,1)S(1)}, bf16[4,256,128]{2,1,0:T(8,128)(2,1)S(1)}, u32[]{:S(2)}, u32[]{:S(2)}) %collective-permute-start.8) | collective-permute-done | bytes 262176 | tf_op jit(solution)/shard_map/ppermute | solution.py:255
  85.3 6.7 %all-to-all-start.2 = ((bf16[16,64,128]{2,1,0:T(8,128)(2,1)}), bf16[16,64,128]{2,1,0:T(8,128)(2,1)S(1)}, u32[]{:S(2)}, u32[]{:S(2)}) async-start(bf16[16,64,128]{2,1,0:T(8,128)(2,1)} %get-tuple-element.27), calls=%async_computation.2 | async-start | bytes 524288 | tf_op jit(solution)/shard_map/all_to_all | solution.py:328
  92.0 1.4 %collective-permute-start.9 = (bf16[4,256,128]{2,1,0:T(8,128)(2,1)S(1)}, bf16[4,256,128]{2,1,0:T(8,128)(2,1)S(1)}, u32[]{:S(2)}, u32[]{:S(2)}) collective-permute-start(bf16[4,256,128]{2,1,0:T(8,128)(2,1)S(1)} %get-tuple-element.24), channel_id=1, source_target_pairs={{0,1},{1,0},{2,3},{3,2},{4,5},{5,4},{6,7},{7,6},{8,9},{9,8},{10,11... | collective-permute-start | bytes 786440 | tf_op jit(solution)/shard_map/ppermute | solution.py:255
  93.4 1.2 collective-permute-start.10
  94.6 5.8 %collective-permute-done.9.beside = bf16[4,256,128]{2,1,0:T(8,128)(2,1)S(1)} collective-permute-done((bf16[4,256,128]{2,1,0:T(8,128)(2,1)S(1)}, bf16[4,256,128]{2,1,0:T(8,128)(2,1)S(1)}, u32[]{:S(2)}, u32[]{:S(2)}) %collective-permute-start.9) | collective-permute-done | bytes 262176 | tf_op jit(solution)/shard_map/ppermute | solution.py:255
  100.3 5.6 %collective-permute-done.10.across = bf16[4,256,128]{2,1,0:T(8,128)(2,1)S(1)} collective-permute-done((bf16[4,256,128]{2,1,0:T(8,128)(2,1)S(1)}, bf16[4,256,128]{2,1,0:T(8,128)(2,1)S(1)}, u32[]{:S(2)}, u32[]{:S(2)}) %collective-permute-start.10) | collective-permute-done | bytes 262176 | tf_op jit(solution)/shard_map/ppermute | solution.py:255
  105.9 0.1 quad_sum.1
  106.0 2.5 %collective-permute-start.11 = (bf16[256,128]{1,0:T(8,128)(2,1)S(1)}, bf16[256,128]{1,0:T(8,128)(2,1)S(1)}, u32[]{:S(2)}, u32[]{:S(2)}) collective-permute-start(bf16[256,128]{1,0:T(8,128)(2,1)S(1)} %get-tuple-element.28), channel_id=1, source_target_pairs={{0,4},{1,5},{2,6},{3,7},{4,8},{5,9},{6,10},{7,11},{8,12},{9,13},{1... | collective-permute-start | bytes 196616 | tf_op jit(solution)/shard_map/ppermute | solution.py:258
  108.6 3.6 %collective-permute-done.11.refs_1_ = bf16[256,128]{1,0:T(8,128)(2,1)S(1)} collective-permute-done((bf16[256,128]{1,0:T(8,128)(2,1)S(1)}, bf16[256,128]{1,0:T(8,128)(2,1)S(1)}, u32[]{:S(2)}, u32[]{:S(2)}) %collective-permute-start.11) | collective-permute-done | bytes 65568 | tf_op jit(solution)/shard_map/ppermute | solution.py:258
  112.2 0.0 all-to-all-done.2.terms
  112.2 0.9 weights_sum.1
  113.1 8.8 %all-to-all-start.3 = ((f32[16,64,128]{2,1,0:T(8,128)}), f32[16,64,128]{2,1,0:T(8,128)S(1)}, u32[]{:S(2)}, u32[]{:S(2)}) async-start(f32[16,64,128]{2,1,0:T(8,128)} %weights_sum.1), calls=%async_computation.3 | async-start | bytes 1048576 | tf_op jit(solution)/shard_map/all_to_all | solution.py:348
  121.9 5.1 %collective-permute-start.12 = (bf16[256,128]{1,0:T(8,128)(2,1)S(1)}, bf16[256,128]{1,0:T(8,128)(2,1)S(1)}, u32[]{:S(2)}, u32[]{:S(2)}) collective-permute-start(bf16[256,128]{1,0:T(8,128)(2,1)S(1)} %get-tuple-element.30), channel_id=1, source_target_pairs={{0,8},{1,9},{2,10},{3,11},{4,12},{5,13},{6,14},{7,15},{8,0},{9,1},... | collective-permute-start | bytes 196616 | tf_op jit(solution)/shard_map/ppermute | solution.py:258
  127.0 0.0 collective-permute-start.13
  127.0 2.3 %collective-permute-done.12.refs_2_ = bf16[256,128]{1,0:T(8,128)(2,1)S(1)} collective-permute-done((bf16[256,128]{1,0:T(8,128)(2,1)S(1)}, bf16[256,128]{1,0:T(8,128)(2,1)S(1)}, u32[]{:S(2)}, u32[]{:S(2)}) %collective-permute-start.12) | collective-permute-done | bytes 65568 | tf_op jit(solution)/shard_map/ppermute | solution.py:258
  129.4 5.0 %collective-permute-done.13.refs_3_ = bf16[256,128]{1,0:T(8,128)(2,1)S(1)} collective-permute-done((bf16[256,128]{1,0:T(8,128)(2,1)S(1)}, bf16[256,128]{1,0:T(8,128)(2,1)S(1)}, u32[]{:S(2)}, u32[]{:S(2)}) %collective-permute-start.13) | collective-permute-done | bytes 65568 | tf_op jit(solution)/shard_map/ppermute | solution.py:258
  134.3 0.8 features_grad.1
  135.2 0.0 all-to-all-done.3
  135.2 0.8 pad_maximum_fusion.1
  (3 shorter events, 0.1 us)
Async XLA Ops:
  0.6 53.6 %copy-start = (bf16[256,256]{1,0:T(8,128)(2,1)S(1)}, bf16[256,256]{1,0:T(8,128)(2,1)}, u32[]{:S(2)}) copy-start(bf16[256,256]{1,0:T(8,128)(2,1)} %refs_4_.1) | copy-start | bytes 393220
  0.6 53.5 %copy-start.1 = (bf16[256,256]{1,0:T(8,128)(2,1)S(1)}, bf16[256,256]{1,0:T(8,128)(2,1)}, u32[]{:S(2)}) copy-start(bf16[256,256]{1,0:T(8,128)(2,1)} %w_out.1) | copy-start | bytes 393220
  0.7 53.5 %copy-start.2 = (bf16[1,128,256]{2,1,0:T(8,128)(2,1)S(1)}, bf16[1,128,256]{2,1,0:T(8,128)(2,1)}, u32[]{:S(2)}) copy-start(bf16[1,128,256]{2,1,0:T(8,128)(2,1)} %param.9) | copy-start | bytes 196612
  0.7 11.1 %collective-permute-start.2 = (bf16[128,256]{1,0:T(8,128)(2,1)}, bf16[128,256]{1,0:T(8,128)(2,1)S(1)}, u32[]{:S(2)}, u32[]{:S(2)}) collective-permute-start(bf16[128,256]{1,0:T(8,128)(2,1)} %bitcast.22), channel_id=1, source_target_pairs={{0,12},{1,13},{2,14},{3,15},{4,0},{5,1},{6,2},{7,3},{8,4},{9,5},{1... | collective-permute-start | bytes 196616 | tf_op jit(solution)/shard_map/ppermute | solution.py:258
  7.6 7.4 %collective-permute-start.1 = (bf16[128,256]{1,0:T(8,128)(2,1)}, bf16[128,256]{1,0:T(8,128)(2,1)S(1)}, u32[]{:S(2)}, u32[]{:S(2)}) collective-permute-start(bf16[128,256]{1,0:T(8,128)(2,1)} %bitcast.23), channel_id=1, source_target_pairs={{0,8},{1,9},{2,10},{3,11},{4,12},{5,13},{6,14},{7,15},{8,0},{9,1},... | collective-permute-start | bytes 196616 | tf_op jit(solution)/shard_map/ppermute | solution.py:258
  8.6 7.1 %collective-permute-start = (bf16[128,256]{1,0:T(8,128)(2,1)}, bf16[128,256]{1,0:T(8,128)(2,1)S(1)}, u32[]{:S(2)}, u32[]{:S(2)}) collective-permute-start(bf16[128,256]{1,0:T(8,128)(2,1)} %bitcast.24), channel_id=1, source_target_pairs={{0,4},{1,5},{2,6},{3,7},{4,8},{5,9},{6,10},{7,11},{8,12},{9,13},{1... | collective-permute-start | bytes 196616 | tf_op jit(solution)/shard_map/ppermute | solution.py:258
  10.8 0.9 copy-start.3
  15.7 6.3 %collective-permute-start.5 = (bf16[4,128,256]{2,1,0:T(8,128)(2,1)S(1)}, bf16[4,128,256]{2,1,0:T(8,128)(2,1)S(1)}, u32[]{:S(2)}, u32[]{:S(2)}) collective-permute-start(bf16[4,128,256]{2,1,0:T(8,128)(2,1)S(1)} %pad_maximum_fusion.own), channel_id=1, source_target_pairs={{0,3},{1,2},{2,1},{3,0},{4,7},{5,6},{6,5},{7,4},{8,11},{9,10},{10,... | collective-permute-start | bytes 786440 | tf_op jit(solution)/shard_map/ppermute | solution.py:255
  17.8 11.9 %collective-permute-start.4 = (bf16[4,128,256]{2,1,0:T(8,128)(2,1)S(1)}, bf16[4,128,256]{2,1,0:T(8,128)(2,1)S(1)}, u32[]{:S(2)}, u32[]{:S(2)}) collective-permute-start(bf16[4,128,256]{2,1,0:T(8,128)(2,1)S(1)} %pad_maximum_fusion.own), channel_id=1, source_target_pairs={{0,1},{1,0},{2,3},{3,2},{4,5},{5,4},{6,7},{7,6},{8,9},{9,8},{10,11... | collective-permute-start | bytes 786440 | tf_op jit(solution)/shard_map/ppermute | solution.py:255
  18.0 11.7 %collective-permute-start.3 = (bf16[4,128,256]{2,1,0:T(8,128)(2,1)S(1)}, bf16[4,128,256]{2,1,0:T(8,128)(2,1)S(1)}, u32[]{:S(2)}, u32[]{:S(2)}) collective-permute-start(bf16[4,128,256]{2,1,0:T(8,128)(2,1)S(1)} %pad_maximum_fusion.own), channel_id=1, source_target_pairs={{0,2},{1,3},{2,0},{3,1},{4,6},{5,7},{6,4},{7,5},{8,10},{9,11},{10,... | collective-permute-start | bytes 786440 | tf_op jit(solution)/shard_map/ppermute | solution.py:255
  32.2 3.1 %collective-permute-start.6 = (bf16[8,128,256]{2,1,0:T(8,128)(2,1)S(1)}, bf16[8,128,256]{2,1,0:T(8,128)(2,1)S(1)}, u32[]{:S(2)}, u32[]{:S(2)}) collective-permute-start(bf16[8,128,256]{2,1,0:T(8,128)(2,1)S(1)} %get-tuple-element.19), channel_id=1, source_target_pairs={{0,16},{16,0},{32,48},{48,32},{64,80},{80,64},{96,112},{112,96},{1... | collective-permute-start | bytes 1572872 | tf_op jit(solution)/shard_map/ppermute | solution.py:296
  70.1 4.5 %collective-permute-start.7 = (bf16[8,384,128]{2,1,0:T(8,128)(2,1)S(1)}, bf16[8,384,128]{2,1,0:T(8,128)(2,1)S(1)}, u32[]{:S(2)}, u32[]{:S(2)}) collective-permute-start(bf16[8,384,128]{2,1,0:T(8,128)(2,1)S(1)} %all_to_all.21.held), channel_id=1, source_target_pairs={{0,16},{16,0},{32,48},{48,32},{64,80},{80,64},{96,112},{112,96},{1... | collective-permute-start | bytes 2359304 | tf_op jit(solution)/shard_map/ppermute | solution.py:310
  77.9 7.4 %collective-permute-start.8 = (bf16[4,256,128]{2,1,0:T(8,128)(2,1)S(1)}, bf16[4,256,128]{2,1,0:T(8,128)(2,1)S(1)}, u32[]{:S(2)}, u32[]{:S(2)}) collective-permute-start(bf16[4,256,128]{2,1,0:T(8,128)(2,1)S(1)} %get-tuple-element.21), channel_id=1, source_target_pairs={{0,2},{1,3},{2,0},{3,1},{4,6},{5,7},{6,4},{7,5},{8,10},{9,11},{10,... | collective-permute-start | bytes 786440 | tf_op jit(solution)/shard_map/ppermute | solution.py:255
  85.3 26.9 %all-to-all-start.2 = ((bf16[16,64,128]{2,1,0:T(8,128)(2,1)}), bf16[16,64,128]{2,1,0:T(8,128)(2,1)S(1)}, u32[]{:S(2)}, u32[]{:S(2)}) async-start(bf16[16,64,128]{2,1,0:T(8,128)(2,1)} %get-tuple-element.27), calls=%async_computation.2 | async-start | bytes 524288 | tf_op jit(solution)/shard_map/all_to_all | solution.py:328
  92.0 8.3 %collective-permute-start.9 = (bf16[4,256,128]{2,1,0:T(8,128)(2,1)S(1)}, bf16[4,256,128]{2,1,0:T(8,128)(2,1)S(1)}, u32[]{:S(2)}, u32[]{:S(2)}) collective-permute-start(bf16[4,256,128]{2,1,0:T(8,128)(2,1)S(1)} %get-tuple-element.24), channel_id=1, source_target_pairs={{0,1},{1,0},{2,3},{3,2},{4,5},{5,4},{6,7},{7,6},{8,9},{9,8},{10,11... | collective-permute-start | bytes 786440 | tf_op jit(solution)/shard_map/ppermute | solution.py:255
  93.4 12.5 %collective-permute-start.10 = (bf16[4,256,128]{2,1,0:T(8,128)(2,1)S(1)}, bf16[4,256,128]{2,1,0:T(8,128)(2,1)S(1)}, u32[]{:S(2)}, u32[]{:S(2)}) collective-permute-start(bf16[4,256,128]{2,1,0:T(8,128)(2,1)S(1)} %get-tuple-element.25), channel_id=1, source_target_pairs={{0,3},{1,2},{2,1},{3,0},{4,7},{5,6},{6,5},{7,4},{8,11},{9,10},{10,... | collective-permute-start | bytes 786440 | tf_op jit(solution)/shard_map/ppermute | solution.py:255
  106.0 6.2 %collective-permute-start.11 = (bf16[256,128]{1,0:T(8,128)(2,1)S(1)}, bf16[256,128]{1,0:T(8,128)(2,1)S(1)}, u32[]{:S(2)}, u32[]{:S(2)}) collective-permute-start(bf16[256,128]{1,0:T(8,128)(2,1)S(1)} %get-tuple-element.28), channel_id=1, source_target_pairs={{0,4},{1,5},{2,6},{3,7},{4,8},{5,9},{6,10},{7,11},{8,12},{9,13},{1... | collective-permute-start | bytes 196616 | tf_op jit(solution)/shard_map/ppermute | solution.py:258
  113.1 22.1 %all-to-all-start.3 = ((f32[16,64,128]{2,1,0:T(8,128)}), f32[16,64,128]{2,1,0:T(8,128)S(1)}, u32[]{:S(2)}, u32[]{:S(2)}) async-start(f32[16,64,128]{2,1,0:T(8,128)} %weights_sum.1), calls=%async_computation.3 | async-start | bytes 1048576 | tf_op jit(solution)/shard_map/all_to_all | solution.py:348
  121.9 7.4 %collective-permute-start.12 = (bf16[256,128]{1,0:T(8,128)(2,1)S(1)}, bf16[256,128]{1,0:T(8,128)(2,1)S(1)}, u32[]{:S(2)}, u32[]{:S(2)}) collective-permute-start(bf16[256,128]{1,0:T(8,128)(2,1)S(1)} %get-tuple-element.30), channel_id=1, source_target_pairs={{0,8},{1,9},{2,10},{3,11},{4,12},{5,13},{6,14},{7,15},{8,0},{9,1},... | collective-permute-start | bytes 196616 | tf_op jit(solution)/shard_map/ppermute | solution.py:258
  127.0 7.3 %collective-permute-start.13 = (bf16[256,128]{1,0:T(8,128)(2,1)S(1)}, bf16[256,128]{1,0:T(8,128)(2,1)S(1)}, u32[]{:S(2)}, u32[]{:S(2)}) collective-permute-start(bf16[256,128]{1,0:T(8,128)(2,1)S(1)} %get-tuple-element.31), channel_id=1, source_target_pairs={{0,12},{1,13},{2,14},{3,15},{4,0},{5,1},{6,2},{7,3},{8,4},{9,5},{1... | collective-permute-start | bytes 196616 | tf_op jit(solution)/shard_map/ppermute | solution.py:258

commit v7 on v6

--- a/solution.py
+++ b/solution.py
@@ -181,10 +181,6 @@
         out[...] = (near + far).astype(bf16)
 
 
-def copy_kernel(source, out):
-    out[...] = source[...]
-
-
 def weights_kernel(terms, total):
     summed = terms[0].astype(f32)
     for piece in range(1, terms.shape[0]):
@@ -260,15 +256,7 @@
         )
 
     arrivals = {step: along_z(own_rows, step) for step in sorted(range(1, steps), key=lambda step: abs(2 * step - steps))}
-    held_rows = pl.pallas_call(
-        copy_kernel,
-        out_shape=struct(own_rows.shape, bf16),
-        in_specs=in_vmem(1),
-        out_specs=in_vmem(1)[0],
-        compiler_params=limits(8),
-        name="own_rows",
-    )(own_rows)
-    column_rows = jnp.stack([held_rows] + [arrivals[step] for step in range(1, steps)])
+    column_rows = jnp.stack([own_rows] + [arrivals[step] for step in range(1, steps)])
     kept, sent = pl.pallas_call(
         forward_kernel,
         out_shape=(
@@ -324,7 +312,6 @@
         cost_estimate=sweep_cost,
         name="backward_sweep",
     )(numbers, held, other, values)
-    pair, weights = lax.optimization_barrier((to_quad(pair, 2), weights))
     chunks = lax.all_to_all(weights, "recv", 0, 0, tiled=True)
     terms = pl.pallas_call(
         quad_kernel,
@@ -333,9 +320,8 @@
         out_specs=tuple(in_vmem(steps)),
         compiler_params=limits(8),
         name="quad_sum",
-    )(own, pair, to_quad(beside, 1), to_quad(across, 3))
-    terms = [terms[0]] + [along_z(terms[step], step) for step in range(1, steps)]
-    chunks, terms[1] = lax.optimization_barrier((chunks, terms[1]))
+    )(own, to_quad(pair, 2), to_quad(beside, 1), to_quad(across, 3))
+    chunks, terms = lax.optimization_barrier((chunks, terms))
 
     total = pl.pallas_call(
         weights_kernel,
@@ -346,6 +332,7 @@
         name="weights_sum",
     )(chunks)
     gathered = lax.all_to_all(total, "emit", 0, 0, tiled=True).reshape(4, width, lanes)
+    terms = [terms[0]] + [along_z(terms[step], step) for step in range(1, steps)]
     grad_features = pl.pallas_call(
         features_kernel,
         out_shape=struct((facet_rows, width), bf16),

time: 136 us -> 129 us (0.949)
  waiting for transfers between devices: 45.5 us -> 39.6 us
  starting transfers between devices: 44.3 us -> 42.6 us
    ppermute x6, waiting for transfers between devices: 14.8 us -> 9.6 us  [along_z(): lax.ppermute(array, 'recv', [(member, (member + 4 * step) % recv_size) fo...]
  transfers between devices with their start and end apart: 16 -> 16, of which waited for: 12 -> 10; matrix products, arithmetic and copies ran while one was open for 1% -> 1% of each run, Pallas kernels for 1% -> 1%
where the time goes in v7:
time: 129 us
  starting transfers between devices  42.6 us (33%)
  waiting for transfers between devices  39.6 us (31%)
  blocking collectives  34.4 us (27%)
  Pallas kernels  8.15 us (6%)
  other arithmetic  1.85 us (1%)
  between operations  1.38 us (1%)
    ppermute x6, waiting for transfers between devices, to_quad(): lax.ppermute(array, 'recv', [(member, member ^ bits) for member in range(...  26.6 us
    all_to_all x1, blocking collectives, per_device(): lax.all_to_all(pair_sum, 'emit', 0, 0, tiled=True, axis_index_groups=same...  18.4 us
    ppermute x6, starting transfers between devices, along_z(): lax.ppermute(array, 'recv', [(member, (member + 4 * step) % recv_size) fo...  18 us
    all_to_all x1, blocking collectives, per_device(): lax.all_to_all(payload, 'emit', 0, 0, tiled=True, axis_index_groups=same_...  16 us
    ppermute x6, waiting for transfers between devices, along_z(): lax.ppermute(array, 'recv', [(member, (member + 4 * step) % recv_size) fo...  9.6 us
    all_to_all x1, starting transfers between devices, per_device(): lax.all_to_all(total, 'emit', 0, 0, tiled=True).reshape(4, width, lanes)  7.5 us
    all_to_all x1, starting transfers between devices, per_device(): chunks = lax.all_to_all(weights, 'recv', 0, 0, tiled=True)  7.46 us
    ppermute x6, starting transfers between devices, to_quad(): lax.ppermute(array, 'recv', [(member, member ^ bits) for member in range(...  5.47 us
  transfers between devices with their start and end apart: 16, of which 10 were waited for; matrix products, arithmetic and copies ran while one was open for 1% of the time, Pallas kernels for 1%

profile of v7, /device:TPU:1, one launch (start us, length us, event | category | flops | bytes accessed | tf_op | source)
XLA Modules:
  0.0 128.8 jit_solution(14813331887681707208)
XLA Ops:
  0.6 0.0 copy-start
  0.6 0.0 copy-start.1
  0.7 0.0 copy-start.2
  0.7 6.9 %collective-permute-start.2 = (bf16[128,256]{1,0:T(8,128)(2,1)}, bf16[128,256]{1,0:T(8,128)(2,1)S(1)}, u32[]{:S(2)}, u32[]{:S(2)}) collective-permute-start(bf16[128,256]{1,0:T(8,128)(2,1)} %bitcast.27), channel_id=1, source_target_pairs={{0,12},{1,13},{2,14},{3,15},{4,0},{5,1},{6,2},{7,3},{8,4},{9,5},{1... | collective-permute-start | bytes 196616 | tf_op jit(solution)/shard_map/ppermute | solution.py:254
  7.6 1.0 collective-permute-start.1
  8.6 2.3 %collective-permute-start = (bf16[128,256]{1,0:T(8,128)(2,1)}, bf16[128,256]{1,0:T(8,128)(2,1)S(1)}, u32[]{:S(2)}, u32[]{:S(2)}) collective-permute-start(bf16[128,256]{1,0:T(8,128)(2,1)} %bitcast.29), channel_id=1, source_target_pairs={{0,4},{1,5},{2,6},{3,7},{4,8},{5,9},{6,10},{7,11},{8,12},{9,13},{1... | collective-permute-start | bytes 196616 | tf_op jit(solution)/shard_map/ppermute | solution.py:254
  10.8 0.0 collective-permute-done.2
  10.8 4.2 %collective-permute-done.1 = bf16[128,256]{1,0:T(8,128)(2,1)S(1)} collective-permute-done((bf16[128,256]{1,0:T(8,128)(2,1)}, bf16[128,256]{1,0:T(8,128)(2,1)S(1)}, u32[]{:S(2)}, u32[]{:S(2)}) %collective-permute-start.1) | collective-permute-done | bytes 65568 | tf_op jit(solution)/shard_map/ppermute | solution.py:254
  15.0 0.6 collective-permute-done
  15.7 0.9 pad_maximum_fusion.own
  16.5 2.1 %collective-permute-start.5 = (bf16[4,128,256]{2,1,0:T(8,128)(2,1)S(1)}, bf16[4,128,256]{2,1,0:T(8,128)(2,1)S(1)}, u32[]{:S(2)}, u32[]{:S(2)}) collective-permute-start(bf16[4,128,256]{2,1,0:T(8,128)(2,1)S(1)} %pad_maximum_fusion.own), channel_id=1, source_target_pairs={{0,3},{1,2},{2,1},{3,0},{4,7},{5,6},{6,5},{7,4},{8,11},{9,10},{10,... | collective-permute-start | bytes 786440 | tf_op jit(solution)/shard_map/ppermute | solution.py:251
  18.7 0.2 collective-permute-start.4
  18.9 0.4 collective-permute-start.3
  19.9 0.8 concatenate.9.numbers
  20.7 2.2 %collective-permute-done.5.across = bf16[4,128,256]{2,1,0:T(8,128)(2,1)S(1)} collective-permute-done((bf16[4,128,256]{2,1,0:T(8,128)(2,1)S(1)}, bf16[4,128,256]{2,1,0:T(8,128)(2,1)S(1)}, u32[]{:S(2)}, u32[]{:S(2)}) %collective-permute-start.5) | collective-permute-done | bytes 262176 | tf_op jit(solution)/shard_map/ppermute | solution.py:251
  22.9 7.7 %collective-permute-done.4.beside = bf16[4,128,256]{2,1,0:T(8,128)(2,1)S(1)} collective-permute-done((bf16[4,128,256]{2,1,0:T(8,128)(2,1)S(1)}, bf16[4,128,256]{2,1,0:T(8,128)(2,1)S(1)}, u32[]{:S(2)}, u32[]{:S(2)}) %collective-permute-start.4) | collective-permute-done | bytes 262176 | tf_op jit(solution)/shard_map/ppermute | solution.py:251
  30.6 0.0 collective-permute-done.3.pair
  30.6 2.5 %forward_sweep.1 = (f32[8,128,256]{2,1,0:T(8,128)S(1)}, bf16[8,128,256]{2,1,0:T(8,128)(2,1)S(1)}) custom-call(s32[133]{0:T(256)S(1)} %concatenate.9.numbers, bf16[4,128,256]{2,1,0:T(8,128)(2,1)S(1)} %pad_maximum_fusion.own, bf16[4,128,256]{2,1,0:T(8,128)(2,1)S(1)} %collective-permute-done.3.pair, bf16[4,128,256]{2,1,0:T(8,128)(2,1)S(1)} %collective-permute-done.4.beside, ...), custom_call_target="tpu_custom_call" | custom-call | flops 2147483648 | bytes 8388608 | tf_op jit(solution)/shard_map/forward_sweep/pallas_call | solution.py:260
  33.1 1.5 %collective-permute-start.6 = (bf16[8,128,256]{2,1,0:T(8,128)(2,1)S(1)}, bf16[8,128,256]{2,1,0:T(8,128)(2,1)S(1)}, u32[]{:S(2)}, u32[]{:S(2)}) collective-permute-start(bf16[8,128,256]{2,1,0:T(8,128)(2,1)S(1)} %get-tuple-element.20), channel_id=1, source_target_pairs={{0,16},{16,0},{32,48},{48,32},{64,80},{80,64},{96,112},{112,96},{1... | collective-permute-start | bytes 1572872 | tf_op jit(solution)/shard_map/ppermute | solution.py:284
  34.6 1.5 %collective-permute-done.6 = bf16[8,128,256]{2,1,0:T(8,128)(2,1)S(1)} collective-permute-done((bf16[8,128,256]{2,1,0:T(8,128)(2,1)S(1)}, bf16[8,128,256]{2,1,0:T(8,128)(2,1)S(1)}, u32[]{:S(2)}, u32[]{:S(2)}) %collective-permute-start.6) | collective-permute-done | bytes 524320 | tf_op jit(solution)/shard_map/ppermute | solution.py:284
  36.1 0.2 add_convert_fusion
  36.3 18.4 %all_to_all.20.terms = bf16[8,128,256]{2,1,0:T(8,128)(2,1)S(1)} all-to-all(bf16[8,128,256]{2,1,0:T(8,128)(2,1)S(1)} %add_convert_fusion), channel_id=1, replica_groups={{0,32,64,96,128,160,192,224},{16,48,80,112,144,176,208,240},{1,33,65,97..., dimensions={0} | all-to-all | bytes 1048576 | tf_op jit(solution)/shard_map/all_to_all | solution.py:286
  54.7 0.0 copy-done
  54.7 0.0 copy-done.1
  54.7 0.0 copy-done.2
  54.7 0.6 middle.1
  55.3 16.0 %all_to_all.21.held = bf16[8,384,128]{2,1,0:T(8,128)(2,1)S(1)} all-to-all(bf16[8,384,128]{2,1,0:T(8,128)(2,1)S(1)} %middle.1), channel_id=1, replica_groups={{0,32,64,96,128,160,192,224},{16,48,80,112,144,176,208,240},{1,33,65,97..., dimensions={0} | all-to-all | bytes 1572864 | tf_op jit(solution)/shard_map/all_to_all | solution.py:297
  71.3 2.7 %collective-permute-start.7 = (bf16[8,384,128]{2,1,0:T(8,128)(2,1)S(1)}, bf16[8,384,128]{2,1,0:T(8,128)(2,1)S(1)}, u32[]{:S(2)}, u32[]{:S(2)}) collective-permute-start(bf16[8,384,128]{2,1,0:T(8,128)(2,1)S(1)} %all_to_all.21.held), channel_id=1, source_target_pairs={{0,16},{16,0},{32,48},{48,32},{64,80},{80,64},{96,112},{112,96},{1... | collective-permute-start | bytes 2359304 | tf_op jit(solution)/shard_map/ppermute | solution.py:298
  74.0 1.9 %collective-permute-done.7.other = bf16[8,384,128]{2,1,0:T(8,128)(2,1)S(1)} collective-permute-done((bf16[8,384,128]{2,1,0:T(8,128)(2,1)S(1)}, bf16[8,384,128]{2,1,0:T(8,128)(2,1)S(1)}, u32[]{:S(2)}, u32[]{:S(2)}) %collective-permute-start.7) | collective-permute-done | bytes 786464 | tf_op jit(solution)/shard_map/ppermute | solution.py:298
  75.9 3.2 %backward_sweep.1 = (bf16[4,256,128]{2,1,0:T(8,128)(2,1)S(1)}, bf16[4,256,128]{2,1,0:T(8,128)(2,1)S(1)}, bf16[4,256,128]{2,1,0:T(8,128)(2,1)S(1)}, bf16[4,256,128]{2,1,0:T(8,128)(2,1)S(1)}, bf16[16,64,128]{2,1,0:T(8,128)(2,1)}) custom-call(s32[133]{0:T(256)S(1)} %concatenate.9.numbers, bf16[8,384,128]{2,1,0:T(8,128)(2,1)S(1)} %all_to_all.21.held, ...), custom_call_target="tpu_custom_call" | custom-call | flops 2147483648 | bytes 8388608 | tf_op jit(solution)/shard_map/backward_sweep/pallas_call | solution.py:300
  79.1 7.5 %all-to-all-start.2 = ((bf16[16,64,128]{2,1,0:T(8,128)(2,1)}), bf16[16,64,128]{2,1,0:T(8,128)(2,1)S(1)}, u32[]{:S(2)}, u32[]{:S(2)}) async-start(bf16[16,64,128]{2,1,0:T(8,128)(2,1)} %get-tuple-element.21), calls=%async_computation.2 | async-start | bytes 524288 | tf_op jit(solution)/shard_map/all_to_all | solution.py:315
  86.6 1.4 %collective-permute-start.8 = (bf16[4,256,128]{2,1,0:T(8,128)(2,1)S(1)}, bf16[4,256,128]{2,1,0:T(8,128)(2,1)S(1)}, u32[]{:S(2)}, u32[]{:S(2)}) collective-permute-start(bf16[4,256,128]{2,1,0:T(8,128)(2,1)S(1)} %get-tuple-element.23), channel_id=1, source_target_pairs={{0,2},{1,3},{2,0},{3,1},{4,6},{5,7},{6,4},{7,5},{8,10},{9,11},{10,... | collective-permute-start | bytes 786440 | tf_op jit(solution)/shard_map/ppermute | solution.py:251
  88.0 1.2 collective-permute-start.9
  89.1 0.2 collective-permute-start.10
  89.3 10.2 %collective-permute-done.8.pair = bf16[4,256,128]{2,1,0:T(8,128)(2,1)S(1)} collective-permute-done((bf16[4,256,128]{2,1,0:T(8,128)(2,1)S(1)}, bf16[4,256,128]{2,1,0:T(8,128)(2,1)S(1)}, u32[]{:S(2)}, u32[]{:S(2)}) %collective-permute-start.8) | collective-permute-done | bytes 262176 | tf_op jit(solution)/shard_map/ppermute | solution.py:251
  99.5 0.0 collective-permute-done.9.beside
  99.5 6.5 %collective-permute-done.10.across = bf16[4,256,128]{2,1,0:T(8,128)(2,1)S(1)} collective-permute-done((bf16[4,256,128]{2,1,0:T(8,128)(2,1)S(1)}, bf16[4,256,128]{2,1,0:T(8,128)(2,1)S(1)}, u32[]{:S(2)}, u32[]{:S(2)}) %collective-permute-start.10) | collective-permute-done | bytes 262176 | tf_op jit(solution)/shard_map/ppermute | solution.py:251
  106.0 0.1 quad_sum.1
  106.1 0.0 all-to-all-done.2.terms
  106.2 0.9 weights_sum.1
  107.0 7.5 %all-to-all-start.3 = ((f32[16,64,128]{2,1,0:T(8,128)}), f32[16,64,128]{2,1,0:T(8,128)S(1)}, u32[]{:S(2)}, u32[]{:S(2)}) async-start(f32[16,64,128]{2,1,0:T(8,128)} %weights_sum.1), calls=%async_computation.3 | async-start | bytes 1048576 | tf_op jit(solution)/shard_map/all_to_all | solution.py:334
  114.5 2.1 %collective-permute-start.11 = (bf16[256,128]{1,0:T(8,128)(2,1)S(1)}, bf16[256,128]{1,0:T(8,128)(2,1)S(1)}, u32[]{:S(2)}, u32[]{:S(2)}) collective-permute-start(bf16[256,128]{1,0:T(8,128)(2,1)S(1)} %get-tuple-element.31), channel_id=1, source_target_pairs={{0,4},{1,5},{2,6},{3,7},{4,8},{5,9},{6,10},{7,11},{8,12},{9,13},{1... | collective-permute-start | bytes 196616 | tf_op jit(solution)/shard_map/ppermute | solution.py:254
  116.6 2.4 %collective-permute-start.12 = (bf16[256,128]{1,0:T(8,128)(2,1)S(1)}, bf16[256,128]{1,0:T(8,128)(2,1)S(1)}, u32[]{:S(2)}, u32[]{:S(2)}) collective-permute-start(bf16[256,128]{1,0:T(8,128)(2,1)S(1)} %get-tuple-element.32), channel_id=1, source_target_pairs={{0,8},{1,9},{2,10},{3,11},{4,12},{5,13},{6,14},{7,15},{8,0},{9,1},... | collective-permute-start | bytes 196616 | tf_op jit(solution)/shard_map/ppermute | solution.py:254
  119.0 3.3 %collective-permute-start.13 = (bf16[256,128]{1,0:T(8,128)(2,1)S(1)}, bf16[256,128]{1,0:T(8,128)(2,1)S(1)}, u32[]{:S(2)}, u32[]{:S(2)}) collective-permute-start(bf16[256,128]{1,0:T(8,128)(2,1)S(1)} %get-tuple-element.33), channel_id=1, source_target_pairs={{0,12},{1,13},{2,14},{3,15},{4,0},{5,1},{6,2},{7,3},{8,4},{9,5},{1... | collective-permute-start | bytes 196616 | tf_op jit(solution)/shard_map/ppermute | solution.py:254
  122.3 0.0 collective-permute-done.11.refs_1_
  122.3 2.2 %collective-permute-done.12.refs_2_ = bf16[256,128]{1,0:T(8,128)(2,1)S(1)} collective-permute-done((bf16[256,128]{1,0:T(8,128)(2,1)S(1)}, bf16[256,128]{1,0:T(8,128)(2,1)S(1)}, u32[]{:S(2)}, u32[]{:S(2)}) %collective-permute-start.12) | collective-permute-done | bytes 65568 | tf_op jit(solution)/shard_map/ppermute | solution.py:254
  124.5 2.5 %collective-permute-done.13.refs_3_ = bf16[256,128]{1,0:T(8,128)(2,1)S(1)} collective-permute-done((bf16[256,128]{1,0:T(8,128)(2,1)S(1)}, bf16[256,128]{1,0:T(8,128)(2,1)S(1)}, u32[]{:S(2)}, u32[]{:S(2)}) %collective-permute-start.13) | collective-permute-done | bytes 65568 | tf_op jit(solution)/shard_map/ppermute | solution.py:254
  127.1 0.8 features_grad.1
  127.9 0.0 all-to-all-done.3
  128.0 0.8 pad_maximum_fusion.1
  (1 shorter events, 0.0 us)
Async XLA Ops:
  0.6 54.1 %copy-start = (bf16[256,256]{1,0:T(8,128)(2,1)S(1)}, bf16[256,256]{1,0:T(8,128)(2,1)}, u32[]{:S(2)}) copy-start(bf16[256,256]{1,0:T(8,128)(2,1)} %refs_4_.1) | copy-start | bytes 393220
  0.6 54.1 %copy-start.1 = (bf16[256,256]{1,0:T(8,128)(2,1)S(1)}, bf16[256,256]{1,0:T(8,128)(2,1)}, u32[]{:S(2)}) copy-start(bf16[256,256]{1,0:T(8,128)(2,1)} %w_out.1) | copy-start | bytes 393220
  0.7 54.1 %copy-start.2 = (bf16[1,128,256]{2,1,0:T(8,128)(2,1)S(1)}, bf16[1,128,256]{2,1,0:T(8,128)(2,1)}, u32[]{:S(2)}) copy-start(bf16[1,128,256]{2,1,0:T(8,128)(2,1)} %param.9) | copy-start | bytes 196612
  0.7 10.2 %collective-permute-start.2 = (bf16[128,256]{1,0:T(8,128)(2,1)}, bf16[128,256]{1,0:T(8,128)(2,1)S(1)}, u32[]{:S(2)}, u32[]{:S(2)}) collective-permute-start(bf16[128,256]{1,0:T(8,128)(2,1)} %bitcast.27), channel_id=1, source_target_pairs={{0,12},{1,13},{2,14},{3,15},{4,0},{5,1},{6,2},{7,3},{8,4},{9,5},{1... | collective-permute-start | bytes 196616 | tf_op jit(solution)/shard_map/ppermute | solution.py:254
  7.6 7.4 %collective-permute-start.1 = (bf16[128,256]{1,0:T(8,128)(2,1)}, bf16[128,256]{1,0:T(8,128)(2,1)S(1)}, u32[]{:S(2)}, u32[]{:S(2)}) collective-permute-start(bf16[128,256]{1,0:T(8,128)(2,1)} %bitcast.28), channel_id=1, source_target_pairs={{0,8},{1,9},{2,10},{3,11},{4,12},{5,13},{6,14},{7,15},{8,0},{9,1},... | collective-permute-start | bytes 196616 | tf_op jit(solution)/shard_map/ppermute | solution.py:254
  8.6 7.1 %collective-permute-start = (bf16[128,256]{1,0:T(8,128)(2,1)}, bf16[128,256]{1,0:T(8,128)(2,1)S(1)}, u32[]{:S(2)}, u32[]{:S(2)}) collective-permute-start(bf16[128,256]{1,0:T(8,128)(2,1)} %bitcast.29), channel_id=1, source_target_pairs={{0,4},{1,5},{2,6},{3,7},{4,8},{5,9},{6,10},{7,11},{8,12},{9,13},{1... | collective-permute-start | bytes 196616 | tf_op jit(solution)/shard_map/ppermute | solution.py:254
  16.5 6.3 %collective-permute-start.5 = (bf16[4,128,256]{2,1,0:T(8,128)(2,1)S(1)}, bf16[4,128,256]{2,1,0:T(8,128)(2,1)S(1)}, u32[]{:S(2)}, u32[]{:S(2)}) collective-permute-start(bf16[4,128,256]{2,1,0:T(8,128)(2,1)S(1)} %pad_maximum_fusion.own), channel_id=1, source_target_pairs={{0,3},{1,2},{2,1},{3,0},{4,7},{5,6},{6,5},{7,4},{8,11},{9,10},{10,... | collective-permute-start | bytes 786440 | tf_op jit(solution)/shard_map/ppermute | solution.py:251
  18.7 11.9 %collective-permute-start.4 = (bf16[4,128,256]{2,1,0:T(8,128)(2,1)S(1)}, bf16[4,128,256]{2,1,0:T(8,128)(2,1)S(1)}, u32[]{:S(2)}, u32[]{:S(2)}) collective-permute-start(bf16[4,128,256]{2,1,0:T(8,128)(2,1)S(1)} %pad_maximum_fusion.own), channel_id=1, source_target_pairs={{0,1},{1,0},{2,3},{3,2},{4,5},{5,4},{6,7},{7,6},{8,9},{9,8},{10,11... | collective-permute-start | bytes 786440 | tf_op jit(solution)/shard_map/ppermute | solution.py:251
  18.9 11.7 %collective-permute-start.3 = (bf16[4,128,256]{2,1,0:T(8,128)(2,1)S(1)}, bf16[4,128,256]{2,1,0:T(8,128)(2,1)S(1)}, u32[]{:S(2)}, u32[]{:S(2)}) collective-permute-start(bf16[4,128,256]{2,1,0:T(8,128)(2,1)S(1)} %pad_maximum_fusion.own), channel_id=1, source_target_pairs={{0,2},{1,3},{2,0},{3,1},{4,6},{5,7},{6,4},{7,5},{8,10},{9,11},{10,... | collective-permute-start | bytes 786440 | tf_op jit(solution)/shard_map/ppermute | solution.py:251
  33.1 3.1 %collective-permute-start.6 = (bf16[8,128,256]{2,1,0:T(8,128)(2,1)S(1)}, bf16[8,128,256]{2,1,0:T(8,128)(2,1)S(1)}, u32[]{:S(2)}, u32[]{:S(2)}) collective-permute-start(bf16[8,128,256]{2,1,0:T(8,128)(2,1)S(1)} %get-tuple-element.20), channel_id=1, source_target_pairs={{0,16},{16,0},{32,48},{48,32},{64,80},{80,64},{96,112},{112,96},{1... | collective-permute-start | bytes 1572872 | tf_op jit(solution)/shard_map/ppermute | solution.py:284
  71.3 4.6 %collective-permute-start.7 = (bf16[8,384,128]{2,1,0:T(8,128)(2,1)S(1)}, bf16[8,384,128]{2,1,0:T(8,128)(2,1)S(1)}, u32[]{:S(2)}, u32[]{:S(2)}) collective-permute-start(bf16[8,384,128]{2,1,0:T(8,128)(2,1)S(1)} %all_to_all.21.held), channel_id=1, source_target_pairs={{0,16},{16,0},{32,48},{48,32},{64,80},{80,64},{96,112},{112,96},{1... | collective-permute-start | bytes 2359304 | tf_op jit(solution)/shard_map/ppermute | solution.py:298
  79.1 27.0 %all-to-all-start.2 = ((bf16[16,64,128]{2,1,0:T(8,128)(2,1)}), bf16[16,64,128]{2,1,0:T(8,128)(2,1)S(1)}, u32[]{:S(2)}, u32[]{:S(2)}) async-start(bf16[16,64,128]{2,1,0:T(8,128)(2,1)} %get-tuple-element.21), calls=%async_computation.2 | async-start | bytes 524288 | tf_op jit(solution)/shard_map/all_to_all | solution.py:315
  86.6 12.9 %collective-permute-start.8 = (bf16[4,256,128]{2,1,0:T(8,128)(2,1)S(1)}, bf16[4,256,128]{2,1,0:T(8,128)(2,1)S(1)}, u32[]{:S(2)}, u32[]{:S(2)}) collective-permute-start(bf16[4,256,128]{2,1,0:T(8,128)(2,1)S(1)} %get-tuple-element.23), channel_id=1, source_target_pairs={{0,2},{1,3},{2,0},{3,1},{4,6},{5,7},{6,4},{7,5},{8,10},{9,11},{10,... | collective-permute-start | bytes 786440 | tf_op jit(solution)/shard_map/ppermute | solution.py:251
  88.0 11.5 %collective-permute-start.9 = (bf16[4,256,128]{2,1,0:T(8,128)(2,1)S(1)}, bf16[4,256,128]{2,1,0:T(8,128)(2,1)S(1)}, u32[]{:S(2)}, u32[]{:S(2)}) collective-permute-start(bf16[4,256,128]{2,1,0:T(8,128)(2,1)S(1)} %get-tuple-element.24), channel_id=1, source_target_pairs={{0,1},{1,0},{2,3},{3,2},{4,5},{5,4},{6,7},{7,6},{8,9},{9,8},{10,11... | collective-permute-start | bytes 786440 | tf_op jit(solution)/shard_map/ppermute | solution.py:251
  89.1 16.9 %collective-permute-start.10 = (bf16[4,256,128]{2,1,0:T(8,128)(2,1)S(1)}, bf16[4,256,128]{2,1,0:T(8,128)(2,1)S(1)}, u32[]{:S(2)}, u32[]{:S(2)}) collective-permute-start(bf16[4,256,128]{2,1,0:T(8,128)(2,1)S(1)} %get-tuple-element.25), channel_id=1, source_target_pairs={{0,3},{1,2},{2,1},{3,0},{4,7},{5,6},{6,5},{7,4},{8,11},{9,10},{10,... | collective-permute-start | bytes 786440 | tf_op jit(solution)/shard_map/ppermute | solution.py:251
  107.0 20.9 %all-to-all-start.3 = ((f32[16,64,128]{2,1,0:T(8,128)}), f32[16,64,128]{2,1,0:T(8,128)S(1)}, u32[]{:S(2)}, u32[]{:S(2)}) async-start(f32[16,64,128]{2,1,0:T(8,128)} %weights_sum.1), calls=%async_computation.3 | async-start | bytes 1048576 | tf_op jit(solution)/shard_map/all_to_all | solution.py:334
  114.5 7.8 %collective-permute-start.11 = (bf16[256,128]{1,0:T(8,128)(2,1)S(1)}, bf16[256,128]{1,0:T(8,128)(2,1)S(1)}, u32[]{:S(2)}, u32[]{:S(2)}) collective-permute-start(bf16[256,128]{1,0:T(8,128)(2,1)S(1)} %get-tuple-element.31), channel_id=1, source_target_pairs={{0,4},{1,5},{2,6},{3,7},{4,8},{5,9},{6,10},{7,11},{8,12},{9,13},{1... | collective-permute-start | bytes 196616 | tf_op jit(solution)/shard_map/ppermute | solution.py:254
  116.6 7.9 %collective-permute-start.12 = (bf16[256,128]{1,0:T(8,128)(2,1)S(1)}, bf16[256,128]{1,0:T(8,128)(2,1)S(1)}, u32[]{:S(2)}, u32[]{:S(2)}) collective-permute-start(bf16[256,128]{1,0:T(8,128)(2,1)S(1)} %get-tuple-element.32), channel_id=1, source_target_pairs={{0,8},{1,9},{2,10},{3,11},{4,12},{5,13},{6,14},{7,15},{8,0},{9,1},... | collective-permute-start | bytes 196616 | tf_op jit(solution)/shard_map/ppermute | solution.py:254
  119.0 8.1 %collective-permute-start.13 = (bf16[256,128]{1,0:T(8,128)(2,1)S(1)}, bf16[256,128]{1,0:T(8,128)(2,1)S(1)}, u32[]{:S(2)}, u32[]{:S(2)}) collective-permute-start(bf16[256,128]{1,0:T(8,128)(2,1)S(1)} %get-tuple-element.33), channel_id=1, source_target_pairs={{0,12},{1,13},{2,14},{3,15},{4,0},{5,1},{6,2},{7,3},{8,4},{9,5},{1... | collective-permute-start | bytes 196616 | tf_op jit(solution)/shard_map/ppermute | solution.py:254

commit v8 on v6

--- a/solution.py
+++ b/solution.py
@@ -121,7 +121,7 @@
 
 
 def backward_kernel(
-    numbers, held, other, tiles, own, pair, beside, across, weights, grads, acc, ring, sems
+    numbers, held, other, tiles, own, pair, beside, across, grads, acc, ring, sems
 ):
     live, core, column, parity, height, emit_block, recv_block = unpack(numbers, tiles.shape[0])
     width, lanes = acc.shape[1], held.shape[2]
@@ -145,14 +145,6 @@
         return jnp.dot(grads[recv_block(slot)], tile, preferred_element_type=f32)
 
     sweep(live, tiles, ring, sems, prepare, product, emit_block, acc)
-    chunk = weights.shape[1]
-    mine = pl.ds(pl.multiple_of(width + core * chunk, chunk), chunk)
-    summed = held[0, mine, :].astype(f32) + other[0, mine, :].astype(f32)
-    for block in range(1, held.shape[0]):
-        summed += held[block, mine, :].astype(f32) + other[block, mine, :].astype(f32)
-    for piece in range(weights.shape[0]):
-        weights[piece] = summed.astype(bf16)
-
     def hand_out(near):
         for out, side, odd in (
             (own, near, parity),
@@ -174,15 +166,31 @@
         hand_out(1)
 
 
+def copy_kernel(source, out):
+    out[...] = source[...]
+
+
+def chunk_kernel(held, other, second_core, out):
+    chunk = out.shape[1]
+    width = held.shape[1] - 2 * chunk
+
+    def summed(rows):
+        total = held[0, rows, :].astype(f32) + other[0, rows, :].astype(f32)
+        for block in range(1, held.shape[0]):
+            total += held[block, rows, :].astype(f32) + other[block, rows, :].astype(f32)
+        return total
+
+    first, second = summed(slice(width, width + chunk)), summed(slice(width + chunk, None))
+    mine = jnp.where(second_core[0:1, :] > 0.5, second, first).astype(bf16)
+    for piece in range(out.shape[0]):
+        out[piece] = mine
+
+
 def quad_kernel(own, pair, beside, across, *outs):
     for step, out in enumerate(outs):
         near = own[step].astype(f32) + pair[step].astype(f32)
         far = beside[step].astype(f32) + across[step].astype(f32)
         out[...] = (near + far).astype(bf16)
-
-
-def copy_kernel(source, out):
-    out[...] = source[...]
 
 
 def weights_kernel(terms, total):
@@ -193,14 +201,18 @@
         total[piece] = summed
 
 
-def features_kernel(*refs):
-    terms, w_msg, grad = refs[:-2], refs[-2], refs[-1]
+def result_kernel(*refs):
+    terms, (w_msg, gathered, grad, grad_w_msg, grad_w_out) = refs[:-5], refs[-5:]
+    lanes = gathered.shape[2]
     summed = terms[0][...].astype(f32)
     for term in terms[1:]:
         summed += term[...].astype(f32)
     grad[...] = lax.dot_general(
         summed.astype(bf16), w_msg[...], (((0,), (1,)), ((), ())), preferred_element_type=f32
     ).astype(bf16)
+    for quarter, out in enumerate((grad_w_out, grad_w_out, grad_w_msg, grad_w_msg)):
+        at = quarter % 2 * lanes
+        out[:, at : at + lanes] = gathered[quarter]
 
 
 def in_vmem(count):
@@ -247,6 +259,7 @@
         pltpu.SemaphoreType.DMA((ring_depth,)),
     ]
 
+    second_core = jnp.broadcast_to(core.astype(f32), (8, lanes))
     sweep_cost = pl.CostEstimate(
         flops=2 * values.size * width, bytes_accessed=2 * values.size, transcendentals=0
     )
@@ -309,12 +322,21 @@
     held = lax.all_to_all(payload, "emit", 0, 0, tiled=True, axis_index_groups=same_core)
     other = lax.ppermute(held, "emit", swap)
 
-    own, pair, beside, across, weights = pl.pallas_call(
+    weights = pl.pallas_call(
+        chunk_kernel,
+        out_shape=struct((recv_size, chunk // 2, lanes), bf16),
+        in_specs=in_vmem(3),
+        out_specs=in_vmem(1)[0],
+        compiler_params=limits(8),
+        name="weights_chunk",
+    )(held, other, second_core)
+    chunks = lax.all_to_all(weights, "recv", 0, 0, tiled=True)
+
+    own, pair, beside, across = pl.pallas_call(
         backward_kernel,
-        out_shape=(struct((steps, width, lanes), bf16),) * 4
-        + (struct((recv_size, chunk // 2, lanes), bf16),),
+        out_shape=(struct((steps, width, lanes), bf16),) * 4,
         in_specs=in_smem(1) + in_vmem(2) + [in_hbm],
-        out_specs=tuple(in_vmem(5)),
+        out_specs=tuple(in_vmem(4)),
         scratch_shapes=[
             pltpu.VMEM((recv_blocks, width, tile_dim), bf16),
             pltpu.VMEM((emit_blocks + 1, width, tile_dim), f32),
@@ -324,8 +346,6 @@
         cost_estimate=sweep_cost,
         name="backward_sweep",
     )(numbers, held, other, values)
-    pair, weights = lax.optimization_barrier((to_quad(pair, 2), weights))
-    chunks = lax.all_to_all(weights, "recv", 0, 0, tiled=True)
     terms = pl.pallas_call(
         quad_kernel,
         out_shape=(struct((width, lanes), bf16),) * steps,
@@ -333,9 +353,8 @@
         out_specs=tuple(in_vmem(steps)),
         compiler_params=limits(8),
         name="quad_sum",
-    )(own, pair, to_quad(beside, 1), to_quad(across, 3))
-    terms = [terms[0]] + [along_z(terms[step], step) for step in range(1, steps)]
-    chunks, terms[1] = lax.optimization_barrier((chunks, terms[1]))
+    )(own, to_quad(pair, 2), to_quad(beside, 1), to_quad(across, 3))
+    chunks, terms = lax.optimization_barrier((chunks, terms))
 
     total = pl.pallas_call(
         weights_kernel,
@@ -346,17 +365,20 @@
         name="weights_sum",
     )(chunks)
     gathered = lax.all_to_all(total, "emit", 0, 0, tiled=True).reshape(4, width, lanes)
-    grad_features = pl.pallas_call(
-        features_kernel,
-        out_shape=struct((facet_rows, width), bf16),
-        in_specs=in_vmem(steps + 1),
-        out_specs=in_vmem(1)[0],
-        compiler_params=limits(8),
-        name="features_grad",
-    )(*terms, w_msg)[None]
-    grad_w_out = jnp.concatenate([gathered[0], gathered[1]], axis=1)
-    grad_w_msg = jnp.concatenate([gathered[2], gathered[3]], axis=1)
-    return (grad_features, grad_w_msg, grad_w_out)
+    terms = [terms[0]] + [along_z(terms[step], step) for step in range(1, steps)]
+    grad_features, grad_w_msg, grad_w_out = pl.pallas_call(
+        result_kernel,
+        out_shape=(
+            struct((facet_rows, width), bf16),
+            struct((width, width), f32),
+            struct((width, width), f32),
+        ),
+        in_specs=in_vmem(steps + 2),
+        out_specs=tuple(in_vmem(3)),
+        compiler_params=limits(8),
+        name="results",
+    )(*terms, w_msg, gathered)
+    return (grad_features[None], grad_w_msg, grad_w_out)
 
 
 def solution(mesh):

time: 136 us -> 122 us (0.90); the launches traced: 136 us -> 120 us
  waiting for transfers between devices: 45.5 us -> 33.2 us
  blocking collectives: 34.1 us -> 31.3 us
    ppermute x6, waiting for transfers between devices: 14.8 us -> 7.28 us  [along_z(): lax.ppermute(array, 'recv', [(member, (member + 4 * step) % recv_size) fo...]
    all_to_all x1, starting transfers between devices: 8.85 us -> 4.01 us  [per_device(): lax.all_to_all(total, 'emit', 0, 0, tiled=True).reshape(4, width, lanes)]
    ppermute x6, waiting for transfers between devices: 27.2 us -> 22.4 us  [to_quad(): lax.ppermute(array, 'recv', [(member, member ^ bits) for member in range(...]
    all_to_all x1, blocking collectives: 18.7 us -> 15.3 us  [per_device(): lax.all_to_all(pair_sum, 'emit', 0, 0, tiled=True, axis_index_groups=same...]
    all_to_all x1, starting transfers between devices: 6.68 us -> 8.53 us  [per_device(): chunks = lax.all_to_all(weights, 'recv', 0, 0, tiled=True)]
    ppermute x6, starting transfers between devices: 6.8 us -> 8.23 us  [to_quad(): lax.ppermute(array, 'recv', [(member, member ^ bits) for member in range(...]
  transfers between devices with their start and end apart: 16 -> 16, of which waited for: 12 -> 11; matrix products, arithmetic and copies ran while one was open for 1% -> 1% of each run, Pallas kernels for 1% -> 2%
where the time goes in v8:
time: 122 us; the launch traced here: 120 us
  starting transfers between devices  43.9 us (36%)
  waiting for transfers between devices  33.2 us (27%)
  blocking collectives  31.3 us (26%)
  Pallas kernels  8.27 us (7%)
  local copies, waits for them, and re-layouts  1.64 us (1%)
  between operations  1.38 us (1%)
    ppermute x6, waiting for transfers between devices, to_quad(): lax.ppermute(array, 'recv', [(member, member ^ bits) for member in range(...  22.4 us
    ppermute x6, starting transfers between devices, along_z(): lax.ppermute(array, 'recv', [(member, (member + 4 * step) % recv_size) fo...  18 us
    all_to_all x1, blocking collectives, per_device(): lax.all_to_all(payload, 'emit', 0, 0, tiled=True, axis_index_groups=same_...  16 us
    all_to_all x1, blocking collectives, per_device(): lax.all_to_all(pair_sum, 'emit', 0, 0, tiled=True, axis_index_groups=same...  15.3 us
    all_to_all x1, starting transfers between devices, per_device(): chunks = lax.all_to_all(weights, 'recv', 0, 0, tiled=True)  8.53 us
    ppermute x6, starting transfers between devices, to_quad(): lax.ppermute(array, 'recv', [(member, member ^ bits) for member in range(...  8.23 us
    ppermute x6, waiting for transfers between devices, along_z(): lax.ppermute(array, 'recv', [(member, (member + 4 * step) % recv_size) fo...  7.28 us
    all_to_all x1, starting transfers between devices, per_device(): lax.all_to_all(total, 'emit', 0, 0, tiled=True).reshape(4, width, lanes)  4.01 us
  transfers between devices with their start and end apart: 16, of which 11 were waited for; matrix products, arithmetic and copies ran while one was open for 1% of the time, Pallas kernels for 2%

profile of v8, /device:TPU:1, one launch (start us, length us, event | category | flops | bytes accessed | tf_op | source)
XLA Modules:
  0.0 119.8 jit_solution(2216913681440191831)
XLA Ops:
  0.6 0.0 copy-start
  0.6 0.0 copy-start.1
  0.7 0.0 copy-start.2
  0.7 6.9 %collective-permute-start.2 = (bf16[128,256]{1,0:T(8,128)(2,1)}, bf16[128,256]{1,0:T(8,128)(2,1)S(1)}, u32[]{:S(2)}, u32[]{:S(2)}) collective-permute-start(bf16[128,256]{1,0:T(8,128)(2,1)} %bitcast.20), channel_id=1, source_target_pairs={{0,12},{1,13},{2,14},{3,15},{4,0},{5,1},{6,2},{7,3},{8,4},{9,5},{1... | collective-permute-start | bytes 196616 | tf_op jit(solution)/shard_map/ppermute | solution.py:271
  7.6 1.0 collective-permute-start.1
  8.6 2.3 %collective-permute-start = (bf16[128,256]{1,0:T(8,128)(2,1)}, bf16[128,256]{1,0:T(8,128)(2,1)S(1)}, u32[]{:S(2)}, u32[]{:S(2)}) collective-permute-start(bf16[128,256]{1,0:T(8,128)(2,1)} %bitcast.22), channel_id=1, source_target_pairs={{0,4},{1,5},{2,6},{3,7},{4,8},{5,9},{6,10},{7,11},{8,12},{9,13},{1... | collective-permute-start | bytes 196616 | tf_op jit(solution)/shard_map/ppermute | solution.py:271
  10.8 0.0 copy-start.3
  10.8 0.9 copy-done.3
  11.7 0.0 collective-permute-done.2
  11.7 3.3 %collective-permute-done.1 = bf16[128,256]{1,0:T(8,128)(2,1)S(1)} collective-permute-done((bf16[128,256]{1,0:T(8,128)(2,1)}, bf16[128,256]{1,0:T(8,128)(2,1)S(1)}, u32[]{:S(2)}, u32[]{:S(2)}) %collective-permute-start.1) | collective-permute-done | bytes 65568 | tf_op jit(solution)/shard_map/ppermute | solution.py:271
  15.0 0.6 collective-permute-done
  15.7 2.1 %collective-permute-start.5 = (bf16[4,128,256]{2,1,0:T(8,128)(2,1)S(1)}, bf16[4,128,256]{2,1,0:T(8,128)(2,1)S(1)}, u32[]{:S(2)}, u32[]{:S(2)}) collective-permute-start(bf16[4,128,256]{2,1,0:T(8,128)(2,1)S(1)} %pad_maximum_fusion.own), channel_id=1, source_target_pairs={{0,3},{1,2},{2,1},{3,0},{4,7},{5,6},{6,5},{7,4},{8,11},{9,10},{10,... | collective-permute-start | bytes 786440 | tf_op jit(solution)/shard_map/ppermute | solution.py:268
  17.8 0.2 collective-permute-start.4
  18.0 0.4 collective-permute-start.3
  19.1 0.8 concatenate.3.numbers
  19.9 2.2 %collective-permute-done.5.across = bf16[4,128,256]{2,1,0:T(8,128)(2,1)S(1)} collective-permute-done((bf16[4,128,256]{2,1,0:T(8,128)(2,1)S(1)}, bf16[4,128,256]{2,1,0:T(8,128)(2,1)S(1)}, u32[]{:S(2)}, u32[]{:S(2)}) %collective-permute-start.5) | collective-permute-done | bytes 262176 | tf_op jit(solution)/shard_map/ppermute | solution.py:268
  22.0 7.7 %collective-permute-done.4.beside = bf16[4,128,256]{2,1,0:T(8,128)(2,1)S(1)} collective-permute-done((bf16[4,128,256]{2,1,0:T(8,128)(2,1)S(1)}, bf16[4,128,256]{2,1,0:T(8,128)(2,1)S(1)}, u32[]{:S(2)}, u32[]{:S(2)}) %collective-permute-start.4) | collective-permute-done | bytes 262176 | tf_op jit(solution)/shard_map/ppermute | solution.py:268
  29.8 0.0 collective-permute-done.3.pair
  29.8 2.5 %forward_sweep.1 = (f32[8,128,256]{2,1,0:T(8,128)S(1)}, bf16[8,128,256]{2,1,0:T(8,128)(2,1)S(1)}) custom-call(s32[133]{0:T(256)S(1)} %concatenate.3.numbers, bf16[4,128,256]{2,1,0:T(8,128)(2,1)S(1)} %pad_maximum_fusion.own, bf16[4,128,256]{2,1,0:T(8,128)(2,1)S(1)} %collective-permute-done.3.pair, bf16[4,128,256]{2,1,0:T(8,128)(2,1)S(1)} %collective-permute-done.4.beside, ...), custom_call_target="tpu_custom_call" | custom-call | flops 2147483648 | bytes 8388608 | tf_op jit(solution)/shard_map/forward_sweep/pallas_call | solution.py:285
  32.2 2.5 %collective-permute-start.6 = (bf16[8,128,256]{2,1,0:T(8,128)(2,1)S(1)}, bf16[8,128,256]{2,1,0:T(8,128)(2,1)S(1)}, u32[]{:S(2)}, u32[]{:S(2)}) collective-permute-start(bf16[8,128,256]{2,1,0:T(8,128)(2,1)S(1)} %get-tuple-element.22), channel_id=1, source_target_pairs={{0,16},{16,0},{32,48},{48,32},{64,80},{80,64},{96,112},{112,96},{1... | collective-permute-start | bytes 1572872 | tf_op jit(solution)/shard_map/ppermute | solution.py:309
  34.7 1.5 %collective-permute-done.6 = bf16[8,128,256]{2,1,0:T(8,128)(2,1)S(1)} collective-permute-done((bf16[8,128,256]{2,1,0:T(8,128)(2,1)S(1)}, bf16[8,128,256]{2,1,0:T(8,128)(2,1)S(1)}, u32[]{:S(2)}, u32[]{:S(2)}) %collective-permute-start.6) | collective-permute-done | bytes 524320 | tf_op jit(solution)/shard_map/ppermute | solution.py:309
  36.2 0.1 add_convert_fusion
  36.4 15.3 %all_to_all.20.terms = bf16[8,128,256]{2,1,0:T(8,128)(2,1)S(1)} all-to-all(bf16[8,128,256]{2,1,0:T(8,128)(2,1)S(1)} %add_convert_fusion), channel_id=1, replica_groups={{0,32,64,96,128,160,192,224},{16,48,80,112,144,176,208,240},{1,33,65,97..., dimensions={0} | all-to-all | bytes 1048576 | tf_op jit(solution)/shard_map/all_to_all | solution.py:311
  51.7 0.0 copy-done
  51.7 0.0 copy-done.1
  51.7 0.0 copy-done.2
  51.7 0.6 middle.1
  52.3 16.0 %all_to_all.21.held = bf16[8,384,128]{2,1,0:T(8,128)(2,1)S(1)} all-to-all(bf16[8,384,128]{2,1,0:T(8,128)(2,1)S(1)} %middle.1), channel_id=1, replica_groups={{0,32,64,96,128,160,192,224},{16,48,80,112,144,176,208,240},{1,33,65,97..., dimensions={0} | all-to-all | bytes 1572864 | tf_op jit(solution)/shard_map/all_to_all | solution.py:322
  68.3 2.7 %collective-permute-start.7 = (bf16[8,384,128]{2,1,0:T(8,128)(2,1)S(1)}, bf16[8,384,128]{2,1,0:T(8,128)(2,1)S(1)}, u32[]{:S(2)}, u32[]{:S(2)}) collective-permute-start(bf16[8,384,128]{2,1,0:T(8,128)(2,1)S(1)} %all_to_all.21.held), channel_id=1, source_target_pairs={{0,16},{16,0},{32,48},{48,32},{64,80},{80,64},{96,112},{112,96},{1... | collective-permute-start | bytes 2359304 | tf_op jit(solution)/shard_map/ppermute | solution.py:323
  71.0 1.9 %collective-permute-done.7.other = bf16[8,384,128]{2,1,0:T(8,128)(2,1)S(1)} collective-permute-done((bf16[8,384,128]{2,1,0:T(8,128)(2,1)S(1)}, bf16[8,384,128]{2,1,0:T(8,128)(2,1)S(1)}, u32[]{:S(2)}, u32[]{:S(2)}) %collective-permute-start.7) | collective-permute-done | bytes 786464 | tf_op jit(solution)/shard_map/ppermute | solution.py:323
  72.9 0.8 weights_chunk.1
  73.7 8.5 %all-to-all-start.2 = ((bf16[16,64,128]{2,1,0:T(8,128)(2,1)}), bf16[16,64,128]{2,1,0:T(8,128)(2,1)S(1)}, u32[]{:S(2)}, u32[]{:S(2)}) async-start(bf16[16,64,128]{2,1,0:T(8,128)(2,1)} %weights_chunk.1), calls=%async_computation.2 | async-start | bytes 524288 | tf_op jit(solution)/shard_map/all_to_all | solution.py:333
  82.2 2.5 %backward_sweep.1 = (bf16[4,256,128]{2,1,0:T(8,128)(2,1)S(1)}, bf16[4,256,128]{2,1,0:T(8,128)(2,1)S(1)}, bf16[4,256,128]{2,1,0:T(8,128)(2,1)S(1)}, bf16[4,256,128]{2,1,0:T(8,128)(2,1)S(1)}) custom-call(s32[133]{0:T(256)S(1)} %concatenate.3.numbers, bf16[8,384,128]{2,1,0:T(8,128)(2,1)S(1)} %all_to_all.21.held, ...), custom_call_target="tpu_custom_call" | custom-call | flops 2147483648 | bytes 8388608 | tf_op jit(solution)/shard_map/backward_sweep/pallas_call | solution.py:335
  84.7 1.4 %collective-permute-start.8 = (bf16[4,256,128]{2,1,0:T(8,128)(2,1)S(1)}, bf16[4,256,128]{2,1,0:T(8,128)(2,1)S(1)}, u32[]{:S(2)}, u32[]{:S(2)}) collective-permute-start(bf16[4,256,128]{2,1,0:T(8,128)(2,1)S(1)} %get-tuple-element.24), channel_id=1, source_target_pairs={{0,2},{1,3},{2,0},{3,1},{4,6},{5,7},{6,4},{7,5},{8,10},{9,11},{10,... | collective-permute-start | bytes 786440 | tf_op jit(solution)/shard_map/ppermute | solution.py:268
  86.2 3.0 %collective-permute-start.9 = (bf16[4,256,128]{2,1,0:T(8,128)(2,1)S(1)}, bf16[4,256,128]{2,1,0:T(8,128)(2,1)S(1)}, u32[]{:S(2)}, u32[]{:S(2)}) collective-permute-start(bf16[4,256,128]{2,1,0:T(8,128)(2,1)S(1)} %get-tuple-element.25), channel_id=1, source_target_pairs={{0,1},{1,0},{2,3},{3,2},{4,5},{5,4},{6,7},{7,6},{8,9},{9,8},{10,11... | collective-permute-start | bytes 786440 | tf_op jit(solution)/shard_map/ppermute | solution.py:268
  89.1 1.1 collective-permute-start.10
  90.2 5.1 %collective-permute-done.8.pair = bf16[4,256,128]{2,1,0:T(8,128)(2,1)S(1)} collective-permute-done((bf16[4,256,128]{2,1,0:T(8,128)(2,1)S(1)}, bf16[4,256,128]{2,1,0:T(8,128)(2,1)S(1)}, u32[]{:S(2)}, u32[]{:S(2)}) %collective-permute-start.8) | collective-permute-done | bytes 262176 | tf_op jit(solution)/shard_map/ppermute | solution.py:268
  95.3 6.0 %collective-permute-done.9.beside = bf16[4,256,128]{2,1,0:T(8,128)(2,1)S(1)} collective-permute-done((bf16[4,256,128]{2,1,0:T(8,128)(2,1)S(1)}, bf16[4,256,128]{2,1,0:T(8,128)(2,1)S(1)}, u32[]{:S(2)}, u32[]{:S(2)}) %collective-permute-start.9) | collective-permute-done | bytes 262176 | tf_op jit(solution)/shard_map/ppermute | solution.py:268
  101.2 1.5 %collective-permute-done.10.across = bf16[4,256,128]{2,1,0:T(8,128)(2,1)S(1)} collective-permute-done((bf16[4,256,128]{2,1,0:T(8,128)(2,1)S(1)}, bf16[4,256,128]{2,1,0:T(8,128)(2,1)S(1)}, u32[]{:S(2)}, u32[]{:S(2)}) %collective-permute-start.10) | collective-permute-done | bytes 262176 | tf_op jit(solution)/shard_map/ppermute | solution.py:268
  102.7 0.1 quad_sum.1
  102.9 0.0 all-to-all-done.2.terms
  102.9 0.9 weights_sum.1
  103.8 4.0 %all-to-all-start.3 = ((f32[16,64,128]{2,1,0:T(8,128)}), f32[16,64,128]{2,1,0:T(8,128)S(1)}, u32[]{:S(2)}, u32[]{:S(2)}) async-start(f32[16,64,128]{2,1,0:T(8,128)} %weights_sum.1), calls=%async_computation.3 | async-start | bytes 1048576 | tf_op jit(solution)/shard_map/all_to_all | solution.py:367
  107.8 2.1 %collective-permute-start.11 = (bf16[256,128]{1,0:T(8,128)(2,1)S(1)}, bf16[256,128]{1,0:T(8,128)(2,1)S(1)}, u32[]{:S(2)}, u32[]{:S(2)}) collective-permute-start(bf16[256,128]{1,0:T(8,128)(2,1)S(1)} %get-tuple-element.32), channel_id=1, source_target_pairs={{0,4},{1,5},{2,6},{3,7},{4,8},{5,9},{6,10},{7,11},{8,12},{9,13},{1... | collective-permute-start | bytes 196616 | tf_op jit(solution)/shard_map/ppermute | solution.py:271
  109.9 2.5 %collective-permute-start.12 = (bf16[256,128]{1,0:T(8,128)(2,1)S(1)}, bf16[256,128]{1,0:T(8,128)(2,1)S(1)}, u32[]{:S(2)}, u32[]{:S(2)}) collective-permute-start(bf16[256,128]{1,0:T(8,128)(2,1)S(1)} %get-tuple-element.33), channel_id=1, source_target_pairs={{0,8},{1,9},{2,10},{3,11},{4,12},{5,13},{6,14},{7,15},{8,0},{9,1},... | collective-permute-start | bytes 196616 | tf_op jit(solution)/shard_map/ppermute | solution.py:271
  112.3 3.2 %collective-permute-start.13 = (bf16[256,128]{1,0:T(8,128)(2,1)S(1)}, bf16[256,128]{1,0:T(8,128)(2,1)S(1)}, u32[]{:S(2)}, u32[]{:S(2)}) collective-permute-start(bf16[256,128]{1,0:T(8,128)(2,1)S(1)} %get-tuple-element.34), channel_id=1, source_target_pairs={{0,12},{1,13},{2,14},{3,15},{4,0},{5,1},{6,2},{7,3},{8,4},{9,5},{1... | collective-permute-start | bytes 196616 | tf_op jit(solution)/shard_map/ppermute | solution.py:271
  115.5 0.0 collective-permute-done.11.refs_1_
  115.5 1.5 %collective-permute-done.12.refs_2_ = bf16[256,128]{1,0:T(8,128)(2,1)S(1)} collective-permute-done((bf16[256,128]{1,0:T(8,128)(2,1)S(1)}, bf16[256,128]{1,0:T(8,128)(2,1)S(1)}, u32[]{:S(2)}, u32[]{:S(2)}) %collective-permute-start.12) | collective-permute-done | bytes 65568 | tf_op jit(solution)/shard_map/ppermute | solution.py:271
  117.0 1.8 %collective-permute-done.13.refs_3_ = bf16[256,128]{1,0:T(8,128)(2,1)S(1)} collective-permute-done((bf16[256,128]{1,0:T(8,128)(2,1)S(1)}, bf16[256,128]{1,0:T(8,128)(2,1)S(1)}, u32[]{:S(2)}, u32[]{:S(2)}) %collective-permute-start.13) | collective-permute-done | bytes 65568 | tf_op jit(solution)/shard_map/ppermute | solution.py:271
  118.9 0.0 all-to-all-done.3
  118.9 0.9 results.1
  (3 shorter events, 0.0 us)
Async XLA Ops:
  0.6 51.1 %copy-start = (bf16[256,256]{1,0:T(8,128)(2,1)S(1)}, bf16[256,256]{1,0:T(8,128)(2,1)}, u32[]{:S(2)}) copy-start(bf16[256,256]{1,0:T(8,128)(2,1)} %refs_4_.1) | copy-start | bytes 393220
  0.6 51.0 %copy-start.1 = (bf16[256,256]{1,0:T(8,128)(2,1)S(1)}, bf16[256,256]{1,0:T(8,128)(2,1)}, u32[]{:S(2)}) copy-start(bf16[256,256]{1,0:T(8,128)(2,1)} %w_out.1) | copy-start | bytes 393220
  0.7 51.0 %copy-start.2 = (bf16[1,128,256]{2,1,0:T(8,128)(2,1)S(1)}, bf16[1,128,256]{2,1,0:T(8,128)(2,1)}, u32[]{:S(2)}) copy-start(bf16[1,128,256]{2,1,0:T(8,128)(2,1)} %param.9) | copy-start | bytes 196612
  0.7 11.1 %collective-permute-start.2 = (bf16[128,256]{1,0:T(8,128)(2,1)}, bf16[128,256]{1,0:T(8,128)(2,1)S(1)}, u32[]{:S(2)}, u32[]{:S(2)}) collective-permute-start(bf16[128,256]{1,0:T(8,128)(2,1)} %bitcast.20), channel_id=1, source_target_pairs={{0,12},{1,13},{2,14},{3,15},{4,0},{5,1},{6,2},{7,3},{8,4},{9,5},{1... | collective-permute-start | bytes 196616 | tf_op jit(solution)/shard_map/ppermute | solution.py:271
  7.6 7.4 %collective-permute-start.1 = (bf16[128,256]{1,0:T(8,128)(2,1)}, bf16[128,256]{1,0:T(8,128)(2,1)S(1)}, u32[]{:S(2)}, u32[]{:S(2)}) collective-permute-start(bf16[128,256]{1,0:T(8,128)(2,1)} %bitcast.21), channel_id=1, source_target_pairs={{0,8},{1,9},{2,10},{3,11},{4,12},{5,13},{6,14},{7,15},{8,0},{9,1},... | collective-permute-start | bytes 196616 | tf_op jit(solution)/shard_map/ppermute | solution.py:271
  8.6 7.1 %collective-permute-start = (bf16[128,256]{1,0:T(8,128)(2,1)}, bf16[128,256]{1,0:T(8,128)(2,1)S(1)}, u32[]{:S(2)}, u32[]{:S(2)}) collective-permute-start(bf16[128,256]{1,0:T(8,128)(2,1)} %bitcast.22), channel_id=1, source_target_pairs={{0,4},{1,5},{2,6},{3,7},{4,8},{5,9},{6,10},{7,11},{8,12},{9,13},{1... | collective-permute-start | bytes 196616 | tf_op jit(solution)/shard_map/ppermute | solution.py:271
  10.8 0.9 copy-start.3
  15.7 6.3 %collective-permute-start.5 = (bf16[4,128,256]{2,1,0:T(8,128)(2,1)S(1)}, bf16[4,128,256]{2,1,0:T(8,128)(2,1)S(1)}, u32[]{:S(2)}, u32[]{:S(2)}) collective-permute-start(bf16[4,128,256]{2,1,0:T(8,128)(2,1)S(1)} %pad_maximum_fusion.own), channel_id=1, source_target_pairs={{0,3},{1,2},{2,1},{3,0},{4,7},{5,6},{6,5},{7,4},{8,11},{9,10},{10,... | collective-permute-start | bytes 786440 | tf_op jit(solution)/shard_map/ppermute | solution.py:268
  17.8 11.9 %collective-permute-start.4 = (bf16[4,128,256]{2,1,0:T(8,128)(2,1)S(1)}, bf16[4,128,256]{2,1,0:T(8,128)(2,1)S(1)}, u32[]{:S(2)}, u32[]{:S(2)}) collective-permute-start(bf16[4,128,256]{2,1,0:T(8,128)(2,1)S(1)} %pad_maximum_fusion.own), channel_id=1, source_target_pairs={{0,1},{1,0},{2,3},{3,2},{4,5},{5,4},{6,7},{7,6},{8,9},{9,8},{10,11... | collective-permute-start | bytes 786440 | tf_op jit(solution)/shard_map/ppermute | solution.py:268
  18.0 11.7 %collective-permute-start.3 = (bf16[4,128,256]{2,1,0:T(8,128)(2,1)S(1)}, bf16[4,128,256]{2,1,0:T(8,128)(2,1)S(1)}, u32[]{:S(2)}, u32[]{:S(2)}) collective-permute-start(bf16[4,128,256]{2,1,0:T(8,128)(2,1)S(1)} %pad_maximum_fusion.own), channel_id=1, source_target_pairs={{0,2},{1,3},{2,0},{3,1},{4,6},{5,7},{6,4},{7,5},{8,10},{9,11},{10,... | collective-permute-start | bytes 786440 | tf_op jit(solution)/shard_map/ppermute | solution.py:268
  32.2 4.0 %collective-permute-start.6 = (bf16[8,128,256]{2,1,0:T(8,128)(2,1)S(1)}, bf16[8,128,256]{2,1,0:T(8,128)(2,1)S(1)}, u32[]{:S(2)}, u32[]{:S(2)}) collective-permute-start(bf16[8,128,256]{2,1,0:T(8,128)(2,1)S(1)} %get-tuple-element.22), channel_id=1, source_target_pairs={{0,16},{16,0},{32,48},{48,32},{64,80},{80,64},{96,112},{112,96},{1... | collective-permute-start | bytes 1572872 | tf_op jit(solution)/shard_map/ppermute | solution.py:309
  68.3 4.6 %collective-permute-start.7 = (bf16[8,384,128]{2,1,0:T(8,128)(2,1)S(1)}, bf16[8,384,128]{2,1,0:T(8,128)(2,1)S(1)}, u32[]{:S(2)}, u32[]{:S(2)}) collective-permute-start(bf16[8,384,128]{2,1,0:T(8,128)(2,1)S(1)} %all_to_all.21.held), channel_id=1, source_target_pairs={{0,16},{16,0},{32,48},{48,32},{64,80},{80,64},{96,112},{112,96},{1... | collective-permute-start | bytes 2359304 | tf_op jit(solution)/shard_map/ppermute | solution.py:323
  73.7 29.2 %all-to-all-start.2 = ((bf16[16,64,128]{2,1,0:T(8,128)(2,1)}), bf16[16,64,128]{2,1,0:T(8,128)(2,1)S(1)}, u32[]{:S(2)}, u32[]{:S(2)}) async-start(bf16[16,64,128]{2,1,0:T(8,128)(2,1)} %weights_chunk.1), calls=%async_computation.2 | async-start | bytes 524288 | tf_op jit(solution)/shard_map/all_to_all | solution.py:333
  84.7 10.5 %collective-permute-start.8 = (bf16[4,256,128]{2,1,0:T(8,128)(2,1)S(1)}, bf16[4,256,128]{2,1,0:T(8,128)(2,1)S(1)}, u32[]{:S(2)}, u32[]{:S(2)}) collective-permute-start(bf16[4,256,128]{2,1,0:T(8,128)(2,1)S(1)} %get-tuple-element.24), channel_id=1, source_target_pairs={{0,2},{1,3},{2,0},{3,1},{4,6},{5,7},{6,4},{7,5},{8,10},{9,11},{10,... | collective-permute-start | bytes 786440 | tf_op jit(solution)/shard_map/ppermute | solution.py:268
  86.2 15.1 %collective-permute-start.9 = (bf16[4,256,128]{2,1,0:T(8,128)(2,1)S(1)}, bf16[4,256,128]{2,1,0:T(8,128)(2,1)S(1)}, u32[]{:S(2)}, u32[]{:S(2)}) collective-permute-start(bf16[4,256,128]{2,1,0:T(8,128)(2,1)S(1)} %get-tuple-element.25), channel_id=1, source_target_pairs={{0,1},{1,0},{2,3},{3,2},{4,5},{5,4},{6,7},{7,6},{8,9},{9,8},{10,11... | collective-permute-start | bytes 786440 | tf_op jit(solution)/shard_map/ppermute | solution.py:268
  89.1 13.6 %collective-permute-start.10 = (bf16[4,256,128]{2,1,0:T(8,128)(2,1)S(1)}, bf16[4,256,128]{2,1,0:T(8,128)(2,1)S(1)}, u32[]{:S(2)}, u32[]{:S(2)}) collective-permute-start(bf16[4,256,128]{2,1,0:T(8,128)(2,1)S(1)} %get-tuple-element.26), channel_id=1, source_target_pairs={{0,3},{1,2},{2,1},{3,0},{4,7},{5,6},{6,5},{7,4},{8,11},{9,10},{10,... | collective-permute-start | bytes 786440 | tf_op jit(solution)/shard_map/ppermute | solution.py:268
  103.8 15.2 %all-to-all-start.3 = ((f32[16,64,128]{2,1,0:T(8,128)}), f32[16,64,128]{2,1,0:T(8,128)S(1)}, u32[]{:S(2)}, u32[]{:S(2)}) async-start(f32[16,64,128]{2,1,0:T(8,128)} %weights_sum.1), calls=%async_computation.3 | async-start | bytes 1048576 | tf_op jit(solution)/shard_map/all_to_all | solution.py:367
  107.8 7.8 %collective-permute-start.11 = (bf16[256,128]{1,0:T(8,128)(2,1)S(1)}, bf16[256,128]{1,0:T(8,128)(2,1)S(1)}, u32[]{:S(2)}, u32[]{:S(2)}) collective-permute-start(bf16[256,128]{1,0:T(8,128)(2,1)S(1)} %get-tuple-element.32), channel_id=1, source_target_pairs={{0,4},{1,5},{2,6},{3,7},{4,8},{5,9},{6,10},{7,11},{8,12},{9,13},{1... | collective-permute-start | bytes 196616 | tf_op jit(solution)/shard_map/ppermute | solution.py:271
  109.9 7.2 %collective-permute-start.12 = (bf16[256,128]{1,0:T(8,128)(2,1)S(1)}, bf16[256,128]{1,0:T(8,128)(2,1)S(1)}, u32[]{:S(2)}, u32[]{:S(2)}) collective-permute-start(bf16[256,128]{1,0:T(8,128)(2,1)S(1)} %get-tuple-element.33), channel_id=1, source_target_pairs={{0,8},{1,9},{2,10},{3,11},{4,12},{5,13},{6,14},{7,15},{8,0},{9,1},... | collective-permute-start | bytes 196616 | tf_op jit(solution)/shard_map/ppermute | solution.py:271
  112.3 6.5 %collective-permute-start.13 = (bf16[256,128]{1,0:T(8,128)(2,1)S(1)}, bf16[256,128]{1,0:T(8,128)(2,1)S(1)}, u32[]{:S(2)}, u32[]{:S(2)}) collective-permute-start(bf16[256,128]{1,0:T(8,128)(2,1)S(1)} %get-tuple-element.34), channel_id=1, source_target_pairs={{0,12},{1,13},{2,14},{3,15},{4,0},{5,1},{6,2},{7,3},{8,4},{9,5},{1... | collective-permute-start | bytes 196616 | tf_op jit(solution)/shard_map/ppermute | solution.py:271

commit v9 on v6

--- a/solution.py
+++ b/solution.py
@@ -121,7 +121,7 @@
 
 
 def backward_kernel(
-    numbers, held, other, tiles, own, pair, beside, across, weights, grads, acc, ring, sems
+    numbers, held, other, tiles, own, pair, beside, across, grads, acc, ring, sems
 ):
     live, core, column, parity, height, emit_block, recv_block = unpack(numbers, tiles.shape[0])
     width, lanes = acc.shape[1], held.shape[2]
@@ -145,14 +145,6 @@
         return jnp.dot(grads[recv_block(slot)], tile, preferred_element_type=f32)
 
     sweep(live, tiles, ring, sems, prepare, product, emit_block, acc)
-    chunk = weights.shape[1]
-    mine = pl.ds(pl.multiple_of(width + core * chunk, chunk), chunk)
-    summed = held[0, mine, :].astype(f32) + other[0, mine, :].astype(f32)
-    for block in range(1, held.shape[0]):
-        summed += held[block, mine, :].astype(f32) + other[block, mine, :].astype(f32)
-    for piece in range(weights.shape[0]):
-        weights[piece] = summed.astype(bf16)
-
     def hand_out(near):
         for out, side, odd in (
             (own, near, parity),
@@ -174,15 +166,31 @@
         hand_out(1)
 
 
+def copy_kernel(source, out):
+    out[...] = source[...]
+
+
+def chunk_kernel(held, other, second_core, out):
+    chunk = out.shape[1]
+    width = held.shape[1] - 2 * chunk
+
+    def summed(rows):
+        total = held[0, rows, :].astype(f32) + other[0, rows, :].astype(f32)
+        for block in range(1, held.shape[0]):
+            total += held[block, rows, :].astype(f32) + other[block, rows, :].astype(f32)
+        return total
+
+    first, second = summed(slice(width, width + chunk)), summed(slice(width + chunk, None))
+    mine = jnp.where(second_core[0:1, :] > 0.5, second, first).astype(bf16)
+    for piece in range(out.shape[0]):
+        out[piece] = mine
+
+
 def quad_kernel(own, pair, beside, across, *outs):
     for step, out in enumerate(outs):
         near = own[step].astype(f32) + pair[step].astype(f32)
         far = beside[step].astype(f32) + across[step].astype(f32)
         out[...] = (near + far).astype(bf16)
-
-
-def copy_kernel(source, out):
-    out[...] = source[...]
 
 
 def weights_kernel(terms, total):
@@ -247,6 +255,8 @@
         pltpu.SemaphoreType.DMA((ring_depth,)),
     ]
 
+    second_core = jnp.broadcast_to(core.astype(f32), (8, lanes))
+    rated_long = pl.CostEstimate(flops=2**37, bytes_accessed=2**24, transcendentals=0)
     sweep_cost = pl.CostEstimate(
         flops=2 * values.size * width, bytes_accessed=2 * values.size, transcendentals=0
     )
@@ -309,12 +319,11 @@
     held = lax.all_to_all(payload, "emit", 0, 0, tiled=True, axis_index_groups=same_core)
     other = lax.ppermute(held, "emit", swap)
 
-    own, pair, beside, across, weights = pl.pallas_call(
+    own, pair, beside, across = pl.pallas_call(
         backward_kernel,
-        out_shape=(struct((steps, width, lanes), bf16),) * 4
-        + (struct((recv_size, chunk // 2, lanes), bf16),),
+        out_shape=(struct((steps, width, lanes), bf16),) * 4,
         in_specs=in_smem(1) + in_vmem(2) + [in_hbm],
-        out_specs=tuple(in_vmem(5)),
+        out_specs=tuple(in_vmem(4)),
         scratch_shapes=[
             pltpu.VMEM((recv_blocks, width, tile_dim), bf16),
             pltpu.VMEM((emit_blocks + 1, width, tile_dim), f32),
@@ -324,18 +333,27 @@
         cost_estimate=sweep_cost,
         name="backward_sweep",
     )(numbers, held, other, values)
-    pair, weights = lax.optimization_barrier((to_quad(pair, 2), weights))
+    own, held, other = lax.optimization_barrier((own, held, other))
+    weights = pl.pallas_call(
+        chunk_kernel,
+        out_shape=struct((recv_size, chunk // 2, lanes), bf16),
+        in_specs=in_vmem(3),
+        out_specs=in_vmem(1)[0],
+        compiler_params=limits(8),
+        name="weights_chunk",
+    )(held, other, second_core)
     chunks = lax.all_to_all(weights, "recv", 0, 0, tiled=True)
+
     terms = pl.pallas_call(
         quad_kernel,
         out_shape=(struct((width, lanes), bf16),) * steps,
         in_specs=in_vmem(4),
         out_specs=tuple(in_vmem(steps)),
         compiler_params=limits(8),
+        cost_estimate=rated_long,
         name="quad_sum",
-    )(own, pair, to_quad(beside, 1), to_quad(across, 3))
-    terms = [terms[0]] + [along_z(terms[step], step) for step in range(1, steps)]
-    chunks, terms[1] = lax.optimization_barrier((chunks, terms[1]))
+    )(own, to_quad(pair, 2), to_quad(beside, 1), to_quad(across, 3))
+    chunks, _ = lax.optimization_barrier((chunks, terms[0]))
 
     total = pl.pallas_call(
         weights_kernel,
@@ -346,12 +364,14 @@
         name="weights_sum",
     )(chunks)
     gathered = lax.all_to_all(total, "emit", 0, 0, tiled=True).reshape(4, width, lanes)
+    terms = [terms[0]] + [along_z(terms[step], step) for step in range(1, steps)]
     grad_features = pl.pallas_call(
         features_kernel,
         out_shape=struct((facet_rows, width), bf16),
         in_specs=in_vmem(steps + 1),
         out_specs=in_vmem(1)[0],
         compiler_params=limits(8),
+        cost_estimate=rated_long,
         name="features_grad",
     )(*terms, w_msg)[None]
     grad_w_out = jnp.concatenate([gathered[0], gathered[1]], axis=1)

time: 136 us -> 124 us (0.912)
  waiting for transfers between devices: 45.5 us -> 32.1 us
  Pallas kernels: 8.16 us -> 13 us
  blocking collectives: 34.1 us -> 32.6 us
    ppermute x6, waiting for transfers between devices: 27.2 us -> 14.4 us  [to_quad(): lax.ppermute(array, 'recv', [(member, member ^ bits) for member in range(...]
    ppermute x6, waiting for transfers between devices: 14.8 us -> 3.95 us  [along_z(): lax.ppermute(array, 'recv', [(member, (member + 4 * step) % recv_size) fo...]
    all_to_all x1, waiting for transfers between devices: 0.01 us -> 10.3 us  [per_device(): lax.all_to_all(total, 'emit', 0, 0, tiled=True).reshape(4, width, lanes)]
    all_to_all x1, starting transfers between devices: 8.85 us -> 12 us  [per_device(): lax.all_to_all(total, 'emit', 0, 0, tiled=True).reshape(4, width, lanes)]
    pallas_call x1, Pallas kernels: 2.46 us -> 4.88 us  [per_device(): pl.pallas_call(forward_kernel, out_shape=(struct((recv_blocks, tile_dim /...]
    pallas_call x1, Pallas kernels: 3.22 us -> 4.86 us  [per_device(): pl.pallas_call(backward_kernel, out_shape=(struct((steps, width, lanes),...]
    all_to_all x1, blocking collectives: 18.7 us -> 17.3 us  [per_device(): lax.all_to_all(pair_sum, 'emit', 0, 0, tiled=True, axis_index_groups=same...]
    all_to_all x1, starting transfers between devices: 6.68 us -> 5.32 us  [per_device(): chunks = lax.all_to_all(weights, 'recv', 0, 0, tiled=True)]
  transfers between devices with their start and end apart: 16 -> 16, of which waited for: 12 -> 8; matrix products, arithmetic and copies ran while one was open for 1% -> 1% of each run, Pallas kernels for 1% -> 2%
where the time goes in v9:
time: 124 us; the launch traced here: 125 us
  starting transfers between devices  43.4 us (35%)
  blocking collectives  32.6 us (26%)
  waiting for transfers between devices  32.1 us (26%)
  Pallas kernels  13 us (10%)
  local copies, waits for them, and re-layouts  1.68 us (1%)
  between operations  1.42 us (1%)
    ppermute x6, starting transfers between devices, along_z(): lax.ppermute(array, 'recv', [(member, (member + 4 * step) % recv_size) fo...  17.5 us
    all_to_all x1, blocking collectives, per_device(): lax.all_to_all(pair_sum, 'emit', 0, 0, tiled=True, axis_index_groups=same...  17.3 us
    all_to_all x1, blocking collectives, per_device(): lax.all_to_all(payload, 'emit', 0, 0, tiled=True, axis_index_groups=same_...  15.3 us
    ppermute x6, waiting for transfers between devices, to_quad(): lax.ppermute(array, 'recv', [(member, member ^ bits) for member in range(...  14.4 us
    all_to_all x1, starting transfers between devices, per_device(): lax.all_to_all(total, 'emit', 0, 0, tiled=True).reshape(4, width, lanes)  12 us
    all_to_all x1, waiting for transfers between devices, per_device(): lax.all_to_all(total, 'emit', 0, 0, tiled=True).reshape(4, width, lanes)  10.3 us
    ppermute x6, starting transfers between devices, to_quad(): lax.ppermute(array, 'recv', [(member, member ^ bits) for member in range(...  5.46 us
    all_to_all x1, starting transfers between devices, per_device(): chunks = lax.all_to_all(weights, 'recv', 0, 0, tiled=True)  5.32 us
  transfers between devices with their start and end apart: 16, of which 8 were waited for; matrix products, arithmetic and copies ran while one was open for 1% of the time, Pallas kernels for 2%

profile of v9, /device:TPU:1, one launch (start us, length us, event | category | flops | bytes accessed | tf_op | source)
XLA Modules:
  0.0 125.2 jit_solution(11152275320625119847)
XLA Ops:
  0.6 0.0 copy-start.1
  0.6 0.0 copy-start
  0.7 0.0 copy-start.2
  0.7 6.9 %collective-permute-start.2 = (bf16[128,256]{1,0:T(8,128)(2,1)}, bf16[128,256]{1,0:T(8,128)(2,1)S(1)}, u32[]{:S(2)}, u32[]{:S(2)}) collective-permute-start(bf16[128,256]{1,0:T(8,128)(2,1)} %bitcast.22), channel_id=1, source_target_pairs={{0,12},{1,13},{2,14},{3,15},{4,0},{5,1},{6,2},{7,3},{8,4},{9,5},{1... | collective-permute-start | bytes 196616 | tf_op jit(solution)/shard_map/ppermute | solution.py:268
  7.6 1.0 collective-permute-start.1
  8.6 2.3 %collective-permute-start = (bf16[128,256]{1,0:T(8,128)(2,1)}, bf16[128,256]{1,0:T(8,128)(2,1)S(1)}, u32[]{:S(2)}, u32[]{:S(2)}) collective-permute-start(bf16[128,256]{1,0:T(8,128)(2,1)} %bitcast.24), channel_id=1, source_target_pairs={{0,4},{1,5},{2,6},{3,7},{4,8},{5,9},{6,10},{7,11},{8,12},{9,13},{1... | collective-permute-start | bytes 196616 | tf_op jit(solution)/shard_map/ppermute | solution.py:268
  10.8 0.0 copy-start.3
  10.8 0.9 copy-done.3
  11.7 0.0 collective-permute-done.2
  11.7 3.3 %collective-permute-done.1 = bf16[128,256]{1,0:T(8,128)(2,1)S(1)} collective-permute-done((bf16[128,256]{1,0:T(8,128)(2,1)}, bf16[128,256]{1,0:T(8,128)(2,1)S(1)}, u32[]{:S(2)}, u32[]{:S(2)}) %collective-permute-start.1) | collective-permute-done | bytes 65568 | tf_op jit(solution)/shard_map/ppermute | solution.py:268
  15.0 0.6 collective-permute-done
  15.7 2.1 %collective-permute-start.5 = (bf16[4,128,256]{2,1,0:T(8,128)(2,1)S(1)}, bf16[4,128,256]{2,1,0:T(8,128)(2,1)S(1)}, u32[]{:S(2)}, u32[]{:S(2)}) collective-permute-start(bf16[4,128,256]{2,1,0:T(8,128)(2,1)S(1)} %pad_maximum_fusion.own), channel_id=1, source_target_pairs={{0,3},{1,2},{2,1},{3,0},{4,7},{5,6},{6,5},{7,4},{8,11},{9,10},{10,... | collective-permute-start | bytes 786440 | tf_op jit(solution)/shard_map/ppermute | solution.py:265
  17.8 0.2 collective-permute-start.4
  18.0 0.4 collective-permute-start.3
  19.1 0.8 concatenate.9.numbers
  19.9 2.2 %collective-permute-done.5.across = bf16[4,128,256]{2,1,0:T(8,128)(2,1)S(1)} collective-permute-done((bf16[4,128,256]{2,1,0:T(8,128)(2,1)S(1)}, bf16[4,128,256]{2,1,0:T(8,128)(2,1)S(1)}, u32[]{:S(2)}, u32[]{:S(2)}) %collective-permute-start.5) | collective-permute-done | bytes 262176 | tf_op jit(solution)/shard_map/ppermute | solution.py:265
  22.0 7.7 %collective-permute-done.4.beside = bf16[4,128,256]{2,1,0:T(8,128)(2,1)S(1)} collective-permute-done((bf16[4,128,256]{2,1,0:T(8,128)(2,1)S(1)}, bf16[4,128,256]{2,1,0:T(8,128)(2,1)S(1)}, u32[]{:S(2)}, u32[]{:S(2)}) %collective-permute-start.4) | collective-permute-done | bytes 262176 | tf_op jit(solution)/shard_map/ppermute | solution.py:265
  29.8 0.0 collective-permute-done.3.pair
  29.8 4.9 %forward_sweep.1 = (f32[8,128,256]{2,1,0:T(8,128)S(1)}, bf16[8,128,256]{2,1,0:T(8,128)(2,1)S(1)}) custom-call(s32[133]{0:T(256)S(1)} %concatenate.9.numbers, bf16[4,128,256]{2,1,0:T(8,128)(2,1)S(1)} %pad_maximum_fusion.own, bf16[4,128,256]{2,1,0:T(8,128)(2,1)S(1)} %collective-permute-done.3.pair, bf16[4,128,256]{2,1,0:T(8,128)(2,1)S(1)} %collective-permute-done.4.beside, ...), custom_call_target="tpu_custom_call" | custom-call | flops 2147483648 | bytes 8388608 | tf_op jit(solution)/shard_map/forward_sweep/pallas_call | solution.py:282
  34.6 0.6 collective-permute-start.6
  35.2 1.5 %collective-permute-done.6 = bf16[8,128,256]{2,1,0:T(8,128)(2,1)S(1)} collective-permute-done((bf16[8,128,256]{2,1,0:T(8,128)(2,1)S(1)}, bf16[8,128,256]{2,1,0:T(8,128)(2,1)S(1)}, u32[]{:S(2)}, u32[]{:S(2)}) %collective-permute-start.6) | collective-permute-done | bytes 524320 | tf_op jit(solution)/shard_map/ppermute | solution.py:306
  36.7 0.2 add_convert_fusion
  36.9 17.3 %all_to_all.20.terms = bf16[8,128,256]{2,1,0:T(8,128)(2,1)S(1)} all-to-all(bf16[8,128,256]{2,1,0:T(8,128)(2,1)S(1)} %add_convert_fusion), channel_id=1, replica_groups={{0,32,64,96,128,160,192,224},{16,48,80,112,144,176,208,240},{1,33,65,97..., dimensions={0} | all-to-all | bytes 1048576 | tf_op jit(solution)/shard_map/all_to_all | solution.py:308
  54.2 0.0 copy-done.1
  54.2 0.0 copy-done
  54.2 0.0 copy-done.2
  54.2 0.6 middle.1
  54.8 15.3 %all_to_all.21.held = bf16[8,384,128]{2,1,0:T(8,128)(2,1)S(1)} all-to-all(bf16[8,384,128]{2,1,0:T(8,128)(2,1)S(1)} %middle.1), channel_id=1, replica_groups={{0,32,64,96,128,160,192,224},{16,48,80,112,144,176,208,240},{1,33,65,97..., dimensions={0} | all-to-all | bytes 1572864 | tf_op jit(solution)/shard_map/all_to_all | solution.py:319
  70.1 2.6 %collective-permute-start.7 = (bf16[8,384,128]{2,1,0:T(8,128)(2,1)S(1)}, bf16[8,384,128]{2,1,0:T(8,128)(2,1)S(1)}, u32[]{:S(2)}, u32[]{:S(2)}) collective-permute-start(bf16[8,384,128]{2,1,0:T(8,128)(2,1)S(1)} %all_to_all.21.held), channel_id=1, source_target_pairs={{0,16},{16,0},{32,48},{48,32},{64,80},{80,64},{96,112},{112,96},{1... | collective-permute-start | bytes 2359304 | tf_op jit(solution)/shard_map/ppermute | solution.py:320
  72.8 1.9 %collective-permute-done.7.other = bf16[8,384,128]{2,1,0:T(8,128)(2,1)S(1)} collective-permute-done((bf16[8,384,128]{2,1,0:T(8,128)(2,1)S(1)}, bf16[8,384,128]{2,1,0:T(8,128)(2,1)S(1)}, u32[]{:S(2)}, u32[]{:S(2)}) %collective-permute-start.7) | collective-permute-done | bytes 786464 | tf_op jit(solution)/shard_map/ppermute | solution.py:320
  74.7 4.9 %backward_sweep.1 = (bf16[4,256,128]{2,1,0:T(8,128)(2,1)S(1)}, bf16[4,256,128]{2,1,0:T(8,128)(2,1)S(1)}, bf16[4,256,128]{2,1,0:T(8,128)(2,1)S(1)}, bf16[4,256,128]{2,1,0:T(8,128)(2,1)S(1)}) custom-call(s32[133]{0:T(256)S(1)} %concatenate.9.numbers, bf16[8,384,128]{2,1,0:T(8,128)(2,1)S(1)} %all_to_all.21.held, ...), custom_call_target="tpu_custom_call" | custom-call | flops 2147483648 | bytes 8388608 | tf_op jit(solution)/shard_map/backward_sweep/pallas_call | solution.py:322
  79.5 0.1 collective-permute-start.8
  79.6 0.1 collective-permute-start.9
  79.7 2.5 %collective-permute-start.10 = (bf16[4,256,128]{2,1,0:T(8,128)(2,1)S(1)}, bf16[4,256,128]{2,1,0:T(8,128)(2,1)S(1)}, u32[]{:S(2)}, u32[]{:S(2)}) collective-permute-start(bf16[4,256,128]{2,1,0:T(8,128)(2,1)S(1)} %get-tuple-element.23), channel_id=1, source_target_pairs={{0,3},{1,2},{2,1},{3,0},{4,7},{5,6},{6,5},{7,4},{8,11},{9,10},{10,... | collective-permute-start | bytes 786440 | tf_op jit(solution)/shard_map/ppermute | solution.py:265
  82.3 0.8 weights_chunk.1
  83.1 5.3 %all-to-all-start.2 = ((bf16[16,64,128]{2,1,0:T(8,128)(2,1)}), bf16[16,64,128]{2,1,0:T(8,128)(2,1)S(1)}, u32[]{:S(2)}, u32[]{:S(2)}) async-start(bf16[16,64,128]{2,1,0:T(8,128)(2,1)} %weights_chunk.1), calls=%async_computation.2 | async-start | bytes 524288 | tf_op jit(solution)/shard_map/all_to_all | solution.py:345
  88.4 0.0 collective-permute-done.8.pair
  88.4 4.5 %collective-permute-done.9.beside = bf16[4,256,128]{2,1,0:T(8,128)(2,1)S(1)} collective-permute-done((bf16[4,256,128]{2,1,0:T(8,128)(2,1)S(1)}, bf16[4,256,128]{2,1,0:T(8,128)(2,1)S(1)}, u32[]{:S(2)}, u32[]{:S(2)}) %collective-permute-start.9) | collective-permute-done | bytes 262176 | tf_op jit(solution)/shard_map/ppermute | solution.py:265
  92.9 0.0 collective-permute-done.10.across
  92.9 0.1 quad_sum.1
  93.0 0.9 collective-permute-start.11
  94.0 4.9 %collective-permute-start.12 = (bf16[256,128]{1,0:T(8,128)(2,1)S(1)}, bf16[256,128]{1,0:T(8,128)(2,1)S(1)}, u32[]{:S(2)}, u32[]{:S(2)}) collective-permute-start(bf16[256,128]{1,0:T(8,128)(2,1)S(1)} %get-tuple-element.26), channel_id=1, source_target_pairs={{0,8},{1,9},{2,10},{3,11},{4,12},{5,13},{6,14},{7,15},{8,0},{9,1},... | collective-permute-start | bytes 196616 | tf_op jit(solution)/shard_map/ppermute | solution.py:268
  98.8 1.5 %collective-permute-start.13 = (bf16[256,128]{1,0:T(8,128)(2,1)S(1)}, bf16[256,128]{1,0:T(8,128)(2,1)S(1)}, u32[]{:S(2)}, u32[]{:S(2)}) collective-permute-start(bf16[256,128]{1,0:T(8,128)(2,1)S(1)} %get-tuple-element.27), channel_id=1, source_target_pairs={{0,12},{1,13},{2,14},{3,15},{4,0},{5,1},{6,2},{7,3},{8,4},{9,5},{1... | collective-permute-start | bytes 196616 | tf_op jit(solution)/shard_map/ppermute | solution.py:268
  100.4 0.0 all-to-all-done.2.terms
  100.4 0.9 weights_sum.1
  101.2 12.0 %all-to-all-start.3 = ((f32[16,64,128]{2,1,0:T(8,128)}), f32[16,64,128]{2,1,0:T(8,128)S(1)}, u32[]{:S(2)}, u32[]{:S(2)}) async-start(f32[16,64,128]{2,1,0:T(8,128)} %weights_sum.1), calls=%async_computation.3 | async-start | bytes 1048576 | tf_op jit(solution)/shard_map/all_to_all | solution.py:366
  113.2 0.0 collective-permute-done.11.refs_1_
  113.2 0.0 collective-permute-done.12.refs_2_
  113.2 0.0 collective-permute-done.13.refs_3_
  113.3 0.9 features_grad.1
  114.1 10.3 %all-to-all-done.3 = f32[16,64,128]{2,1,0:T(8,128)S(1)} async-done(((f32[16,64,128]{2,1,0:T(8,128)}), f32[16,64,128]{2,1,0:T(8,128)S(1)}, u32[]{:S(2)}, u32[]{:S(2)}) %all-to-all-start.3) | async-done | bytes 524320 | tf_op jit(solution)/shard_map/all_to_all | solution.py:366
  124.4 0.8 pad_maximum_fusion.1
  (4 shorter events, 0.1 us)
Async XLA Ops:
  0.6 53.6 %copy-start.1 = (bf16[256,256]{1,0:T(8,128)(2,1)S(1)}, bf16[256,256]{1,0:T(8,128)(2,1)}, u32[]{:S(2)}) copy-start(bf16[256,256]{1,0:T(8,128)(2,1)} %refs_4_.1) | copy-start | bytes 393220
  0.6 53.5 %copy-start = (bf16[256,256]{1,0:T(8,128)(2,1)S(1)}, bf16[256,256]{1,0:T(8,128)(2,1)}, u32[]{:S(2)}) copy-start(bf16[256,256]{1,0:T(8,128)(2,1)} %w_out.1) | copy-start | bytes 393220
  0.7 53.5 %copy-start.2 = (bf16[1,128,256]{2,1,0:T(8,128)(2,1)S(1)}, bf16[1,128,256]{2,1,0:T(8,128)(2,1)}, u32[]{:S(2)}) copy-start(bf16[1,128,256]{2,1,0:T(8,128)(2,1)} %param.9) | copy-start | bytes 196612
  0.7 11.1 %collective-permute-start.2 = (bf16[128,256]{1,0:T(8,128)(2,1)}, bf16[128,256]{1,0:T(8,128)(2,1)S(1)}, u32[]{:S(2)}, u32[]{:S(2)}) collective-permute-start(bf16[128,256]{1,0:T(8,128)(2,1)} %bitcast.22), channel_id=1, source_target_pairs={{0,12},{1,13},{2,14},{3,15},{4,0},{5,1},{6,2},{7,3},{8,4},{9,5},{1... | collective-permute-start | bytes 196616 | tf_op jit(solution)/shard_map/ppermute | solution.py:268
  7.6 7.4 %collective-permute-start.1 = (bf16[128,256]{1,0:T(8,128)(2,1)}, bf16[128,256]{1,0:T(8,128)(2,1)S(1)}, u32[]{:S(2)}, u32[]{:S(2)}) collective-permute-start(bf16[128,256]{1,0:T(8,128)(2,1)} %bitcast.23), channel_id=1, source_target_pairs={{0,8},{1,9},{2,10},{3,11},{4,12},{5,13},{6,14},{7,15},{8,0},{9,1},... | collective-permute-start | bytes 196616 | tf_op jit(solution)/shard_map/ppermute | solution.py:268
  8.6 7.1 %collective-permute-start = (bf16[128,256]{1,0:T(8,128)(2,1)}, bf16[128,256]{1,0:T(8,128)(2,1)S(1)}, u32[]{:S(2)}, u32[]{:S(2)}) collective-permute-start(bf16[128,256]{1,0:T(8,128)(2,1)} %bitcast.24), channel_id=1, source_target_pairs={{0,4},{1,5},{2,6},{3,7},{4,8},{5,9},{6,10},{7,11},{8,12},{9,13},{1... | collective-permute-start | bytes 196616 | tf_op jit(solution)/shard_map/ppermute | solution.py:268
  10.8 0.9 copy-start.3
  15.7 6.3 %collective-permute-start.5 = (bf16[4,128,256]{2,1,0:T(8,128)(2,1)S(1)}, bf16[4,128,256]{2,1,0:T(8,128)(2,1)S(1)}, u32[]{:S(2)}, u32[]{:S(2)}) collective-permute-start(bf16[4,128,256]{2,1,0:T(8,128)(2,1)S(1)} %pad_maximum_fusion.own), channel_id=1, source_target_pairs={{0,3},{1,2},{2,1},{3,0},{4,7},{5,6},{6,5},{7,4},{8,11},{9,10},{10,... | collective-permute-start | bytes 786440 | tf_op jit(solution)/shard_map/ppermute | solution.py:265
  17.8 11.9 %collective-permute-start.4 = (bf16[4,128,256]{2,1,0:T(8,128)(2,1)S(1)}, bf16[4,128,256]{2,1,0:T(8,128)(2,1)S(1)}, u32[]{:S(2)}, u32[]{:S(2)}) collective-permute-start(bf16[4,128,256]{2,1,0:T(8,128)(2,1)S(1)} %pad_maximum_fusion.own), channel_id=1, source_target_pairs={{0,1},{1,0},{2,3},{3,2},{4,5},{5,4},{6,7},{7,6},{8,9},{9,8},{10,11... | collective-permute-start | bytes 786440 | tf_op jit(solution)/shard_map/ppermute | solution.py:265
  18.0 11.7 %collective-permute-start.3 = (bf16[4,128,256]{2,1,0:T(8,128)(2,1)S(1)}, bf16[4,128,256]{2,1,0:T(8,128)(2,1)S(1)}, u32[]{:S(2)}, u32[]{:S(2)}) collective-permute-start(bf16[4,128,256]{2,1,0:T(8,128)(2,1)S(1)} %pad_maximum_fusion.own), channel_id=1, source_target_pairs={{0,2},{1,3},{2,0},{3,1},{4,6},{5,7},{6,4},{7,5},{8,10},{9,11},{10,... | collective-permute-start | bytes 786440 | tf_op jit(solution)/shard_map/ppermute | solution.py:265
  34.6 2.1 %collective-permute-start.6 = (bf16[8,128,256]{2,1,0:T(8,128)(2,1)S(1)}, bf16[8,128,256]{2,1,0:T(8,128)(2,1)S(1)}, u32[]{:S(2)}, u32[]{:S(2)}) collective-permute-start(bf16[8,128,256]{2,1,0:T(8,128)(2,1)S(1)} %get-tuple-element.18), channel_id=1, source_target_pairs={{0,16},{16,0},{32,48},{48,32},{64,80},{80,64},{96,112},{112,96},{1... | collective-permute-start | bytes 1572872 | tf_op jit(solution)/shard_map/ppermute | solution.py:306
  70.1 4.5 %collective-permute-start.7 = (bf16[8,384,128]{2,1,0:T(8,128)(2,1)S(1)}, bf16[8,384,128]{2,1,0:T(8,128)(2,1)S(1)}, u32[]{:S(2)}, u32[]{:S(2)}) collective-permute-start(bf16[8,384,128]{2,1,0:T(8,128)(2,1)S(1)} %all_to_all.21.held), channel_id=1, source_target_pairs={{0,16},{16,0},{32,48},{48,32},{64,80},{80,64},{96,112},{112,96},{1... | collective-permute-start | bytes 2359304 | tf_op jit(solution)/shard_map/ppermute | solution.py:320
  79.5 8.9 %collective-permute-start.8 = (bf16[4,256,128]{2,1,0:T(8,128)(2,1)S(1)}, bf16[4,256,128]{2,1,0:T(8,128)(2,1)S(1)}, u32[]{:S(2)}, u32[]{:S(2)}) collective-permute-start(bf16[4,256,128]{2,1,0:T(8,128)(2,1)S(1)} %get-tuple-element.21), channel_id=1, source_target_pairs={{0,2},{1,3},{2,0},{3,1},{4,6},{5,7},{6,4},{7,5},{8,10},{9,11},{10,... | collective-permute-start | bytes 786440 | tf_op jit(solution)/shard_map/ppermute | solution.py:265
  79.6 13.3 %collective-permute-start.9 = (bf16[4,256,128]{2,1,0:T(8,128)(2,1)S(1)}, bf16[4,256,128]{2,1,0:T(8,128)(2,1)S(1)}, u32[]{:S(2)}, u32[]{:S(2)}) collective-permute-start(bf16[4,256,128]{2,1,0:T(8,128)(2,1)S(1)} %get-tuple-element.22), channel_id=1, source_target_pairs={{0,1},{1,0},{2,3},{3,2},{4,5},{5,4},{6,7},{7,6},{8,9},{9,8},{10,11... | collective-permute-start | bytes 786440 | tf_op jit(solution)/shard_map/ppermute | solution.py:265
  79.7 13.2 %collective-permute-start.10 = (bf16[4,256,128]{2,1,0:T(8,128)(2,1)S(1)}, bf16[4,256,128]{2,1,0:T(8,128)(2,1)S(1)}, u32[]{:S(2)}, u32[]{:S(2)}) collective-permute-start(bf16[4,256,128]{2,1,0:T(8,128)(2,1)S(1)} %get-tuple-element.23), channel_id=1, source_target_pairs={{0,3},{1,2},{2,1},{3,0},{4,7},{5,6},{6,5},{7,4},{8,11},{9,10},{10,... | collective-permute-start | bytes 786440 | tf_op jit(solution)/shard_map/ppermute | solution.py:265
  83.1 17.3 %all-to-all-start.2 = ((bf16[16,64,128]{2,1,0:T(8,128)(2,1)}), bf16[16,64,128]{2,1,0:T(8,128)(2,1)S(1)}, u32[]{:S(2)}, u32[]{:S(2)}) async-start(bf16[16,64,128]{2,1,0:T(8,128)(2,1)} %weights_chunk.1), calls=%async_computation.2 | async-start | bytes 524288 | tf_op jit(solution)/shard_map/all_to_all | solution.py:345
  93.0 20.2 %collective-permute-start.11 = (bf16[256,128]{1,0:T(8,128)(2,1)S(1)}, bf16[256,128]{1,0:T(8,128)(2,1)S(1)}, u32[]{:S(2)}, u32[]{:S(2)}) collective-permute-start(bf16[256,128]{1,0:T(8,128)(2,1)S(1)} %get-tuple-element.25), channel_id=1, source_target_pairs={{0,4},{1,5},{2,6},{3,7},{4,8},{5,9},{6,10},{7,11},{8,12},{9,13},{1... | collective-permute-start | bytes 196616 | tf_op jit(solution)/shard_map/ppermute | solution.py:268
  94.0 19.3 %collective-permute-start.12 = (bf16[256,128]{1,0:T(8,128)(2,1)S(1)}, bf16[256,128]{1,0:T(8,128)(2,1)S(1)}, u32[]{:S(2)}, u32[]{:S(2)}) collective-permute-start(bf16[256,128]{1,0:T(8,128)(2,1)S(1)} %get-tuple-element.26), channel_id=1, source_target_pairs={{0,8},{1,9},{2,10},{3,11},{4,12},{5,13},{6,14},{7,15},{8,0},{9,1},... | collective-permute-start | bytes 196616 | tf_op jit(solution)/shard_map/ppermute | solution.py:268
  98.8 14.4 %collective-permute-start.13 = (bf16[256,128]{1,0:T(8,128)(2,1)S(1)}, bf16[256,128]{1,0:T(8,128)(2,1)S(1)}, u32[]{:S(2)}, u32[]{:S(2)}) collective-permute-start(bf16[256,128]{1,0:T(8,128)(2,1)S(1)} %get-tuple-element.27), channel_id=1, source_target_pairs={{0,12},{1,13},{2,14},{3,15},{4,0},{5,1},{6,2},{7,3},{8,4},{9,5},{1... | collective-permute-start | bytes 196616 | tf_op jit(solution)/shard_map/ppermute | solution.py:268
  101.2 23.1 %all-to-all-start.3 = ((f32[16,64,128]{2,1,0:T(8,128)}), f32[16,64,128]{2,1,0:T(8,128)S(1)}, u32[]{:S(2)}, u32[]{:S(2)}) async-start(f32[16,64,128]{2,1,0:T(8,128)} %weights_sum.1), calls=%async_computation.3 | async-start | bytes 1048576 | tf_op jit(solution)/shard_map/all_to_all | solution.py:366

commit v10 on v8

--- a/solution.py
+++ b/solution.py
@@ -260,6 +260,7 @@
     ]
 
     second_core = jnp.broadcast_to(core.astype(f32), (8, lanes))
+    rated_long = pl.CostEstimate(flops=2**37, bytes_accessed=2**24, transcendentals=0)
     sweep_cost = pl.CostEstimate(
         flops=2 * values.size * width, bytes_accessed=2 * values.size, transcendentals=0
     )
@@ -322,16 +323,6 @@
     held = lax.all_to_all(payload, "emit", 0, 0, tiled=True, axis_index_groups=same_core)
     other = lax.ppermute(held, "emit", swap)
 
-    weights = pl.pallas_call(
-        chunk_kernel,
-        out_shape=struct((recv_size, chunk // 2, lanes), bf16),
-        in_specs=in_vmem(3),
-        out_specs=in_vmem(1)[0],
-        compiler_params=limits(8),
-        name="weights_chunk",
-    )(held, other, second_core)
-    chunks = lax.all_to_all(weights, "recv", 0, 0, tiled=True)
-
     own, pair, beside, across = pl.pallas_call(
         backward_kernel,
         out_shape=(struct((steps, width, lanes), bf16),) * 4,
@@ -346,12 +337,24 @@
         cost_estimate=sweep_cost,
         name="backward_sweep",
     )(numbers, held, other, values)
+    own, held, other = lax.optimization_barrier((own, held, other))
+    weights = pl.pallas_call(
+        chunk_kernel,
+        out_shape=struct((recv_size, chunk // 2, lanes), bf16),
+        in_specs=in_vmem(3),
+        out_specs=in_vmem(1)[0],
+        compiler_params=limits(8),
+        name="weights_chunk",
+    )(held, other, second_core)
+    chunks = lax.all_to_all(weights, "recv", 0, 0, tiled=True)
+
     terms = pl.pallas_call(
         quad_kernel,
         out_shape=(struct((width, lanes), bf16),) * steps,
         in_specs=in_vmem(4),
         out_specs=tuple(in_vmem(steps)),
         compiler_params=limits(8),
+        cost_estimate=rated_long,
         name="quad_sum",
     )(own, to_quad(pair, 2), to_quad(beside, 1), to_quad(across, 3))
     chunks, terms = lax.optimization_barrier((chunks, terms))

time: 122 us -> 121 us (level); the launches traced: 120 us -> 121 us
  starting transfers between devices: 43.9 us -> 38.7 us
  waiting for transfers between devices: 33.2 us -> 35.6 us
  blocking collectives: 31.3 us -> 33.4 us
  Pallas kernels: 8.27 us -> 10.2 us
    ppermute x6, waiting for transfers between devices: 22.4 us -> 13.5 us  [to_quad(): lax.ppermute(array, 'recv', [(member, member ^ bits) for member in range(...]
    all_to_all x1, waiting for transfers between devices: 0.01 us -> 7.09 us  [per_device(): chunks = lax.all_to_all(weights, 'recv', 0, 0, tiled=True)]
    ppermute x6, waiting for transfers between devices: 7.28 us -> 11.6 us  [along_z(): lax.ppermute(array, 'recv', [(member, (member + 4 * step) % recv_size) fo...]
    ppermute x6, starting transfers between devices: 18 us -> 14.6 us  [along_z(): lax.ppermute(array, 'recv', [(member, (member + 4 * step) % recv_size) fo...]
    all_to_all x1, starting transfers between devices: 4.01 us -> 6.87 us  [per_device(): lax.all_to_all(total, 'emit', 0, 0, tiled=True).reshape(4, width, lanes)]
    all_to_all x1, blocking collectives: 15.3 us -> 17.4 us  [per_device(): lax.all_to_all(pair_sum, 'emit', 0, 0, tiled=True, axis_index_groups=same...]
    ppermute x6, starting transfers between devices: 8.23 us -> 6.27 us  [to_quad(): lax.ppermute(array, 'recv', [(member, member ^ bits) for member in range(...]
    ppermute x1, starting transfers between devices: 2.49 us -> 0.55 us  [per_device(): arrived = lax.ppermute(sent, 'emit', swap)]
  transfers between devices with their start and end apart: 16 -> 16, of which waited for: 11 -> 11; matrix products, arithmetic and copies ran while one was open for 1% -> 1% of each run, Pallas kernels for 2% -> 1%
where the time goes in v10:
time: 121 us
  starting transfers between devices  38.7 us (32%)
  waiting for transfers between devices  35.6 us (29%)
  blocking collectives  33.4 us (28%)
  Pallas kernels  10.2 us (8%)
  local copies, waits for them, and re-layouts  1.64 us (1%)
  between operations  1.38 us (1%)
    all_to_all x1, blocking collectives, per_device(): lax.all_to_all(pair_sum, 'emit', 0, 0, tiled=True, axis_index_groups=same...  17.4 us
    all_to_all x1, blocking collectives, per_device(): lax.all_to_all(payload, 'emit', 0, 0, tiled=True, axis_index_groups=same_...  16 us
    ppermute x6, starting transfers between devices, along_z(): lax.ppermute(array, 'recv', [(member, (member + 4 * step) % recv_size) fo...  14.6 us
    ppermute x6, waiting for transfers between devices, to_quad(): lax.ppermute(array, 'recv', [(member, member ^ bits) for member in range(...  13.5 us
    ppermute x6, waiting for transfers between devices, along_z(): lax.ppermute(array, 'recv', [(member, (member + 4 * step) % recv_size) fo...  11.6 us
    all_to_all x1, starting transfers between devices, per_device(): chunks = lax.all_to_all(weights, 'recv', 0, 0, tiled=True)  7.66 us
    all_to_all x1, waiting for transfers between devices, per_device(): chunks = lax.all_to_all(weights, 'recv', 0, 0, tiled=True)  7.09 us
    all_to_all x1, starting transfers between devices, per_device(): lax.all_to_all(total, 'emit', 0, 0, tiled=True).reshape(4, width, lanes)  6.87 us
  transfers between devices with their start and end apart: 16, of which 11 were waited for; matrix products, arithmetic and copies ran while one was open for 1% of the time, Pallas kernels for 1%

profile of v10, /device:TPU:1, one launch (start us, length us, event | category | flops | bytes accessed | tf_op | source)
XLA Modules:
  0.0 121.1 jit_solution(4678962820904347766)
XLA Ops:
  0.6 0.0 copy-start
  0.6 0.0 copy-start.1
  0.7 0.0 copy-start.2
  0.7 6.9 %collective-permute-start.2 = (bf16[128,256]{1,0:T(8,128)(2,1)}, bf16[128,256]{1,0:T(8,128)(2,1)S(1)}, u32[]{:S(2)}, u32[]{:S(2)}) collective-permute-start(bf16[128,256]{1,0:T(8,128)(2,1)} %bitcast.20), channel_id=1, source_target_pairs={{0,12},{1,13},{2,14},{3,15},{4,0},{5,1},{6,2},{7,3},{8,4},{9,5},{1... | collective-permute-start | bytes 196616 | tf_op jit(solution)/shard_map/ppermute | solution.py:272
  7.6 1.0 collective-permute-start.1
  8.6 2.3 %collective-permute-start = (bf16[128,256]{1,0:T(8,128)(2,1)}, bf16[128,256]{1,0:T(8,128)(2,1)S(1)}, u32[]{:S(2)}, u32[]{:S(2)}) collective-permute-start(bf16[128,256]{1,0:T(8,128)(2,1)} %bitcast.22), channel_id=1, source_target_pairs={{0,4},{1,5},{2,6},{3,7},{4,8},{5,9},{6,10},{7,11},{8,12},{9,13},{1... | collective-permute-start | bytes 196616 | tf_op jit(solution)/shard_map/ppermute | solution.py:272
  10.8 0.0 copy-start.3
  10.8 0.9 copy-done.3
  11.7 0.0 collective-permute-done.2
  11.7 3.3 %collective-permute-done.1 = bf16[128,256]{1,0:T(8,128)(2,1)S(1)} collective-permute-done((bf16[128,256]{1,0:T(8,128)(2,1)}, bf16[128,256]{1,0:T(8,128)(2,1)S(1)}, u32[]{:S(2)}, u32[]{:S(2)}) %collective-permute-start.1) | collective-permute-done | bytes 65568 | tf_op jit(solution)/shard_map/ppermute | solution.py:272
  15.0 0.6 collective-permute-done
  15.7 2.1 %collective-permute-start.5 = (bf16[4,128,256]{2,1,0:T(8,128)(2,1)S(1)}, bf16[4,128,256]{2,1,0:T(8,128)(2,1)S(1)}, u32[]{:S(2)}, u32[]{:S(2)}) collective-permute-start(bf16[4,128,256]{2,1,0:T(8,128)(2,1)S(1)} %pad_maximum_fusion.own), channel_id=1, source_target_pairs={{0,3},{1,2},{2,1},{3,0},{4,7},{5,6},{6,5},{7,4},{8,11},{9,10},{10,... | collective-permute-start | bytes 786440 | tf_op jit(solution)/shard_map/ppermute | solution.py:269
  17.8 0.2 collective-permute-start.4
  18.0 0.4 collective-permute-start.3
  19.1 0.8 concatenate.3.numbers
  19.9 2.2 %collective-permute-done.5.across = bf16[4,128,256]{2,1,0:T(8,128)(2,1)S(1)} collective-permute-done((bf16[4,128,256]{2,1,0:T(8,128)(2,1)S(1)}, bf16[4,128,256]{2,1,0:T(8,128)(2,1)S(1)}, u32[]{:S(2)}, u32[]{:S(2)}) %collective-permute-start.5) | collective-permute-done | bytes 262176 | tf_op jit(solution)/shard_map/ppermute | solution.py:269
  22.0 7.7 %collective-permute-done.4.beside = bf16[4,128,256]{2,1,0:T(8,128)(2,1)S(1)} collective-permute-done((bf16[4,128,256]{2,1,0:T(8,128)(2,1)S(1)}, bf16[4,128,256]{2,1,0:T(8,128)(2,1)S(1)}, u32[]{:S(2)}, u32[]{:S(2)}) %collective-permute-start.4) | collective-permute-done | bytes 262176 | tf_op jit(solution)/shard_map/ppermute | solution.py:269
  29.8 0.0 collective-permute-done.3.pair
  29.8 3.4 %forward_sweep.1 = (f32[8,128,256]{2,1,0:T(8,128)S(1)}, bf16[8,128,256]{2,1,0:T(8,128)(2,1)S(1)}) custom-call(s32[133]{0:T(256)S(1)} %concatenate.3.numbers, bf16[4,128,256]{2,1,0:T(8,128)(2,1)S(1)} %pad_maximum_fusion.own, bf16[4,128,256]{2,1,0:T(8,128)(2,1)S(1)} %collective-permute-done.3.pair, bf16[4,128,256]{2,1,0:T(8,128)(2,1)S(1)} %collective-permute-done.4.beside, ...), custom_call_target="tpu_custom_call" | custom-call | flops 2147483648 | bytes 8388608 | tf_op jit(solution)/shard_map/forward_sweep/pallas_call | solution.py:286
  33.2 0.6 collective-permute-start.6
  33.7 1.5 %collective-permute-done.6 = bf16[8,128,256]{2,1,0:T(8,128)(2,1)S(1)} collective-permute-done((bf16[8,128,256]{2,1,0:T(8,128)(2,1)S(1)}, bf16[8,128,256]{2,1,0:T(8,128)(2,1)S(1)}, u32[]{:S(2)}, u32[]{:S(2)}) %collective-permute-start.6) | collective-permute-done | bytes 524320 | tf_op jit(solution)/shard_map/ppermute | solution.py:310
  35.3 0.2 add_convert_fusion
  35.4 17.4 %all_to_all.20.terms = bf16[8,128,256]{2,1,0:T(8,128)(2,1)S(1)} all-to-all(bf16[8,128,256]{2,1,0:T(8,128)(2,1)S(1)} %add_convert_fusion), channel_id=1, replica_groups={{0,32,64,96,128,160,192,224},{16,48,80,112,144,176,208,240},{1,33,65,97..., dimensions={0} | all-to-all | bytes 1048576 | tf_op jit(solution)/shard_map/all_to_all | solution.py:312
  52.9 0.0 copy-done
  52.9 0.0 copy-done.1
  52.9 0.0 copy-done.2
  52.9 0.6 middle.1
  53.5 16.0 %all_to_all.21.held = bf16[8,384,128]{2,1,0:T(8,128)(2,1)S(1)} all-to-all(bf16[8,384,128]{2,1,0:T(8,128)(2,1)S(1)} %middle.1), channel_id=1, replica_groups={{0,32,64,96,128,160,192,224},{16,48,80,112,144,176,208,240},{1,33,65,97..., dimensions={0} | all-to-all | bytes 1572864 | tf_op jit(solution)/shard_map/all_to_all | solution.py:323
  69.5 2.7 %collective-permute-start.7 = (bf16[8,384,128]{2,1,0:T(8,128)(2,1)S(1)}, bf16[8,384,128]{2,1,0:T(8,128)(2,1)S(1)}, u32[]{:S(2)}, u32[]{:S(2)}) collective-permute-start(bf16[8,384,128]{2,1,0:T(8,128)(2,1)S(1)} %all_to_all.21.held), channel_id=1, source_target_pairs={{0,16},{16,0},{32,48},{48,32},{64,80},{80,64},{96,112},{112,96},{1... | collective-permute-start | bytes 2359304 | tf_op jit(solution)/shard_map/ppermute | solution.py:324
  72.2 1.9 %collective-permute-done.7.other = bf16[8,384,128]{2,1,0:T(8,128)(2,1)S(1)} collective-permute-done((bf16[8,384,128]{2,1,0:T(8,128)(2,1)S(1)}, bf16[8,384,128]{2,1,0:T(8,128)(2,1)S(1)}, u32[]{:S(2)}, u32[]{:S(2)}) %collective-permute-start.7) | collective-permute-done | bytes 786464 | tf_op jit(solution)/shard_map/ppermute | solution.py:324
  74.1 3.4 %backward_sweep.1 = (bf16[4,256,128]{2,1,0:T(8,128)(2,1)S(1)}, bf16[4,256,128]{2,1,0:T(8,128)(2,1)S(1)}, bf16[4,256,128]{2,1,0:T(8,128)(2,1)S(1)}, bf16[4,256,128]{2,1,0:T(8,128)(2,1)S(1)}) custom-call(s32[133]{0:T(256)S(1)} %concatenate.3.numbers, bf16[8,384,128]{2,1,0:T(8,128)(2,1)S(1)} %all_to_all.21.held, ...), custom_call_target="tpu_custom_call" | custom-call | flops 2147483648 | bytes 8388608 | tf_op jit(solution)/shard_map/backward_sweep/pallas_call | solution.py:326
  77.5 2.3 %collective-permute-start.8 = (bf16[4,256,128]{2,1,0:T(8,128)(2,1)S(1)}, bf16[4,256,128]{2,1,0:T(8,128)(2,1)S(1)}, u32[]{:S(2)}, u32[]{:S(2)}) collective-permute-start(bf16[4,256,128]{2,1,0:T(8,128)(2,1)S(1)} %get-tuple-element.30), channel_id=1, source_target_pairs={{0,2},{1,3},{2,0},{3,1},{4,6},{5,7},{6,4},{7,5},{8,10},{9,11},{10,... | collective-permute-start | bytes 786440 | tf_op jit(solution)/shard_map/ppermute | solution.py:269
  79.8 0.0 collective-permute-start.9
  79.8 1.3 %collective-permute-start.10 = (bf16[4,256,128]{2,1,0:T(8,128)(2,1)S(1)}, bf16[4,256,128]{2,1,0:T(8,128)(2,1)S(1)}, u32[]{:S(2)}, u32[]{:S(2)}) collective-permute-start(bf16[4,256,128]{2,1,0:T(8,128)(2,1)S(1)} %get-tuple-element.32), channel_id=1, source_target_pairs={{0,3},{1,2},{2,1},{3,0},{4,7},{5,6},{6,5},{7,4},{8,11},{9,10},{10,... | collective-permute-start | bytes 786440 | tf_op jit(solution)/shard_map/ppermute | solution.py:269
  81.1 0.8 weights_chunk.1
  81.9 7.7 %all-to-all-start.2 = ((bf16[16,64,128]{2,1,0:T(8,128)(2,1)}), bf16[16,64,128]{2,1,0:T(8,128)(2,1)S(1)}, u32[]{:S(2)}, u32[]{:S(2)}) async-start(bf16[16,64,128]{2,1,0:T(8,128)(2,1)} %weights_chunk.1), calls=%async_computation.2 | async-start | bytes 524288 | tf_op jit(solution)/shard_map/all_to_all | solution.py:349
  89.5 0.0 collective-permute-done.8.pair
  89.5 3.6 %collective-permute-done.9.beside = bf16[4,256,128]{2,1,0:T(8,128)(2,1)S(1)} collective-permute-done((bf16[4,256,128]{2,1,0:T(8,128)(2,1)S(1)}, bf16[4,256,128]{2,1,0:T(8,128)(2,1)S(1)}, u32[]{:S(2)}, u32[]{:S(2)}) %collective-permute-start.9) | collective-permute-done | bytes 262176 | tf_op jit(solution)/shard_map/ppermute | solution.py:269
  93.1 0.0 collective-permute-done.10.across
  93.1 0.1 quad_sum.1
  93.3 7.1 %all-to-all-done.2.terms = bf16[16,64,128]{2,1,0:T(8,128)(2,1)S(1)} async-done(((bf16[16,64,128]{2,1,0:T(8,128)(2,1)}), bf16[16,64,128]{2,1,0:T(8,128)(2,1)S(1)}, u32[]{:S(2)}, u32[]{:S(2)}) %all-to-all-start.2) | async-done | bytes 262176 | tf_op jit(solution)/shard_map/all_to_all | solution.py:349
  100.3 0.9 weights_sum.1
  101.2 6.9 %all-to-all-start.3 = ((f32[16,64,128]{2,1,0:T(8,128)}), f32[16,64,128]{2,1,0:T(8,128)S(1)}, u32[]{:S(2)}, u32[]{:S(2)}) async-start(f32[16,64,128]{2,1,0:T(8,128)} %weights_sum.1), calls=%async_computation.3 | async-start | bytes 1048576 | tf_op jit(solution)/shard_map/all_to_all | solution.py:370
  108.1 0.3 collective-permute-start.11
  108.4 2.2 %collective-permute-start.12 = (bf16[256,128]{1,0:T(8,128)(2,1)S(1)}, bf16[256,128]{1,0:T(8,128)(2,1)S(1)}, u32[]{:S(2)}, u32[]{:S(2)}) collective-permute-start(bf16[256,128]{1,0:T(8,128)(2,1)S(1)} %get-tuple-element.39), channel_id=1, source_target_pairs={{0,8},{1,9},{2,10},{3,11},{4,12},{5,13},{6,14},{7,15},{8,0},{9,1},... | collective-permute-start | bytes 196616 | tf_op jit(solution)/shard_map/ppermute | solution.py:272
  110.6 1.9 %collective-permute-start.13 = (bf16[256,128]{1,0:T(8,128)(2,1)S(1)}, bf16[256,128]{1,0:T(8,128)(2,1)S(1)}, u32[]{:S(2)}, u32[]{:S(2)}) collective-permute-start(bf16[256,128]{1,0:T(8,128)(2,1)S(1)} %get-tuple-element.40), channel_id=1, source_target_pairs={{0,12},{1,13},{2,14},{3,15},{4,0},{5,1},{6,2},{7,3},{8,4},{9,5},{1... | collective-permute-start | bytes 196616 | tf_op jit(solution)/shard_map/ppermute | solution.py:272
  112.5 1.8 %collective-permute-done.11.refs_1_ = bf16[256,128]{1,0:T(8,128)(2,1)S(1)} collective-permute-done((bf16[256,128]{1,0:T(8,128)(2,1)S(1)}, bf16[256,128]{1,0:T(8,128)(2,1)S(1)}, u32[]{:S(2)}, u32[]{:S(2)}) %collective-permute-start.11) | collective-permute-done | bytes 65568 | tf_op jit(solution)/shard_map/ppermute | solution.py:272
  114.4 1.4 %collective-permute-done.12.refs_2_ = bf16[256,128]{1,0:T(8,128)(2,1)S(1)} collective-permute-done((bf16[256,128]{1,0:T(8,128)(2,1)S(1)}, bf16[256,128]{1,0:T(8,128)(2,1)S(1)}, u32[]{:S(2)}, u32[]{:S(2)}) %collective-permute-start.12) | collective-permute-done | bytes 65568 | tf_op jit(solution)/shard_map/ppermute | solution.py:272
  115.7 4.5 %collective-permute-done.13.refs_3_ = bf16[256,128]{1,0:T(8,128)(2,1)S(1)} collective-permute-done((bf16[256,128]{1,0:T(8,128)(2,1)S(1)}, bf16[256,128]{1,0:T(8,128)(2,1)S(1)}, u32[]{:S(2)}, u32[]{:S(2)}) %collective-permute-start.13) | collective-permute-done | bytes 65568 | tf_op jit(solution)/shard_map/ppermute | solution.py:272
  120.2 0.0 all-to-all-done.3
  120.2 0.9 results.1
  (3 shorter events, 0.0 us)
Async XLA Ops:
  0.6 52.3 %copy-start = (bf16[256,256]{1,0:T(8,128)(2,1)S(1)}, bf16[256,256]{1,0:T(8,128)(2,1)}, u32[]{:S(2)}) copy-start(bf16[256,256]{1,0:T(8,128)(2,1)} %refs_4_.1) | copy-start | bytes 393220
  0.6 52.3 %copy-start.1 = (bf16[256,256]{1,0:T(8,128)(2,1)S(1)}, bf16[256,256]{1,0:T(8,128)(2,1)}, u32[]{:S(2)}) copy-start(bf16[256,256]{1,0:T(8,128)(2,1)} %w_out.1) | copy-start | bytes 393220
  0.7 52.2 %copy-start.2 = (bf16[1,128,256]{2,1,0:T(8,128)(2,1)S(1)}, bf16[1,128,256]{2,1,0:T(8,128)(2,1)}, u32[]{:S(2)}) copy-start(bf16[1,128,256]{2,1,0:T(8,128)(2,1)} %param.9) | copy-start | bytes 196612
  0.7 11.1 %collective-permute-start.2 = (bf16[128,256]{1,0:T(8,128)(2,1)}, bf16[128,256]{1,0:T(8,128)(2,1)S(1)}, u32[]{:S(2)}, u32[]{:S(2)}) collective-permute-start(bf16[128,256]{1,0:T(8,128)(2,1)} %bitcast.20), channel_id=1, source_target_pairs={{0,12},{1,13},{2,14},{3,15},{4,0},{5,1},{6,2},{7,3},{8,4},{9,5},{1... | collective-permute-start | bytes 196616 | tf_op jit(solution)/shard_map/ppermute | solution.py:272
  7.6 7.4 %collective-permute-start.1 = (bf16[128,256]{1,0:T(8,128)(2,1)}, bf16[128,256]{1,0:T(8,128)(2,1)S(1)}, u32[]{:S(2)}, u32[]{:S(2)}) collective-permute-start(bf16[128,256]{1,0:T(8,128)(2,1)} %bitcast.21), channel_id=1, source_target_pairs={{0,8},{1,9},{2,10},{3,11},{4,12},{5,13},{6,14},{7,15},{8,0},{9,1},... | collective-permute-start | bytes 196616 | tf_op jit(solution)/shard_map/ppermute | solution.py:272
  8.6 7.1 %collective-permute-start = (bf16[128,256]{1,0:T(8,128)(2,1)}, bf16[128,256]{1,0:T(8,128)(2,1)S(1)}, u32[]{:S(2)}, u32[]{:S(2)}) collective-permute-start(bf16[128,256]{1,0:T(8,128)(2,1)} %bitcast.22), channel_id=1, source_target_pairs={{0,4},{1,5},{2,6},{3,7},{4,8},{5,9},{6,10},{7,11},{8,12},{9,13},{1... | collective-permute-start | bytes 196616 | tf_op jit(solution)/shard_map/ppermute | solution.py:272
  10.8 0.9 copy-start.3
  15.7 6.3 %collective-permute-start.5 = (bf16[4,128,256]{2,1,0:T(8,128)(2,1)S(1)}, bf16[4,128,256]{2,1,0:T(8,128)(2,1)S(1)}, u32[]{:S(2)}, u32[]{:S(2)}) collective-permute-start(bf16[4,128,256]{2,1,0:T(8,128)(2,1)S(1)} %pad_maximum_fusion.own), channel_id=1, source_target_pairs={{0,3},{1,2},{2,1},{3,0},{4,7},{5,6},{6,5},{7,4},{8,11},{9,10},{10,... | collective-permute-start | bytes 786440 | tf_op jit(solution)/shard_map/ppermute | solution.py:269
  17.8 11.9 %collective-permute-start.4 = (bf16[4,128,256]{2,1,0:T(8,128)(2,1)S(1)}, bf16[4,128,256]{2,1,0:T(8,128)(2,1)S(1)}, u32[]{:S(2)}, u32[]{:S(2)}) collective-permute-start(bf16[4,128,256]{2,1,0:T(8,128)(2,1)S(1)} %pad_maximum_fusion.own), channel_id=1, source_target_pairs={{0,1},{1,0},{2,3},{3,2},{4,5},{5,4},{6,7},{7,6},{8,9},{9,8},{10,11... | collective-permute-start | bytes 786440 | tf_op jit(solution)/shard_map/ppermute | solution.py:269
  18.0 11.7 %collective-permute-start.3 = (bf16[4,128,256]{2,1,0:T(8,128)(2,1)S(1)}, bf16[4,128,256]{2,1,0:T(8,128)(2,1)S(1)}, u32[]{:S(2)}, u32[]{:S(2)}) collective-permute-start(bf16[4,128,256]{2,1,0:T(8,128)(2,1)S(1)} %pad_maximum_fusion.own), channel_id=1, source_target_pairs={{0,2},{1,3},{2,0},{3,1},{4,6},{5,7},{6,4},{7,5},{8,10},{9,11},{10,... | collective-permute-start | bytes 786440 | tf_op jit(solution)/shard_map/ppermute | solution.py:269
  33.2 2.1 %collective-permute-start.6 = (bf16[8,128,256]{2,1,0:T(8,128)(2,1)S(1)}, bf16[8,128,256]{2,1,0:T(8,128)(2,1)S(1)}, u32[]{:S(2)}, u32[]{:S(2)}) collective-permute-start(bf16[8,128,256]{2,1,0:T(8,128)(2,1)S(1)} %get-tuple-element.25), channel_id=1, source_target_pairs={{0,16},{16,0},{32,48},{48,32},{64,80},{80,64},{96,112},{112,96},{1... | collective-permute-start | bytes 1572872 | tf_op jit(solution)/shard_map/ppermute | solution.py:310
  69.5 4.6 %collective-permute-start.7 = (bf16[8,384,128]{2,1,0:T(8,128)(2,1)S(1)}, bf16[8,384,128]{2,1,0:T(8,128)(2,1)S(1)}, u32[]{:S(2)}, u32[]{:S(2)}) collective-permute-start(bf16[8,384,128]{2,1,0:T(8,128)(2,1)S(1)} %all_to_all.21.held), channel_id=1, source_target_pairs={{0,16},{16,0},{32,48},{48,32},{64,80},{80,64},{96,112},{112,96},{1... | collective-permute-start | bytes 2359304 | tf_op jit(solution)/shard_map/ppermute | solution.py:324
  77.5 12.0 %collective-permute-start.8 = (bf16[4,256,128]{2,1,0:T(8,128)(2,1)S(1)}, bf16[4,256,128]{2,1,0:T(8,128)(2,1)S(1)}, u32[]{:S(2)}, u32[]{:S(2)}) collective-permute-start(bf16[4,256,128]{2,1,0:T(8,128)(2,1)S(1)} %get-tuple-element.30), channel_id=1, source_target_pairs={{0,2},{1,3},{2,0},{3,1},{4,6},{5,7},{6,4},{7,5},{8,10},{9,11},{10,... | collective-permute-start | bytes 786440 | tf_op jit(solution)/shard_map/ppermute | solution.py:269
  79.8 13.3 %collective-permute-start.9 = (bf16[4,256,128]{2,1,0:T(8,128)(2,1)S(1)}, bf16[4,256,128]{2,1,0:T(8,128)(2,1)S(1)}, u32[]{:S(2)}, u32[]{:S(2)}) collective-permute-start(bf16[4,256,128]{2,1,0:T(8,128)(2,1)S(1)} %get-tuple-element.31), channel_id=1, source_target_pairs={{0,1},{1,0},{2,3},{3,2},{4,5},{5,4},{6,7},{7,6},{8,9},{9,8},{10,11... | collective-permute-start | bytes 786440 | tf_op jit(solution)/shard_map/ppermute | solution.py:269
  79.8 13.3 %collective-permute-start.10 = (bf16[4,256,128]{2,1,0:T(8,128)(2,1)S(1)}, bf16[4,256,128]{2,1,0:T(8,128)(2,1)S(1)}, u32[]{:S(2)}, u32[]{:S(2)}) collective-permute-start(bf16[4,256,128]{2,1,0:T(8,128)(2,1)S(1)} %get-tuple-element.32), channel_id=1, source_target_pairs={{0,3},{1,2},{2,1},{3,0},{4,7},{5,6},{6,5},{7,4},{8,11},{9,10},{10,... | collective-permute-start | bytes 786440 | tf_op jit(solution)/shard_map/ppermute | solution.py:269
  81.9 18.5 %all-to-all-start.2 = ((bf16[16,64,128]{2,1,0:T(8,128)(2,1)}), bf16[16,64,128]{2,1,0:T(8,128)(2,1)S(1)}, u32[]{:S(2)}, u32[]{:S(2)}) async-start(bf16[16,64,128]{2,1,0:T(8,128)(2,1)} %weights_chunk.1), calls=%async_computation.2 | async-start | bytes 524288 | tf_op jit(solution)/shard_map/all_to_all | solution.py:349
  101.2 19.0 %all-to-all-start.3 = ((f32[16,64,128]{2,1,0:T(8,128)}), f32[16,64,128]{2,1,0:T(8,128)S(1)}, u32[]{:S(2)}, u32[]{:S(2)}) async-start(f32[16,64,128]{2,1,0:T(8,128)} %weights_sum.1), calls=%async_computation.3 | async-start | bytes 1048576 | tf_op jit(solution)/shard_map/all_to_all | solution.py:370
  108.1 6.3 %collective-permute-start.11 = (bf16[256,128]{1,0:T(8,128)(2,1)S(1)}, bf16[256,128]{1,0:T(8,128)(2,1)S(1)}, u32[]{:S(2)}, u32[]{:S(2)}) collective-permute-start(bf16[256,128]{1,0:T(8,128)(2,1)S(1)} %get-tuple-element.38), channel_id=1, source_target_pairs={{0,4},{1,5},{2,6},{3,7},{4,8},{5,9},{6,10},{7,11},{8,12},{9,13},{1... | collective-permute-start | bytes 196616 | tf_op jit(solution)/shard_map/ppermute | solution.py:272
  108.4 7.3 %collective-permute-start.12 = (bf16[256,128]{1,0:T(8,128)(2,1)S(1)}, bf16[256,128]{1,0:T(8,128)(2,1)S(1)}, u32[]{:S(2)}, u32[]{:S(2)}) collective-permute-start(bf16[256,128]{1,0:T(8,128)(2,1)S(1)} %get-tuple-element.39), channel_id=1, source_target_pairs={{0,8},{1,9},{2,10},{3,11},{4,12},{5,13},{6,14},{7,15},{8,0},{9,1},... | collective-permute-start | bytes 196616 | tf_op jit(solution)/shard_map/ppermute | solution.py:272
  110.6 9.6 %collective-permute-start.13 = (bf16[256,128]{1,0:T(8,128)(2,1)S(1)}, bf16[256,128]{1,0:T(8,128)(2,1)S(1)}, u32[]{:S(2)}, u32[]{:S(2)}) collective-permute-start(bf16[256,128]{1,0:T(8,128)(2,1)S(1)} %get-tuple-element.40), channel_id=1, source_target_pairs={{0,12},{1,13},{2,14},{3,15},{4,0},{5,1},{6,2},{7,3},{8,4},{9,5},{1... | collective-permute-start | bytes 196616 | tf_op jit(solution)/shard_map/ppermute | solution.py:272
